TPU v7x, 256 devices: a whole 4x4x8 slice. The times are simulated.
256 devices in a mesh: section: 8 (over z_hi, core), ctx: 32 (over y, z_lo, x).
Axes of the slice: x: 4, y: 4, z: 8 (z_hi: 4, z_lo: 2; z = z_hi * 2 + z_lo), core: 2. Of those that a mesh axis runs over, the one named last changes fastest.
Arguments:
- queries: bfloat16 [8, 4096, 2560], P('section', 'ctx'), may hold values from -150 to 150
- attn_out: bfloat16 [8, 4096, 2560], P('section', 'ctx'), may hold values from -6 to 6
- grad_out: bfloat16 [8, 4096, 2560], P('section', 'ctx'), may hold values from -6 to 6
- shared_kv: bfloat16 [4096, 1024], P('ctx', 'section'), may hold values from -7 to 7
- ret_query: bfloat16 [4096, 512], P('ctx'), may hold values from -6 to 6
- ret_key: bfloat16 [4096, 512], P('ctx'), may hold values from -6 to 6
- ret_value: bfloat16 [4096, 1024], P('ctx', 'section'), may hold values from -6 to 6
- log_decay: float32 [4096, 4], P('ctx'), may hold values from -0.8 to 0, as said below
Outputs:
- d_queries: bfloat16 [8, 4096, 2560], P('section', 'ctx')
- d_ret_query: float32 [4096, 512], P('ctx')
- d_ret_key: float32 [4096, 512], P('ctx')
- d_ret_value: float32 [4096, 1024], P('ctx', 'section')
- d_log_decay: float32 [4096, 4], P('ctx')
Inputs may be any that keep to these rules, and one draw needn't show every extreme that they name: `log_decay`: every entry is negative.
All inputs are finite; a program needn't handle non-finite values.
Results may differ from a plain program's by a relative error of at most 0.0064.
Values may be sent and summed in bfloat16 or wider, within the bound.
No kernel may reach another device: no remote copies, remote signals or barrier semaphores. Data moves between devices by JAX's collectives and lax.ppermute only.
A program may use at most 128 MiB of HBM per device.

v0:
```python
import jax
import jax.numpy as jnp
from jax import lax
from jax.sharding import PartitionSpec as P

exact_variant = lax.Precision.HIGHEST


def prefix(part, axis, combine, identity, reverse):
    count = lax.axis_size(axis)
    place = lax.axis_index(axis)
    ahead = count - 1 - place if reverse else place
    gathered = jax.tree.map(lambda a: lax.all_gather(a, axis), part)
    state = jax.tree.map(lambda a, e: jnp.zeros_like(a) + jnp.asarray(e, a.dtype), part, identity)

    def one(step, state):
        source = count - 1 - step if reverse else step
        return combine(
            state, jax.tree.map(lambda a: lax.dynamic_index_in_dim(a, source, 0, False), gathered)
        )

    return lax.fori_loop(0, ahead, one, state)


def norm_backward(retained, d_shared, head_size):
    row_count = retained.shape[0]
    grouped = retained.reshape(row_count, -1, head_size)
    upstream = d_shared.reshape(row_count, -1, head_size)
    inverse = lax.rsqrt(jnp.mean(grouped * grouped, axis=-1, keepdims=True) + 1e-06)
    normed = grouped * inverse
    result = (upstream - normed * jnp.mean(normed * upstream, axis=-1, keepdims=True)) * inverse
    return result.reshape(retained.shape)


def state_terms(key_rows, value_rows, decay_rows, head_mask, head_size):
    tok_rows, kv_heads = decay_rows.shape
    key_heads = key_rows.reshape(tok_rows, kv_heads, head_size)
    cumulative = jnp.cumsum(decay_rows, axis=0)
    decay_total = cumulative[-1]
    weighted = key_heads * jnp.exp(decay_total - cumulative)[:, :, None]
    local_state = jnp.einsum(
        "thd,tc,hc->dc", weighted, value_rows, head_mask, precision=exact_variant
    )
    return (cumulative, decay_total, local_state)


def retention_local(query_rows, key_rows, value_rows, decay_rows, state_in, head_mask, head_size):
    tok_rows, kv_heads = decay_rows.shape
    scaled = query_rows.reshape(tok_rows, kv_heads, head_size) * head_size ** (-0.5)
    key_heads = key_rows.reshape(tok_rows, kv_heads, head_size)
    cumulative, decay_total, local_state = state_terms(
        key_rows, value_rows, decay_rows, head_mask, head_size
    )
    lower_tri = jnp.arange(tok_rows)[:, None] >= jnp.arange(tok_rows)[None, :]
    spread = jnp.where(
        lower_tri[:, :, None], cumulative[:, None, :] - cumulative[None, :, :], -jnp.inf
    )
    inner_prod = jnp.einsum("thd,shd->hts", scaled, key_heads, precision=exact_variant) * jnp.exp(
        spread
    ).transpose(2, 0, 1)
    within = jnp.einsum("hts,sc,hc->tc", inner_prod, value_rows, head_mask, precision=exact_variant)
    carried = jnp.einsum(
        "thd,dc,hc->tc",
        scaled * jnp.exp(cumulative)[:, :, None],
        state_in,
        head_mask,
        precision=exact_variant,
    )
    column_decay = jnp.exp(jnp.dot(decay_total, head_mask, precision=exact_variant))
    state_out = column_decay[None, :] * state_in + local_state
    return (within + carried, state_out)


def make_combine(head_mask):

    def combine(earlier, later_part):
        column_decay = jnp.exp(jnp.dot(later_part[0], head_mask, precision=exact_variant))
        return (earlier[0] + later_part[0], column_decay[None, :] * earlier[1] + later_part[1])

    return combine


def on_device(queries, attn_out, grad_out, shared_kv, ret_query, ret_key, ret_value, log_decay):
    tok_rows = queries.shape[1]
    kv_heads = log_decay.shape[1]
    head_size = ret_query.shape[1] // kv_heads
    q_group = queries.shape[2] // (kv_heads * head_size)
    columns = ret_value.shape[1]
    seq_length = tok_rows * lax.axis_size("ctx")
    scaling = head_size ** (-0.5)
    first_col = lax.axis_index("section") * columns
    head_of = (first_col + jnp.arange(columns)) // (2 * head_size)
    head_mask = (jnp.arange(kv_heads)[:, None] == head_of[None, :]).astype(jnp.float32)
    combine = make_combine(head_mask)
    query_f = ret_query.astype(jnp.float32)
    key_f = ret_key.astype(jnp.float32)
    value_f = ret_value.astype(jnp.float32)
    cumulative, decay_total, local_state = state_terms(
        key_f, value_f, log_decay, head_mask, head_size
    )
    empty_pair = (jnp.zeros((kv_heads,), jnp.float32), jnp.zeros((head_size, columns), jnp.float32))
    prefix_decay, state_in = prefix((decay_total, local_state), "ctx", combine, empty_pair, False)
    own_rows = lax.all_gather(shared_kv, "section", axis=1, tiled=True)
    kv_full = lax.all_gather(own_rows, "ctx", axis=0, tiled=True)
    paired = kv_full.reshape(seq_length, kv_heads, 2, head_size)
    query_heads = queries[0].reshape(tok_rows, kv_heads, q_group, head_size)
    grad_heads = grad_out[0].reshape(tok_rows, kv_heads, q_group, head_size)
    saved_heads = attn_out[0].reshape(tok_rows, kv_heads, q_group, head_size)
    row_offset = lax.axis_index("ctx") * tok_rows
    positions = row_offset + jnp.arange(tok_rows)
    key_block = min(512, seq_length)
    block_count = seq_length // key_block
    last_row = row_offset + tok_rows - 1
    output_change = jnp.sum(
        grad_heads.astype(jnp.float32) * saved_heads.astype(jnp.float32), axis=-1
    ).transpose(1, 2, 0)

    def scores(block_start):
        kv_piece = lax.dynamic_slice_in_dim(paired, block_start, key_block, 0)
        raw_scores = (
            jnp.einsum(
                "tgrd,kgd->grtk", query_heads, kv_piece[:, :, 0], preferred_element_type=jnp.float32
            )
            * scaling
        )
        is_valid = (block_start + jnp.arange(key_block))[None, :] <= positions[:, None]
        return (jnp.where(is_valid, raw_scores, -jnp.inf), kv_piece)

    def stat_step(block_index, running):
        block_start = block_index * key_block

        def stat_update(current):
            running_max, running_sum = current
            masked, kv_piece = scores(block_start)
            new_max = jnp.maximum(running_max, jnp.max(masked, axis=-1))
            running_sum = running_sum * jnp.exp(running_max - new_max) + jnp.sum(
                jnp.exp(masked - new_max[..., None]), axis=-1
            )
            return (new_max, running_sum)

        return lax.cond(block_start <= last_row, stat_update, lambda current: current, running)

    start_max = jnp.full((kv_heads, q_group, tok_rows), -jnp.inf, jnp.float32)
    start_sum = jnp.zeros((kv_heads, q_group, tok_rows), jnp.float32)
    running_max, running_sum = lax.fori_loop(0, block_count, stat_step, (start_max, start_sum))
    lse_rows = running_max + jnp.log(running_sum)

    def grad_step(block_index, running):
        block_start = block_index * key_block

        def grad_update(current):
            dq_sum, grad_terms = current
            masked, kv_piece = scores(block_start)
            weights = jnp.exp(masked - lse_rows[..., None])
            weights_b = weights.astype(jnp.bfloat16)
            d_weight = jnp.einsum(
                "tgrd,kgd->grtk", grad_heads, kv_piece[:, :, 1], preferred_element_type=jnp.float32
            )
            d_score = (weights * (d_weight - output_change[..., None])).astype(jnp.bfloat16)
            dq_sum = dq_sum + jnp.einsum(
                "grtk,kgd->tgrd", d_score, kv_piece[:, :, 0], preferred_element_type=jnp.float32
            )
            d_keys = (
                jnp.einsum(
                    "grtk,tgrd->kgd", d_score, query_heads, preferred_element_type=jnp.float32
                )
                * scaling
            )
            d_values = jnp.einsum(
                "grtk,tgrd->kgd", weights_b, grad_heads, preferred_element_type=jnp.float32
            )
            block_terms = (
                jnp.stack([d_keys, d_values], axis=2)
                .reshape(key_block, 2 * kv_heads * head_size)
                .astype(jnp.bfloat16)
            )
            block_terms = lax.optimization_barrier(block_terms).astype(jnp.float32)
            return (
                dq_sum,
                lax.dynamic_update_slice_in_dim(grad_terms, block_terms, block_start, 0),
            )

        return lax.cond(block_start <= last_row, grad_update, lambda current: current, running)

    start_dq = jnp.zeros((tok_rows, kv_heads, q_group, head_size), jnp.float32)
    start_terms = jnp.zeros((seq_length, 2 * kv_heads * head_size), jnp.float32)
    dq_sum, grad_terms = lax.fori_loop(0, block_count, grad_step, (start_dq, start_terms))
    d_queries = (
        (dq_sum * scaling).astype(jnp.bfloat16).reshape(1, tok_rows, q_group * kv_heads * head_size)
    )
    token_sum = lax.psum_scatter(grad_terms, "ctx", scatter_dimension=0, tiled=True)
    d_shared = lax.psum_scatter(token_sum, "section", scatter_dimension=1, tiled=True)

    def forward_piece(query_in, key_in, value_in, decay_in, state_start):
        return retention_local(
            query_in, key_in, value_in, decay_in, state_start, head_mask, head_size
        )

    (retained, state_out), pullback = jax.vjp(
        forward_piece, query_f, key_f, value_f, log_decay, state_in
    )
    d_retained = norm_backward(retained, d_shared, head_size)
    query_decayed = (
        query_f.reshape(tok_rows, kv_heads, head_size) * scaling * jnp.exp(cumulative)[:, :, None]
    )
    carry_grad = jnp.einsum(
        "thd,tc,hc->dc", query_decayed, d_retained, head_mask, precision=exact_variant
    )
    suffix_decay, d_state = prefix((decay_total, carry_grad), "ctx", combine, empty_pair, True)
    d_query, d_key, d_value, d_decay, d_start = pullback((d_retained, d_state))
    d_query, d_key, d_decay = lax.psum((d_query, d_key, d_decay), "section")
    return (d_queries, d_query, d_key, d_value, d_decay)


def solution(mesh):
    return jax.shard_map(
        on_device,
        mesh=mesh,
        in_specs=(
            P("section", "ctx", None),
            P("section", "ctx", None),
            P("section", "ctx", None),
            P("ctx", "section"),
            P("ctx", None),
            P("ctx", None),
            P("ctx", "section"),
            P("ctx", None),
        ),
        out_specs=(
            P("section", "ctx", None),
            P("ctx", None),
            P("ctx", None),
            P("ctx", "section"),
            P("ctx", None),
        ),
        check_vma=False,
    )
```

profile of v0, /device:TPU:2, one launch (start us, length us, event | category | flops | bytes accessed | tf_op | source)
XLA Modules:
  0.0 1040.8 jit_solution(14431417360042687573)
XLA Ops:
  8.1 19.3 %all_gather.22 = bf16[128,1024]{0,1:T(8,128)(2,1)} all-gather(bf16[128,128]{0,1:T(8,128)(2,1)S(1)} %copy.95), channel_id=1, replica_groups=mesh['section'=8,'ctx'=32] {'section'}, dimensions={1}, use_global_device_ids=true | all-gather | bytes 294912 | tf_op jit(solution)/shard_map/all_gather | solution.py:103
  27.5 1.4 copy.96
  29.3 1.4 copy.99
  30.7 1.6 copy.100
  32.4 166.4 %all-gather.7.cloned.1.call-done = bf16[4096,1024]{0,1:T(8,128)(2,1)} async-done(((bf16[128,1024]{0,1:T(8,128)(2,1)}), bf16[4096,1024]{0,1:T(8,128)(2,1)}) %all-gather.7.cloned.1.call-update) | async-done | bytes 8388624 | tf_op jit(solution)/shard_map/all_gather | solution.py:104
  198.8 11.9 %copy.101 = bf16[4096,4,2,128]{3,0,1,2:T(8,128)(2,1)} copy(bf16[4096,4,2,128]{0,3,2,1:T(8,128)(2,1)} %bitcast.278) | data formatting | bytes 16777216
  210.8 3.6 while.63
  210.8 3.2 conditional.6
  211.0 1.9 fusion.8
  212.9 1.1 exponential_reduce_fusion
  214.6 7.8 broadcast_in_dim.79
  222.4 15.8 %while.64 = (s32[]{:T(128)}, f32[128,4,5,128]{0,3,2,1:T(8,128)S(1)}, f32[4096,1024]{0,1:T(8,128)}, s32[]{:T(128)}, bf16[4096,4,2,128]{3,0,1,2:T(8,128)(2,1)}, /*...) while((s32[]{:T(128)}, ...), condition=%wide.region_10.11_spmd.clone, body=%wide.region_7.10_spmd.clone.sunk | while | flops 1693057664 | bytes 60002672 | solution.py:187
  222.4 15.5 %conditional.7 = ((f32[128,4,5,128]{0,3,2,1:T(8,128)S(1)}, f32[4096,1024]{0,1:T(8,128)})) conditional(s32[]{:T(128)} %convert_element_type.76, (f32[128,4,5,128]{0,3,2,1:T(8,128)S(1)}, f32[4096,1024]{0,1:T(8,128)}) %tuple.155, (s32[]{:T(128)}, bf16[4096,4,2,128]{3,0,1,2:T(8,128)(2,1)}, s32[]{:T(128)}, bf16[128,4,5,128]{0,3,2,1:T(8,128)(2,1)S(1)}, ...), branch_computations={%region_8.8_spmd, %region_9.9_spmd} | conditional | flops 1693057664 | bytes 60001916 | solution.py:183
  222.4 4.3 fusion.35
  226.8 4.2 fusion.12
  231.1 2.2 fusion.22
  233.7 1.4 fusion.32
  235.1 1.0 fusion.31
  236.3 1.7 convert_dynamic-update-slice_fusion
  239.8 1.1 convolution_bitcast_fusion.10
  241.3 205.7 %all-gather.2 = f32[32,1,4]{2,1,0:T(1,128)S(1)} all-gather(f32[1,1,4]{2,1,0:T(1,128)S(1)} %get-tuple-element.763), channel_id=1, replica_groups=mesh['section'=8,'ctx'=32] {'ctx'}, dimensions={0}, use_global_device_ids=true | all-gather | bytes 528 | tf_op jit(solution)/shard_map/all_gather | solution.py:13
  447.7 124.5 %reduce-scatter.3.cloned.1.call-done = f32[128,1024]{0,1:T(8,128)} async-done(((f32[4096,1024]{0,1:T(8,128)}), f32[128,1024]{0,1:T(8,128)}) %reduce-scatter.3.cloned.1.call-update) | async-done | bytes 524304 | tf_op jit(solution)/shard_map/reduce_scatter | solution.py:191
  572.3 157.6 %all-gather.9.cloned.1.call-done = f32[4096,128]{1,0:T(8,128)} async-done(((f32[128,128]{1,0:T(8,128)}), f32[4096,128]{1,0:T(8,128)}) %all-gather.9.cloned.1.call-update) | async-done | bytes 2097168 | tf_op jit(solution)/shard_map/all_gather | solution.py:13
  729.8 1.0 while.65
  731.9 37.9 %reduce-scatter.5.cloned.1.call-done = f32[128,128]{0,1:T(8,128)} async-done(((f32[128,1024]{0,1:T(8,128)}), f32[128,128]{0,1:T(8,128)}) %reduce-scatter.5.cloned.1.call-update) | async-done | bytes 65552 | tf_op jit(solution)/shard_map/reduce_scatter | solution.py:192
  769.7 0.9 multiply_reduce_fusion.3
  771.5 1.1 convolution_bitcast_fusion.8
  773.2 1.1 copy.132
  777.7 148.1 %all-gather.11.cloned.1.call-done = f32[4096,128]{1,0:T(8,128)} async-done(((f32[128,128]{1,0:T(8,128)}), f32[4096,128]{1,0:T(8,128)}) %all-gather.11.cloned.1.call-update) | async-done | bytes 2097168 | tf_op jit(solution)/shard_map/all_gather | solution.py:13
  925.8 30.8 %while.66 = (s32[]{:T(128)}, f32[128,128]{1,0:T(8,128)S(1)}, s32[]{:T(128)}, f32[32,4]{1,0:T(8,128)S(1)}, f32[32,128,128]{2,1,0:T(8,128)}, /*index=5*/s32[128]{0...) while((s32[]{:T(128)}, f32[128,128]{1,0:T(8,128)S(1)}, s32[]{:T(128)}, ...), condition=%wide.region_20.21_spmd.clone, body=%wide.region_19.20_spmd.clone.sunk | while | flops 39942 | bytes 198819 | solution.py:22
  927.0 0.9 bitcast_add_fusion.5
  928.0 0.9 bitcast_add_fusion.5
  929.0 0.9 bitcast_add_fusion.5
  930.1 0.9 bitcast_add_fusion.5
  931.1 0.9 bitcast_add_fusion.5
  932.1 0.9 bitcast_add_fusion.5
  933.1 0.9 bitcast_add_fusion.5
  934.2 0.9 bitcast_add_fusion.5
  935.2 0.9 bitcast_add_fusion.5
  936.2 0.9 bitcast_add_fusion.5
  937.2 0.9 bitcast_add_fusion.5
  938.3 0.9 bitcast_add_fusion.5
  939.3 0.9 bitcast_add_fusion.5
  940.3 0.9 bitcast_add_fusion.5
  941.4 0.9 bitcast_add_fusion.5
  942.4 0.9 bitcast_add_fusion.5
  943.4 0.9 bitcast_add_fusion.5
  944.4 0.9 bitcast_add_fusion.5
  945.5 0.9 bitcast_add_fusion.5
  946.5 0.9 bitcast_add_fusion.5
  947.5 0.9 bitcast_add_fusion.5
  948.5 0.9 bitcast_add_fusion.5
  949.6 0.9 bitcast_add_fusion.5
  950.6 0.9 bitcast_add_fusion.5
  951.6 0.9 bitcast_add_fusion.5
  952.6 0.9 bitcast_add_fusion.5
  953.7 0.9 bitcast_add_fusion.5
  954.7 0.9 bitcast_add_fusion.5
  955.7 0.9 bitcast_add_fusion.5
  959.5 1.1 reduce_window_sum.25
  960.6 27.7 %psum.23 = f32[128,4]{1,0:T(8,128)S(1)} all-reduce(f32[128,4]{1,0:T(8,128)S(1)} %reduce_window_sum.25), channel_id=1, replica_groups=mesh['section'=8,'ctx'=32] {'section'}, use_global_device_ids=true, to_apply=%region_29.30 | all-reduce | flops 512 | bytes 4096 | tf_op jit(solution)/shard_map/psum | solution.py:211
  989.5 41.1 %all-reduce.4.cloned.1.call-done = (f32[128,512]{1,0:T(8,128)}, f32[128,512]{1,0:T(8,128)}) async-done(((f32[128,512]{1,0:T(8,128)}, f32[128,512]{1,0:T(8,128)}), (f32[128,512]{1,0:T(8,128)}, f32[128,512]{1,0:T(8,128)})) %all-reduce.4.cloned.1.call-update) | async-done | bytes 524304 | tf_op jit(solution)/shard_map/psum | solution.py:211
  1030.6 1.7 copy.212
  1032.3 1.7 copy.213
  (162 shorter events, 21.3 us)
Async XLA Ops:
  7.2 191.7 %all-gather.7.cloned.1.call-start = ((), (), s32[]{:S(2)}) async-start(), calls=%async_computation.2 | async-start | bytes 8650752 | tf_op jit(solution)/shard_map/all_gather | solution.py:104
  27.4 544.7 %reduce-scatter.3.cloned.1.call-start = ((), (), s32[]{:S(2)}) async-start(), calls=%async_computation.3 | async-start | bytes 17301504 | tf_op jit(solution)/shard_map/reduce_scatter | solution.py:191
  30.7 180.1 %copy-start.1 = (bf16[1,128,2560]{1,2,0:T(8,128)(2,1)}, bf16[1,128,2560]{1,2,0:T(8,128)(2,1)S(1)}, u32[]{:S(2)}) copy-start(bf16[1,128,2560]{1,2,0:T(8,128)(2,1)S(1)} %copy.99) | copy-start | bytes 1966084
  214.6 7.8 copy-start.2
  231.1 2.6 copy-start
  238.2 0.9 copy-start.4
  238.2 1.0 copy-start.6
  238.2 1.4 copy-start.5
  238.3 2.9 copy-start.3
  238.3 491.5 %all-gather.9.cloned.1.call-start = ((), (), s32[]{:S(2)}) async-start(), calls=%async_computation.5 | async-start | bytes 2162688 | tf_op jit(solution)/shard_map/all_gather | solution.py:13
  240.9 528.8 %reduce-scatter.5.cloned.1.call-start = ((), (), s32[]{:S(2)}) async-start(), calls=%async_computation.4 | async-start | bytes 589824 | tf_op jit(solution)/shard_map/reduce_scatter | solution.py:192
  572.2 353.6 %all-gather.11.cloned.1.call-start = ((), (), s32[]{:S(2)}) async-start(), calls=%async_computation.6 | async-start | bytes 2162688 | tf_op jit(solution)/shard_map/all_gather | solution.py:13
  772.6 258.0 %all-reduce.4.cloned.1.call-start = ((), (), s32[]{:S(2)}) async-start(), calls=%async_computation.7 | async-start | bytes 1048576 | tf_op jit(solution)/shard_map/psum | solution.py:211
Sparse Core Ops, SparseCore 0:
  27.6 171.2 all-gather.6
  238.4 333.7 reduce-scatter.2
  574.6 155.2 all-gather.8
  732.2 37.5 reduce-scatter.4
  772.7 153.0 all-gather.10
  959.4 71.1 all-reduce.3
where the time goes:
time: 1040 us
  waiting for transfers between devices  676 us (65%)
  blocking collectives  253 us (24%)
  local copies, waits for them, and re-layouts  35.4 us (3%)
  other arithmetic  34.5 us (3%)
  matrix products  26.3 us (3%)
  between operations  14.5 us (1%)
    all_gather x2, waiting for transfers between devices, prefix(): gathered = jax.tree.map(lambda a: lax.all_gather(a, axis), part)  306 us
    all_gather x1, blocking collectives, prefix(): gathered = jax.tree.map(lambda a: lax.all_gather(a, axis), part)  206 us
    all_gather x1, waiting for transfers between devices, on_device(): kv_full = lax.all_gather(own_rows, 'ctx', axis=0, tiled=True)  166 us
    reduce_scatter x1, waiting for transfers between devices, on_device(): lax.psum_scatter(grad_terms, 'ctx', scatter_dimension=0, tiled=True)  125 us
    psum x1, waiting for transfers between devices, on_device(): d_query, d_key, d_decay = lax.psum((d_query, d_key, d_decay), 'section')  41.1 us
    reduce_scatter x1, waiting for transfers between devices, on_device(): lax.psum_scatter(token_sum, 'section', scatter_dimension=1, tiled=True)  37.9 us
    psum x1, blocking collectives, on_device(): d_query, d_key, d_decay = lax.psum((d_query, d_key, d_decay), 'section')  27.7 us
    add x31, other arithmetic, combine(): column_decay[None, :] * earlier[1] + later_part[1]  27 us
  transfers between devices with their start and end apart: 6, of which 6 were waited for; matrix products, arithmetic and copies ran while one was open for 2% of the time, Pallas kernels for 0%

commit v1 on v0

v1 whole, which is shorter than its diff:
```python
import functools
import math

import jax
import jax.numpy as jnp
from jax import lax
from jax.experimental import pallas as pl
from jax.experimental.pallas import tpu as pltpu
from jax.sharding import Mesh, PartitionSpec as P

bf16 = jnp.bfloat16
f32 = jnp.float32
EXACT = lax.Precision.HIGHEST
TOK = 128
HD = 128
GROUP = 5
WIDE = GROUP * HD
EXTRA = 16
BLOCKS = 32
SCALE = HD**-0.5
LOG2E = math.log2(math.e)
CTX = ("y", "zlo", "x")
VMEM = pl.BlockSpec(memory_space=pltpu.VMEM)
SMEM = pl.BlockSpec(memory_space=pltpu.SMEM)


ANY = pl.BlockSpec(memory_space=pl.ANY)


def in_hbm(x):
    return pltpu.with_memory_space_constraint(x, pltpu.HBM)


def loaded(kernel, inputs, outputs, *refs):
    ids, far, rest = refs[0], refs[1 : 1 + inputs], refs[1 + inputs :]
    results, near, scratch = rest[:outputs], rest[outputs : outputs + inputs], rest[outputs + inputs : -1]
    copies = [pltpu.make_async_copy(f, n, rest[-1].at[i]) for i, (f, n) in enumerate(zip(far, near))]
    for copy in copies:
        copy.start()
    for copy in copies:
        copy.wait()
    kernel(ids, *near, *results, *scratch)


def call(kernel, outs, args, name, loose=0, scratch=(), limit=8, flops=0, nbytes=0, free=()):
    cost = None
    if flops:
        cost = pl.CostEstimate(flops=flops, bytes_accessed=nbytes, transcendentals=0)
    inputs = [x if i < loose else in_hbm(x) for i, x in enumerate(args[1:])]
    near = [pltpu.VMEM(x.shape, x.dtype) for x in inputs]
    return pl.pallas_call(
        functools.partial(loaded, kernel, len(inputs), len(outs)),
        out_shape=[jax.ShapeDtypeStruct(s, t) if i in free else pltpu.HBM(s, t) for i, (s, t) in enumerate(outs)],
        in_specs=[SMEM] + [ANY] * len(inputs),
        out_specs=[VMEM] * len(outs),
        scratch_shapes=near + list(scratch) + [pltpu.SemaphoreType.DMA((len(inputs),))],
        compiler_params=pltpu.CompilerParams(vmem_limit_bytes=limit * 2**20),
        cost_estimate=cost,
        name=name,
    )(args[0], *inputs)


def dot(a, b, ca, cb):
    return lax.dot_general(a, b, (((ca,), (cb,)), ((), ())), precision=EXACT, preferred_element_type=f32)


def thirds(x):
    hi = x.astype(bf16).astype(f32)
    mid = (x - hi).astype(bf16).astype(f32)
    return hi, mid, x - hi - mid


def pack_kernel(ids, q_ref, do_ref, o_ref, kv_ref, rq_ref, rk_ref, rv_ref, a_ref, *outs):
    *outs, mine, tables = outs
    row = lax.broadcasted_iota(jnp.int32, (EXTRA, HD), 0)
    ones = jnp.ones((EXTRA, HD), f32)

    def rows_of(x):
        hi, mid, lo = thirds(x)
        return jnp.where(row == 0, hi, jnp.where(row == 1, mid, jnp.where(row == 2, lo, 0.0))).astype(bf16)

    for k, out in enumerate(outs):

        @pl.when(pl.program_id(0) == k)
        def _():
            out[0:TOK, 0:WIDE] = q_ref[...]
            out[0:TOK, WIDE : 2 * WIDE] = do_ref[...]
            for h in range(GROUP):
                cols = slice(h * HD, (h + 1) * HD)
                product = do_ref[:, cols].astype(f32) * o_ref[:, cols].astype(f32)
                out[TOK : TOK + EXTRA, cols] = rows_of(dot(ones, product, 1, 1))
            out[TOK : TOK + EXTRA, WIDE : 2 * WIDE] = jnp.zeros((EXTRA, WIDE), bf16)

    @pl.when(pl.program_id(0) == 0)
    def _():
        head = ids[0]
        q = rq_ref[...].astype(f32) * SCALE
        k = rk_ref[...].astype(f32)
        v = rv_ref[...].astype(f32)
        pick = lax.broadcasted_iota(jnp.int32, a_ref.shape, 0) == head
        a = jnp.sum(jnp.where(pick, a_ref[...], 0.0), axis=0, keepdims=True)
        a = jnp.broadcast_to(a, (HD, TOK))
        t = lax.broadcasted_iota(jnp.int32, (TOK, TOK), 0)
        s = lax.broadcasted_iota(jnp.int32, (TOK, TOK), 1)
        cum = dot((s <= t).astype(f32), a, 1, 1)
        across = dot(a, (t <= s).astype(f32), 1, 0)
        decay = jnp.exp(jnp.where(s <= t, cum - across, -jnp.inf))
        total = cum[TOK - 1 : TOK, :]
        state = dot(k * jnp.exp(total - cum), v, 0, 0)
        tables[0] = q
        tables[1] = k
        tables[2] = cum
        tables[3] = decay
        tables[4] = decay * dot(q, k, 1, 1)
        tables[5] = state
        total = rows_of(jnp.broadcast_to(total, (EXTRA, HD)))
        mine[0:TOK, :] = kv_ref[...]
        high = state.astype(bf16)
        mine[TOK : TOK + HD, :] = high
        mine[TOK + HD : TOK + 2 * HD, :] = (state - high.astype(f32)).astype(bf16)
        mine[TOK + 2 * HD :, :] = total


def pack_rows(ids, queries, grad_out, attn_out, shared_kv, ret_query, ret_key, ret_value, log_decay):
    pack = (TOK + EXTRA, 2 * WIDE)
    mine = (TOK + 2 * HD + EXTRA, HD)
    tables = (6, TOK, HD)
    rows = pl.BlockSpec((TOK, WIDE), lambda k, ids: (0, lax.rem(ids[0] + k, 4)))
    own = pl.BlockSpec((TOK, HD), lambda k, ids: (0, ids[0]))
    whole = lambda shape: pl.BlockSpec(shape, lambda k, ids: (0,) * len(shape))
    args = (queries, grad_out, attn_out, shared_kv, ret_query, ret_key, ret_value, log_decay)
    return pl.pallas_call(
        pack_kernel,
        out_shape=[pltpu.HBM(pack, bf16)] * 4 + [pltpu.HBM(mine, bf16), pltpu.HBM(tables, f32)],
        grid_spec=pltpu.PrefetchScalarGridSpec(
            num_scalar_prefetch=1,
            grid=(4,),
            in_specs=[rows] * 3 + [whole(shared_kv.shape), own, own, whole(ret_value.shape), whole(log_decay.shape)],
            out_specs=[whole(pack)] * 4 + [whole(mine), whole(tables)],
        ),
        compiler_params=pltpu.CompilerParams(vmem_limit_bytes=16 * 2**20),
        name="pack_rows",
    )(ids, *map(in_hbm, args))


def copies_kernel(ids, theirs_ref, mine_ref, out_ref):
    for i in range(out_ref.shape[0]):
        out_ref[i, 0] = mine_ref[...]
        out_ref[i, 1] = theirs_ref[...]


def place_of(ids, b):
    low = lax.rem(lax.div(b, 4), 2)
    return lax.div(b, 8) * 4 + lax.rem(b, 4), lax.rem(low + lax.div(ids[1], 4), 2)


def attn_kernel(count, B, T, *refs):
    ids, own, other = refs[:3]
    packs, dqs = refs[3 : 3 + count], refs[3 + count : 3 + 2 * count]
    keep, send, ks, vs, kt, qs, dos, delta, p_s, dq_s, dk, dv = refs[3 + 2 * count :]
    c, core = ids[1], ids[2]

    def fill(out, ref):
        def one(b, _):
            i, p = place_of(ids, b)
            out[pl.ds(pl.multiple_of(b * TOK, TOK), TOK), :] = ref[i, p]
            return 0

        lax.fori_loop(0, BLOCKS, one, 0)

    @pl.when(core == 0)
    def _():
        fill(ks, own)
        fill(vs, other)

    @pl.when(core != 0)
    def _():
        fill(ks, other)
        fill(vs, own)

    for r in range(0, ks.shape[0], 512):
        kt[:, r : r + 512] = ks[r : r + 512, :].T
    for i in range(count):
        for h in range(GROUP):
            r = (i * GROUP + h) * TOK
            qs[r : r + TOK, :] = packs[i][0:TOK, h * HD : (h + 1) * HD]
            dos[r : r + TOK, :] = packs[i][0:TOK, (GROUP + h) * HD : (GROUP + h + 1) * HD]
        d = packs[i][TOK : TOK + EXTRA, 0:WIDE].astype(f32)
        delta[0:1, i * WIDE : (i + 1) * WIDE] = d[0:1] + d[1:2] + d[2:3]
    dk[...] = jnp.zeros_like(dk)
    dv[...] = jnp.zeros_like(dv)
    blocks = (c * TOK + TOK + B - 1) // B

    def tile(t, _):
        t0 = pl.multiple_of(t * T, T)
        q = qs[pl.ds(t0, T), :]
        do = dos[pl.ds(t0, T), :]
        dl = delta[0:1, pl.ds(t0, T)]

        def scores(j, m, masked):
            j0 = pl.multiple_of(j * B, B)
            s = lax.dot_general(ks[pl.ds(j0, B), :], q, (((1,), (1,)), ((), ())), preferred_element_type=f32)
            s = s * (SCALE * LOG2E)
            if masked:
                key = j0 + lax.broadcasted_iota(jnp.int32, (B, T), 0)
                row = c * TOK + (lax.broadcasted_iota(jnp.int32, (B, T), 1) & (TOK - 1))
                s = jnp.where(key <= row, s, -jnp.inf)
            p_s[pl.ds(j0, B), :] = s
            return jnp.maximum(m, jnp.max(s, axis=0, keepdims=True))

        m = jnp.full((1, T), -jnp.inf, f32)
        m = lax.fori_loop(0, blocks - 1, lambda j, m: scores(j, m, False), m)
        m = scores(blocks - 1, m, True)

        def exponents(j, total):
            rows = pl.ds(pl.multiple_of(j * B, B), B)
            e = jnp.exp2(p_s[rows, :] - m)
            p_s[rows, :] = e
            return total + jnp.sum(e, axis=0, keepdims=True)

        inverse = 1.0 / lax.fori_loop(0, blocks, exponents, jnp.zeros((1, T), f32))
        dq_s[...] = jnp.zeros_like(dq_s)

        def backward(j, _):
            j0 = pl.multiple_of(j * B, B)
            rows = pl.ds(j0, B)
            w = p_s[rows, :] * inverse
            dp = lax.dot_general(vs[rows, :], do, (((1,), (1,)), ((), ())), preferred_element_type=f32)
            ds = (w * (dp - dl)).astype(bf16)
            dv[rows, :] += jnp.dot(w.astype(bf16), do, preferred_element_type=f32).astype(bf16).astype(f32)
            part = jnp.dot(ds, q, preferred_element_type=f32) * SCALE
            dk[rows, :] += part.astype(bf16).astype(f32)
            dq_s[...] += jnp.dot(kt[:, rows], ds, preferred_element_type=f32)
            return 0

        lax.fori_loop(0, blocks, backward, 0)
        for r in range(0, T, TOK):
            qs[pl.ds(t0 + r, TOK), :] = (dq_s[:, r : r + TOK].T * SCALE).astype(bf16)
        return 0

    lax.fori_loop(0, count * WIDE // T, tile, 0)
    for i in range(count):
        for h in range(GROUP):
            r = (i * GROUP + h) * TOK
            dqs[i][:, h * HD : (h + 1) * HD] = qs[r : r + TOK, :]

    @pl.when(core == 0)
    def _():
        keep[...] = dk[...]
        send[...] = dv[...]

    @pl.when(core != 0)
    def _():
        keep[...] = dv[...]
        send[...] = dk[...]


def attention(ids, own, other, packs, B=1024, T=WIDE):
    count, length, rows = len(packs), BLOCKS * TOK, len(packs) * WIDE
    got = call(
        functools.partial(attn_kernel, count, B, T),
        [((TOK, WIDE), bf16)] * count + [((length, HD), f32)] * 2,
        [ids, own, other, *packs],
        "attention",
        1 + count,
        [
            pltpu.VMEM((length, HD), bf16),
            pltpu.VMEM((length, HD), bf16),
            pltpu.VMEM((HD, length), bf16),
            pltpu.VMEM((rows, HD), bf16),
            pltpu.VMEM((rows, HD), bf16),
            pltpu.VMEM((8, rows), f32),
            pltpu.VMEM((length, T), f32),
            pltpu.VMEM((HD, T), f32),
            pltpu.VMEM((length, HD), f32),
            pltpu.VMEM((length, HD), f32),
        ],
        limit=50,
        flops=10 * rows * length * HD,
        nbytes=12 * length * HD,
        free=(count, count + 1),
    )
    return got[:count], got[count:]


def retain_kernel(ids, all_ref, tables, v_ref, out_ref, totals_ref):
    def step(b, state):
        i, p = place_of(ids, b)
        added = all_ref[i, p, TOK : TOK + 2 * HD, :].astype(f32)
        return jnp.exp(totals_ref[pl.ds(b, 1), :]) * state + (added[0:HD] + added[HD:])

    for b in range(BLOCKS):
        i, p = place_of(ids, jnp.int32(b))
        totals_ref[b : b + 1, :] = jnp.sum(all_ref[i, p, TOK + 2 * HD :, :].astype(f32), axis=0, keepdims=True)
    state = lax.fori_loop(0, ids[1], step, jnp.zeros((HD, HD), f32))
    q, cum, inner = tables[0], tables[2], tables[4]
    out_ref[0] = state
    out_ref[1] = jnp.exp(cum[TOK - 1 : TOK, :]) * state + tables[5]
    out_ref[2] = dot(inner, v_ref[...].astype(f32), 1, 0) + dot(q * jnp.exp(cum), state, 1, 0)


def norm_kernel(ids, parts_ref, states, tables, out_ref, carry_ref):
    def add(i, total):
        return total + parts_ref[i].astype(f32)

    upstream = lax.fori_loop(1, BLOCKS, add, parts_ref[0].astype(f32))
    retained = states[2]
    inverse = lax.rsqrt(jnp.mean(retained * retained, axis=1, keepdims=True) + 1e-06)
    normed = retained * inverse
    grad = (upstream - normed * jnp.mean(normed * upstream, axis=1, keepdims=True)) * inverse
    out_ref[...] = grad
    carry_ref[...] = dot(tables[0] * jnp.exp(tables[2]), grad, 0, 0)


def decay_over(totals, low, high):
    add = lambda m, total: total + totals[pl.ds(m, 1), :]
    return jnp.exp(lax.fori_loop(low, high, add, jnp.zeros((1, HD), f32)))


def scan_x_kernel(ids, r1, r2, r3, carry_ref, totals, group_ref, out_ref, held):
    c = ids[1]
    x = lax.rem(c, 4)
    for k, ref in enumerate((carry_ref, r1, r2, r3)):
        held[k] = ref[...]

    def step(i, grad):
        m = 3 - i
        return held[lax.rem(m - x + 4, 4)] + jnp.exp(totals[pl.ds(c - x + m, 1), :]) * grad

    zero = jnp.zeros((HD, HD), f32)
    group_ref[...] = lax.fori_loop(0, 4, step, zero)
    out_ref[...] = lax.fori_loop(0, 3 - x, step, zero)


def scan_z_kernel(ids, theirs_ref, mine_ref, leaving_ref, totals, both_ref, out_ref):
    c = ids[1]
    first = lax.rem(lax.div(c, 4), 2) == 0
    start = lax.div(c, 8) * 8
    theirs, mine = theirs_ref[...], mine_ref[...]
    low, high = jnp.where(first, mine, theirs), jnp.where(first, theirs, mine)
    both_ref[...] = low + decay_over(totals, start, start + 4) * high
    out_ref[...] = leaving_ref[...] + jnp.where(first, decay_over(totals, c + 1, start + 4) * theirs, 0.0)


def grads_kernel(
    ids, r1, r2, r3, leaving_ref, totals, grad_ref, states, tables, v_ref, dv_ref, part_ref, held
):
    c = ids[1]
    y = lax.div(c, 8)
    for k, ref in enumerate((r1, r2, r3)):
        held[k] = ref[...]

    def step(i, later):
        m = 3 - i
        return held[m - y - 1] + decay_over(totals, m * 8, m * 8 + 8) * later

    later = lax.fori_loop(0, 3 - y, step, jnp.zeros((HD, HD), f32))
    leaving = leaving_ref[...] + decay_over(totals, c + 1, y * 8 + 8) * later
    grad, state = grad_ref[...], states[0]
    q, k, cum, decay, inner = (tables[i] for i in range(5))
    v = v_ref[...].astype(f32)
    total = cum[TOK - 1 : TOK, :]
    tail = jnp.exp(total - cum)
    pair = decay * dot(grad, v, 1, 1)
    dq = jnp.exp(cum) * dot(grad, state, 1, 1) + dot(pair, k, 1, 0)
    dk = dot(pair, q, 0, 0) + tail * dot(v, leaving, 1, 1)
    dv_ref[...] = dot(inner, grad, 0, 0) + tail * dot(k, leaving, 1, 0)
    through = jnp.sum(jnp.sum(leaving * states[1], axis=1, keepdims=True), axis=0, keepdims=True)
    change = jnp.sum(grad * states[2], axis=1, keepdims=True) - jnp.sum(k * dk, axis=1, keepdims=True)
    t = lax.broadcasted_iota(jnp.int32, (TOK, TOK), 0)
    s = lax.broadcasted_iota(jnp.int32, (TOK, TOK), 1)
    da = dot(jnp.broadcast_to(change, (TOK, HD)), (s <= t).astype(f32), 0, 0) + through
    part_ref[0:TOK, 0:HD] = dq * SCALE
    part_ref[0:TOK, HD : 2 * HD] = dk
    part_ref[TOK : TOK + EXTRA, 0:HD] = da[0:EXTRA]
    part_ref[TOK : TOK + EXTRA, HD : 2 * HD] = jnp.zeros((EXTRA, HD), f32)


def message_kernel(ids, a_ref, b_ref, out_ref):
    out_ref[0:TOK, :] = (a_ref[0:TOK, :] + b_ref[0:TOK, :]).astype(bf16)
    tail = slice(TOK, TOK + EXTRA)
    hi, mid, lo = thirds(a_ref[tail, :] + b_ref[tail, :])
    row = lax.broadcasted_iota(jnp.int32, hi.shape, 0)
    parts = jnp.where(row == 0, hi, jnp.where(row == 1, mid, jnp.where(row == 2, lo, 0.0)))
    out_ref[tail, :] = parts.astype(bf16)


def finish_kernel(ids, *refs):
    messages, (dq_ref, dk_ref, da_ref) = refs[:4], refs[4:]
    row = lax.broadcasted_iota(jnp.int32, da_ref.shape, 0)
    da = jnp.zeros(da_ref.shape, f32)
    for k, ref in enumerate(messages):
        head = lax.rem(ids[0] + 3 - k, 4)
        cols = pl.ds(pl.multiple_of(head * HD, HD), HD)
        dq_ref[:, cols] = ref[0:TOK, 0:HD].astype(f32)
        dk_ref[:, cols] = ref[0:TOK, HD : 2 * HD].astype(f32)
        value = jnp.sum(ref[TOK : TOK + EXTRA, 0:HD].astype(f32), axis=0, keepdims=True)
        da = jnp.where(row == head, value, da)
    da_ref[...] = da


def rows_kernel(ids, *refs):
    parts, out = refs[:4], refs[4]
    for k, ref in enumerate(parts):
        start = pl.multiple_of(lax.rem(ids[0] + 1 + k, 4) * WIDE, HD)
        out[:, pl.ds(start, WIDE)] = ref[...]


def shift(x, k):
    return lax.ppermute(x, "zhi", [(i, (i + k) % 4) for i in range(4)])


def from_next(x, axis, k):
    return lax.ppermute(x, axis, [(i, (i - k) % 4) for i in range(4)])


def swap(x):
    return lax.ppermute(x, "core", [(0, 1), (1, 0)])


def spread(x):
    return lax.all_to_all(x, CTX, 0, 0)


def on_device(queries, attn_out, grad_out, shared_kv, ret_query, ret_key, ret_value, log_decay):
    z = lax.axis_index("zhi")
    ids = jnp.stack([z, lax.axis_index(CTX), lax.axis_index("core")]).astype(jnp.int32)
    *packs, mine, tables = pack_rows(
        ids, queries[0], grad_out[0], attn_out[0], shared_kv, ret_query, ret_key, ret_value, log_decay.T
    )
    from1, from3, from2 = shift(packs[1], 1), shift(packs[3], 3), shift(packs[2], 2)
    theirs = lax.ppermute(mine, "zlo", [(0, 1), (1, 0)])
    (copies,) = call(copies_kernel, [((16, 2, *mine.shape), bf16)], [ids, theirs, mine], "copies", 1)
    blocks = lax.all_to_all(copies, ("y", "x"), 0, 0)
    own = blocks[:, :, 0:TOK]
    own, from1, from3, from2 = lax.optimization_barrier((own, from1, from3, from2))
    other = swap(own)
    (dq1, dq3, dq2, dq0), (keep, send) = attention(ids, own, other, [from1, from3, from2, packs[0]])
    back1, back3, back2 = shift(dq1, 3), shift(dq3, 1), shift(dq2, 2)

    square = ((TOK, HD), f32)
    states, totals = call(
        retain_kernel, [((3, TOK, HD), f32), ((BLOCKS, HD), f32)], [ids, blocks, tables, ret_value], "retention_forward", 1
    )
    part = (keep + swap(send)).astype(bf16)
    parts = spread(part.reshape(BLOCKS, TOK, HD))
    parts, back1, back3 = lax.optimization_barrier((parts, back1, back3))
    grad, carry = call(
        norm_kernel, [square] * 2, [ids, parts, states, tables], "norm_backward", 1, free=(1,)
    )
    held = pltpu.VMEM((4, HD, HD), f32)
    near = [from_next(carry, "x", k) for k in (1, 2, 3)]
    group, leaving = call(scan_x_kernel, [square] * 2, [ids, *near, carry, totals], "scan_x", 4, [held], free=(0, 1))
    theirs = lax.ppermute(group, "zlo", [(0, 1), (1, 0)])
    both, leaving = call(scan_z_kernel, [square] * 2, [ids, theirs, group, leaving, totals], "scan_z", 3, free=(0, 1))
    far = [from_next(both, "y", k) for k in (1, 2, 3)]
    *far, back2 = lax.optimization_barrier((*far, back2))
    d_value, half = call(
        grads_kernel,
        [square, ((TOK + EXTRA, 2 * HD), f32)],
        [ids, *far, leaving, totals, grad, states, tables, ret_value],
        "retention_grads",
        4,
        [held],
        free=(1,),
    )
    (message,) = call(
        message_kernel, [((TOK + EXTRA, 2 * HD), bf16)], [ids, swap(half), half], "message", 2, free=(0,)
    )
    d_query, d_key, d_decay = call(
        finish_kernel,
        [(ret_query.shape, f32), (ret_key.shape, f32), (log_decay.shape[::-1], f32)],
        [ids, *(shift(message, k) for k in (1, 2, 3)), message],
        "finish",
        4,
    )
    (d_queries,) = call(
        rows_kernel, [((TOK, 4 * WIDE), bf16)], [ids, back1, back2, back3, dq0], "query_rows", 3
    )
    return d_queries[None], d_query, d_key, d_value, d_decay.T


def solution(mesh):
    fine = Mesh(mesh.devices.reshape(4, 2, 4, 2, 4), ("zhi", "core", "y", "zlo", "x"))
    section = ("zhi", "core")
    rows = P(section, CTX, None)
    return jax.shard_map(
        on_device,
        mesh=fine,
        in_specs=(rows, rows, rows, P(CTX, section), P(CTX, None), P(CTX, None), P(CTX, section), P(CTX, None)),
        out_specs=(rows, P(CTX, None), P(CTX, None), P(CTX, section), P(CTX, None)),
        check_vma=False,
    )
```

time: 1040 us -> 207 us (0.20)
  waiting for transfers between devices: 676 us -> 70.9 us
  blocking collectives: 253 us -> 0 us
  starting transfers between devices: 0.42 us -> 83.4 us
  Pallas kernels: 0 us -> 46.3 us
  local copies, waits for them, and re-layouts: 35.4 us -> 0.78 us
  other arithmetic: 34.5 us -> 2.85 us
  matrix products: 26.3 us -> 0 us
  between operations: 14.5 us -> 0.96 us
    all_gather x3 -> x0, waiting for transfers between devices: 472 us -> none  [the longest x2 306 us: prefix(): gathered = jax.tree.map(lambda a: lax.all_gather(a, axis), part)]
    all_gather x2 -> x0, blocking collectives: 225 us -> none  [the longest x1 206 us: prefix(): gathered = jax.tree.map(lambda a: lax.all_gather(a, axis), part)]
    reduce_scatter x2 -> x0, waiting for transfers between devices: 162 us -> none  [the longest x1 125 us: on_device(): lax.psum_scatter(grad_terms, 'ctx', scatter_dimension=0, tiled=True)]
    pallas_call x0 -> x11, Pallas kernels: none -> 46.3 us  [the longest x10 39.5 us: call(): pl.pallas_call(functools.partial(loaded, kernel, len(inputs), len(outs)),...]
    all_to_all x0 -> x2, starting transfers between devices: none -> 44.6 us  [the longest x1 37.1 us: spread(): return lax.all_to_all(x, CTX, 0, 0)]
    psum x1 -> x0, waiting for transfers between devices: 41.1 us -> none  [on_device(): d_query, d_key, d_decay = lax.psum((d_query, d_key, d_decay), 'section')]
    ppermute x0 -> x20, waiting for transfers between devices: none -> 39.9 us  [the longest x9 20 us: shift(): return lax.ppermute(x, 'zhi', [(i, (i + k) % 4) for i in range(4)])]
    ppermute x0 -> x20, starting transfers between devices: none -> 38.9 us  [the longest x9 24.9 us: shift(): return lax.ppermute(x, 'zhi', [(i, (i + k) % 4) for i in range(4)])]
  transfers between devices with their start and end apart: 6 -> 22, of which waited for: 6 -> 13; matrix products, arithmetic and copies ran while one was open for 2% -> 0% of each run, Pallas kernels for 0% -> 5%
where the time goes in v1:
time: 207 us; the launch traced here: 205 us
  starting transfers between devices  83.4 us (40%)
  waiting for transfers between devices  70.9 us (34%)
  Pallas kernels  46.3 us (22%)
  other arithmetic  2.85 us (1%)
    pallas_call x10, Pallas kernels, call(): pl.pallas_call(functools.partial(loaded, kernel, len(inputs), len(outs)),...  39.5 us
    all_to_all x1, starting transfers between devices, spread(): return lax.all_to_all(x, CTX, 0, 0)  37.1 us
    all_to_all x1, waiting for transfers between devices, on_device(): blocks = lax.all_to_all(copies, ('y', 'x'), 0, 0)  31 us
    ppermute x9, starting transfers between devices, shift(): return lax.ppermute(x, 'zhi', [(i, (i + k) % 4) for i in range(4)])  24.9 us
    ppermute x9, waiting for transfers between devices, shift(): return lax.ppermute(x, 'zhi', [(i, (i + k) % 4) for i in range(4)])  20 us
    ppermute x6, starting transfers between devices, from_next(): return lax.ppermute(x, axis, [(i, (i - k) % 4) for i in range(4)])  10.5 us
    ppermute x3, waiting for transfers between devices, swap(): return lax.ppermute(x, 'core', [(0, 1), (1, 0)])  8.24 us
    all_to_all x1, starting transfers between devices, on_device(): blocks = lax.all_to_all(copies, ('y', 'x'), 0, 0)  7.49 us
  transfers between devices with their start and end apart: 22, of which 13 were waited for; matrix products, arithmetic and copies ran while one was open for 0% of the time, Pallas kernels for 5%

profile of v1, /device:TPU:2, one launch (start us, length us, event | category | flops | bytes accessed | tf_op | source)
XLA Modules:
  0.0 205.2 jit_solution(18166084760370162209)
XLA Ops:
  0.6 0.1 pad_add_fusion.ids.refs_0_
  0.7 6.8 %pack_rows.1 = (bf16[144,1280]{1,0:T(8,128)(2,1)}, bf16[144,1280]{1,0:T(8,128)(2,1)}, bf16[144,1280]{1,0:T(8,128)(2,1)}, bf16[144,1280]{1,0:T(8,128)(2,1)}, bf16...) custom-call(s32[3]{0:T(128)S(1)} %pad_add_fusion.ids.refs_0_, bf16[128,2560]{1,0:T(8,128)(2,1)} %bitcast.12, ...), custom_call_target="tpu_custom_call" | custom-call | tf_op jit(solution)/shard_map/pack_rows/pallas_call | solution.py:132
  7.5 1.9 collective-permute-start
  9.4 3.1 %collective-permute-done.refs_1_ = bf16[400,128]{1,0:T(8,128)(2,1)S(1)} collective-permute-done((bf16[400,128]{1,0:T(8,128)(2,1)}, bf16[400,128]{1,0:T(8,128)(2,1)S(1)}, u32[]{:S(2)}, u32[]{:S(2)}) %collective-permute-start) | collective-permute-done | bytes 102432 | tf_op jit(solution)/shard_map/ppermute | solution.py:432
  12.5 3.7 %copies.1 = bf16[16,2,400,128]{3,2,1,0:T(8,128)(2,1)} custom-call(s32[3]{0:T(128)S(1)} %pad_add_fusion.ids.refs_0_, bf16[400,128]{1,0:T(8,128)(2,1)S(1)} %collective-permute-done.refs_1_, bf16[400,128]{1,0:T(8,128)(2,1)} %get-tuple-element.41.refs_2_), custom_call_target="tpu_custom_call" | custom-call | tf_op jit(solution)/shard_map/copies/pallas_call | solution.py:51
  16.2 7.5 %all-to-all-start = ((bf16[16,2,400,128]{3,2,1,0:T(8,128)(2,1)}), bf16[16,2,400,128]{3,2,1,0:T(8,128)(2,1)S(1)}, u32[]{:S(2)}, u32[]{:S(2)}) async-start(bf16[16,2,400,128]{3,2,1,0:T(8,128)(2,1)} %copies.1), calls=%async_computation | async-start | bytes 6553600 | tf_op jit(solution)/shard_map/all_to_all | solution.py:434
  23.7 3.3 %collective-permute-start.1 = (bf16[144,1280]{1,0:T(8,128)(2,1)}, bf16[144,1280]{1,0:T(8,128)(2,1)}, u32[]{:S(2)}, u32[]{:S(2)}) collective-permute-start(bf16[144,1280]{1,0:T(8,128)(2,1)} %get-tuple-element.42), channel_id=1, source_target_pairs={{0,64},{64,128},{128,192},{192,0},{1,65},{65,129},{129,193},{193,1... | collective-permute-start | bytes 1105928 | tf_op jit(solution)/shard_map/ppermute | solution.py:410
  27.0 3.0 %collective-permute-start.2 = (bf16[144,1280]{1,0:T(8,128)(2,1)}, bf16[144,1280]{1,0:T(8,128)(2,1)}, u32[]{:S(2)}, u32[]{:S(2)}) collective-permute-start(bf16[144,1280]{1,0:T(8,128)(2,1)} %get-tuple-element.43), channel_id=1, source_target_pairs={{0,192},{64,0},{128,64},{192,128},{1,193},{65,1},{129,65},{193,129... | collective-permute-start | bytes 1105928 | tf_op jit(solution)/shard_map/ppermute | solution.py:410
  29.9 4.9 %collective-permute-start.3 = (bf16[144,1280]{1,0:T(8,128)(2,1)}, bf16[144,1280]{1,0:T(8,128)(2,1)}, u32[]{:S(2)}, u32[]{:S(2)}) collective-permute-start(bf16[144,1280]{1,0:T(8,128)(2,1)} %get-tuple-element.44), channel_id=1, source_target_pairs={{0,128},{64,192},{128,0},{192,64},{1,129},{65,193},{129,1},{193,65... | collective-permute-start | bytes 1105928 | tf_op jit(solution)/shard_map/ppermute | solution.py:410
  34.9 31.0 %all-to-all-done.refs_1_ = bf16[16,2,400,128]{3,2,1,0:T(8,128)(2,1)S(1)} async-done(((bf16[16,2,400,128]{3,2,1,0:T(8,128)(2,1)}), bf16[16,2,400,128]{3,2,1,0:T(8,128)(2,1)S(1)}, u32[]{:S(2)}, u32[]{:S(2)}) %all-to-all-start) | async-done | bytes 3276832 | tf_op jit(solution)/shard_map/all_to_all | solution.py:434
  65.9 0.1 slice.4.refs_1_
  66.0 0.0 collective-permute-done.1.refs_3_
  66.0 0.0 collective-permute-done.2.refs_4_
  66.0 0.0 collective-permute-done.3.refs_5_
  66.0 0.1 collective-permute-start.4
  66.1 2.6 %collective-permute-done.4.refs_2_ = bf16[16,2,128,128]{3,2,1,0:T(8,128)(2,1)S(1)} collective-permute-done((bf16[16,2,128,128]{3,2,1,0:T(8,128)(2,1)S(1)}, bf16[16,2,128,128]{3,2,1,0:T(8,128)(2,1)S(1)}, u32[]{:S(2)}, u32[]{:S(2)}) %collective-permute-start.4) | collective-permute-done | bytes 1048608 | tf_op jit(solution)/shard_map/ppermute | solution.py:418
  68.8 16.7 %attention.1 = (bf16[128,640]{1,0:T(8,128)(2,1)}, bf16[128,640]{1,0:T(8,128)(2,1)}, bf16[128,640]{1,0:T(8,128)(2,1)}, bf16[128,640]{1,0:T(8,128)(2,1)}, f32[4096,128]{1,0:T(8,128)}, /*index=5*/f32[4096,128]{1,0:T(8,128)}) custom-call(s32[3]{0:T(128)S(1)} %pad_add_fusion.ids.refs_0_, bf16[16,2,128,128]{3,2,1,0:T(8,128)(2,1)S(1)} %slice.4.refs_1_, ...), custom_call_target="tpu_custom_call" | custom-call | flops 13421772800 | bytes 6291456 | tf_op jit(solution)/shard_map/attention/pallas_call | solution.py:51
  85.5 0.2 collective-permute-start.5
  85.7 4.2 %collective-permute-done.5 = f32[4096,128]{1,0:T(8,128)S(1)} collective-permute-done((f32[4096,128]{1,0:T(8,128)}, f32[4096,128]{1,0:T(8,128)S(1)}, u32[]{:S(2)}, u32[]{:S(2)}) %collective-permute-start.5) | collective-permute-done | bytes 2097184 | tf_op jit(solution)/shard_map/ppermute | solution.py:418
  89.9 2.8 %add_convert_fusion = bf16[4096,128]{1,0:T(8,128)(2,1)} fusion(f32[4096,128]{1,0:T(8,128)} %get-tuple-element.50, f32[4096,128]{1,0:T(8,128)S(1)} %collective-permute-done.5), kind=kLoop, calls=%fused_computation | loop fusion | flops 1048576 | bytes 5242880 | tf_op jit(solution)/shard_map/convert_element_type | solution.py:445
  92.7 37.1 %all-to-all-start.1 = ((bf16[32,128,128]{2,1,0:T(8,128)(2,1)}), bf16[32,128,128]{2,1,0:T(8,128)(2,1)}, u32[]{:S(2)}, u32[]{:S(2)}) async-start(bf16[32,128,128]{2,1,0:T(8,128)(2,1)} %bitcast.10), calls=%async_computation.1 | async-start | bytes 2097152 | tf_op jit(solution)/shard_map/all_to_all | solution.py:422
  129.8 5.5 %collective-permute-start.6 = (bf16[128,640]{1,0:T(8,128)(2,1)}, bf16[128,640]{1,0:T(8,128)(2,1)S(1)}, u32[]{:S(2)}, u32[]{:S(2)}) collective-permute-start(bf16[128,640]{1,0:T(8,128)(2,1)} %get-tuple-element.52), channel_id=1, source_target_pairs={{0,192},{64,0},{128,64},{192,128},{1,193},{65,1},{129,65},{193,129... | collective-permute-start | bytes 491528 | tf_op jit(solution)/shard_map/ppermute | solution.py:410
  135.3 0.0 collective-permute-start.7
  135.3 3.0 %retention_forward.1 = (f32[3,128,128]{2,1,0:T(8,128)}, f32[32,128]{1,0:T(8,128)}) custom-call(s32[3]{0:T(128)S(1)} %pad_add_fusion.ids.refs_0_, bf16[16,2,400,128]{3,2,1,0:T(8,128)(2,1)S(1)} %all-to-all-done.refs_1_, f32[6,128,128]{2,1,0:T(8,128)} %get-tuple-element.56.refs_2_.refs_3_.refs_8_, bf16[128,128]{1,0:T(8,128)(2,1)} %refs_9_.1), custom_call_target="tpu_custom_call" | custom-call | tf_op jit(solution)/shard_map/retention_forward/pallas_call | solution.py:51
  138.3 0.6 collective-permute-done.6.refs_1_
  138.9 14.9 %collective-permute-done.7.refs_3_ = bf16[128,640]{1,0:T(8,128)(2,1)S(1)} collective-permute-done((bf16[128,640]{1,0:T(8,128)(2,1)}, bf16[128,640]{1,0:T(8,128)(2,1)S(1)}, u32[]{:S(2)}, u32[]{:S(2)}) %collective-permute-start.7) | collective-permute-done | bytes 163872 | tf_op jit(solution)/shard_map/ppermute | solution.py:410
  153.8 0.0 copy-start
  153.8 0.7 copy-done
  154.4 0.0 all-to-all-done.1.refs_1_
  154.4 0.0 copy-start.1
  154.4 3.1 %norm_backward.1 = (f32[128,128]{1,0:T(8,128)}, f32[128,128]{1,0:T(8,128)S(1)}) custom-call(s32[3]{0:T(128)S(1)} %pad_add_fusion.ids.refs_0_, bf16[32,128,128]{2,1,0:T(8,128)(2,1)} %all-to-all-done.1.refs_1_, f32[3,128,128]{2,1,0:T(8,128)} %get-tuple-element.57.refs_2_.refs_7_, f32[6,128,128]{2,1,0:T(8,128)} %get-tuple-element.56.refs_2_.refs_3_.refs_8_), custom_call_target="tpu_custom_call" | custom-call | tf_op jit(solution)/shard_map/norm_backward/pallas_call | solution.py:51
  157.5 1.5 collective-permute-start.10
  159.0 1.0 collective-permute-start.9
  160.1 2.2 %collective-permute-start.8 = (f32[128,128]{1,0:T(8,128)S(1)}, f32[128,128]{1,0:T(8,128)S(1)}, u32[]{:S(2)}, u32[]{:S(2)}) collective-permute-start(f32[128,128]{1,0:T(8,128)S(1)} %get-tuple-element.58.refs_4_), channel_id=1, source_target_pairs={{0,3},{1,0},{2,1},{3,2},{4,7},{5,4},{6,5},{7,6},{8,11},{9,8},{10,9... | collective-permute-start | bytes 196616 | tf_op jit(solution)/shard_map/ppermute | solution.py:414
  162.3 1.6 collective-permute-start.15
  163.9 0.0 collective-permute-done.10.refs_3_
  163.9 1.0 collective-permute-done.9.refs_2_
  164.9 0.1 collective-permute-done.8.refs_1_
  165.0 1.8 scan_x.1
  166.8 1.2 collective-permute-start.11
  168.0 4.6 %collective-permute-done.11.refs_1_ = f32[128,128]{1,0:T(8,128)S(1)} collective-permute-done((f32[128,128]{1,0:T(8,128)S(1)}, f32[128,128]{1,0:T(8,128)S(1)}, u32[]{:S(2)}, u32[]{:S(2)}) %collective-permute-start.11) | collective-permute-done | bytes 65568 | tf_op jit(solution)/shard_map/ppermute | solution.py:454
  172.5 1.6 scan_z.1
  174.2 1.5 collective-permute-start.14
  175.7 2.8 %collective-permute-start.13 = (f32[128,128]{1,0:T(8,128)S(1)}, f32[128,128]{1,0:T(8,128)S(1)}, u32[]{:S(2)}, u32[]{:S(2)}) collective-permute-start(f32[128,128]{1,0:T(8,128)S(1)} %get-tuple-element.62), channel_id=1, source_target_pairs={{0,16},{8,24},{16,0},{24,8},{1,17},{9,25},{17,1},{25,9},{2,18},{10... | collective-permute-start | bytes 196616 | tf_op jit(solution)/shard_map/ppermute | solution.py:414
  178.5 1.4 collective-permute-start.12
  179.9 0.0 collective-permute-done.15.refs_2_
  179.9 0.0 collective-permute-done.14.refs_3_
  179.9 1.6 collective-permute-done.13.refs_2_
  181.5 1.3 collective-permute-done.12.refs_1_
  182.7 4.0 %retention_grads.1 = (f32[128,128]{1,0:T(8,128)}, f32[144,256]{1,0:T(8,128)S(1)}) custom-call(s32[3]{0:T(128)S(1)} %pad_add_fusion.ids.refs_0_, f32[128,128]{1,0:T(8,128)S(1)} %collective-permute-done.12.refs_1_, f32[128,128]{1,0:T(8,128)S(1)} %collective-permute-done.13.refs_2_, f32[128,128]{1,0:T(8,128)S(1)} %collective-permute-done.14.refs_3_, ...), custom_call_target="tpu_custom_call" | custom-call | tf_op jit(solution)/shard_map/retention_grads/pallas_call | solution.py:51
  186.7 0.1 collective-permute-start.16
  186.8 1.4 collective-permute-done.16.refs_1_
  188.2 1.0 message.1.refs_4_
  189.2 3.7 %collective-permute-start.19 = (bf16[144,256]{1,0:T(8,128)(2,1)S(1)}, bf16[144,256]{1,0:T(8,128)(2,1)S(1)}, u32[]{:S(2)}, u32[]{:S(2)}) collective-permute-start(bf16[144,256]{1,0:T(8,128)(2,1)S(1)} %message.1.refs_4_), channel_id=1, source_target_pairs={{0,192},{64,0},{128,64},{192,128},{1,193},{65,1},{129,65},{193,129... | collective-permute-start | bytes 221192 | tf_op jit(solution)/shard_map/ppermute | solution.py:410
  192.8 0.6 collective-permute-start.18
  193.4 2.3 %collective-permute-start.17 = (bf16[144,256]{1,0:T(8,128)(2,1)S(1)}, bf16[144,256]{1,0:T(8,128)(2,1)S(1)}, u32[]{:S(2)}, u32[]{:S(2)}) collective-permute-start(bf16[144,256]{1,0:T(8,128)(2,1)S(1)} %message.1.refs_4_), channel_id=1, source_target_pairs={{0,64},{64,128},{128,192},{192,0},{1,65},{65,129},{129,193},{193,1... | collective-permute-start | bytes 221192 | tf_op jit(solution)/shard_map/ppermute | solution.py:410
  195.7 0.0 copy-done.1
  195.7 3.0 %query_rows.1 = bf16[128,2560]{1,0:T(8,128)(2,1)} custom-call(s32[3]{0:T(128)S(1)} %pad_add_fusion.ids.refs_0_, bf16[128,640]{1,0:T(8,128)(2,1)S(1)} %collective-permute-done.6.refs_1_, bf16[128,640]{1,0:T(8,128)(2,1)S(1)} %collective-permute-done.15.refs_2_, bf16[128,640]{1,0:T(8,128)(2,1)S(1)} %copy-done.1, bf16[128,640]{1,0:T(8,128)(2,1)} %get-tuple-element.66.refs_4_), custom_call_target="tpu_custom_call" | custom-call | tf_op jit(solution)/shard_map/query_rows/pallas_call | solution.py:51
  198.8 0.0 collective-permute-done.19.refs_3_
  198.8 4.5 %collective-permute-done.18.refs_2_ = bf16[144,256]{1,0:T(8,128)(2,1)S(1)} collective-permute-done((bf16[144,256]{1,0:T(8,128)(2,1)S(1)}, bf16[144,256]{1,0:T(8,128)(2,1)S(1)}, u32[]{:S(2)}, u32[]{:S(2)}) %collective-permute-start.18) | collective-permute-done | bytes 73760 | tf_op jit(solution)/shard_map/ppermute | solution.py:410
  203.3 0.0 collective-permute-done.17.refs_1_
  203.3 1.8 finish.1
Async XLA Ops:
  7.5 5.0 %collective-permute-start = (bf16[400,128]{1,0:T(8,128)(2,1)}, bf16[400,128]{1,0:T(8,128)(2,1)S(1)}, u32[]{:S(2)}, u32[]{:S(2)}) collective-permute-start(bf16[400,128]{1,0:T(8,128)(2,1)} %get-tuple-element.41.refs_2_), channel_id=1, source_target_pairs={{0,4},{4,0},{1,5},{5,1},{2,6},{6,2},{3,7},{7,3},{8,12},{12,8},{9,1... | collective-permute-start | bytes 307208 | tf_op jit(solution)/shard_map/ppermute | solution.py:432
  16.2 49.7 %all-to-all-start = ((bf16[16,2,400,128]{3,2,1,0:T(8,128)(2,1)}), bf16[16,2,400,128]{3,2,1,0:T(8,128)(2,1)S(1)}, u32[]{:S(2)}, u32[]{:S(2)}) async-start(bf16[16,2,400,128]{3,2,1,0:T(8,128)(2,1)} %copies.1), calls=%async_computation | async-start | bytes 6553600 | tf_op jit(solution)/shard_map/all_to_all | solution.py:434
  23.7 42.3 %collective-permute-start.1 = (bf16[144,1280]{1,0:T(8,128)(2,1)}, bf16[144,1280]{1,0:T(8,128)(2,1)}, u32[]{:S(2)}, u32[]{:S(2)}) collective-permute-start(bf16[144,1280]{1,0:T(8,128)(2,1)} %get-tuple-element.42), channel_id=1, source_target_pairs={{0,64},{64,128},{128,192},{192,0},{1,65},{65,129},{129,193},{193,1... | collective-permute-start | bytes 1105928 | tf_op jit(solution)/shard_map/ppermute | solution.py:410
  27.0 39.0 %collective-permute-start.2 = (bf16[144,1280]{1,0:T(8,128)(2,1)}, bf16[144,1280]{1,0:T(8,128)(2,1)}, u32[]{:S(2)}, u32[]{:S(2)}) collective-permute-start(bf16[144,1280]{1,0:T(8,128)(2,1)} %get-tuple-element.43), channel_id=1, source_target_pairs={{0,192},{64,0},{128,64},{192,128},{1,193},{65,1},{129,65},{193,129... | collective-permute-start | bytes 1105928 | tf_op jit(solution)/shard_map/ppermute | solution.py:410
  29.9 36.1 %collective-permute-start.3 = (bf16[144,1280]{1,0:T(8,128)(2,1)}, bf16[144,1280]{1,0:T(8,128)(2,1)}, u32[]{:S(2)}, u32[]{:S(2)}) collective-permute-start(bf16[144,1280]{1,0:T(8,128)(2,1)} %get-tuple-element.44), channel_id=1, source_target_pairs={{0,128},{64,192},{128,0},{192,64},{1,129},{65,193},{129,1},{193,65... | collective-permute-start | bytes 1105928 | tf_op jit(solution)/shard_map/ppermute | solution.py:410
  66.0 2.7 %collective-permute-start.4 = (bf16[16,2,128,128]{3,2,1,0:T(8,128)(2,1)S(1)}, bf16[16,2,128,128]{3,2,1,0:T(8,128)(2,1)S(1)}, u32[]{:S(2)}, u32[]{:S(2)}) collective-permute-start(bf16[16,2,128,128]{3,2,1,0:T(8,128)(2,1)S(1)} %slice.4.refs_1_), channel_id=1, source_target_pairs={{0,32},{32,0},{1,33},{33,1},{2,34},{34,2},{3,35},{35,3},{4,36},{36... | collective-permute-start | bytes 3145736 | tf_op jit(solution)/shard_map/ppermute | solution.py:418
  85.5 4.5 %collective-permute-start.5 = (f32[4096,128]{1,0:T(8,128)}, f32[4096,128]{1,0:T(8,128)S(1)}, u32[]{:S(2)}, u32[]{:S(2)}) collective-permute-start(f32[4096,128]{1,0:T(8,128)} %get-tuple-element.51), channel_id=1, source_target_pairs={{0,32},{32,0},{1,33},{33,1},{2,34},{34,2},{3,35},{35,3},{4,36},{36... | collective-permute-start | bytes 6291464 | tf_op jit(solution)/shard_map/ppermute | solution.py:418
  92.7 61.7 %all-to-all-start.1 = ((bf16[32,128,128]{2,1,0:T(8,128)(2,1)}), bf16[32,128,128]{2,1,0:T(8,128)(2,1)}, u32[]{:S(2)}, u32[]{:S(2)}) async-start(bf16[32,128,128]{2,1,0:T(8,128)(2,1)} %bitcast.10), calls=%async_computation.1 | async-start | bytes 2097152 | tf_op jit(solution)/shard_map/all_to_all | solution.py:422
  129.8 9.1 %collective-permute-start.6 = (bf16[128,640]{1,0:T(8,128)(2,1)}, bf16[128,640]{1,0:T(8,128)(2,1)S(1)}, u32[]{:S(2)}, u32[]{:S(2)}) collective-permute-start(bf16[128,640]{1,0:T(8,128)(2,1)} %get-tuple-element.52), channel_id=1, source_target_pairs={{0,192},{64,0},{128,64},{192,128},{1,193},{65,1},{129,65},{193,129... | collective-permute-start | bytes 491528 | tf_op jit(solution)/shard_map/ppermute | solution.py:410
  135.3 18.5 %collective-permute-start.7 = (bf16[128,640]{1,0:T(8,128)(2,1)}, bf16[128,640]{1,0:T(8,128)(2,1)S(1)}, u32[]{:S(2)}, u32[]{:S(2)}) collective-permute-start(bf16[128,640]{1,0:T(8,128)(2,1)} %get-tuple-element.53), channel_id=1, source_target_pairs={{0,64},{64,128},{128,192},{192,0},{1,65},{65,129},{129,193},{193,1... | collective-permute-start | bytes 491528 | tf_op jit(solution)/shard_map/ppermute | solution.py:410
  153.8 0.7 copy-start
  154.4 41.3 %copy-start.1 = (bf16[128,640]{1,0:T(8,128)(2,1)S(1)}, bf16[128,640]{1,0:T(8,128)(2,1)}, u32[]{:S(2)}) copy-start(bf16[128,640]{1,0:T(8,128)(2,1)} %copy-done) | copy-start | bytes 491524
  157.5 6.4 %collective-permute-start.10 = (f32[128,128]{1,0:T(8,128)S(1)}, f32[128,128]{1,0:T(8,128)S(1)}, u32[]{:S(2)}, u32[]{:S(2)}) collective-permute-start(f32[128,128]{1,0:T(8,128)S(1)} %get-tuple-element.58.refs_4_), channel_id=1, source_target_pairs={{0,1},{1,2},{2,3},{3,0},{4,5},{5,6},{6,7},{7,4},{8,9},{9,10},{10,1... | collective-permute-start | bytes 196616 | tf_op jit(solution)/shard_map/ppermute | solution.py:414
  159.0 5.9 %collective-permute-start.9 = (f32[128,128]{1,0:T(8,128)S(1)}, f32[128,128]{1,0:T(8,128)S(1)}, u32[]{:S(2)}, u32[]{:S(2)}) collective-permute-start(f32[128,128]{1,0:T(8,128)S(1)} %get-tuple-element.58.refs_4_), channel_id=1, source_target_pairs={{0,2},{1,3},{2,0},{3,1},{4,6},{5,7},{6,4},{7,5},{8,10},{9,11},{10,... | collective-permute-start | bytes 196616 | tf_op jit(solution)/shard_map/ppermute | solution.py:414
  160.1 5.0 %collective-permute-start.8 = (f32[128,128]{1,0:T(8,128)S(1)}, f32[128,128]{1,0:T(8,128)S(1)}, u32[]{:S(2)}, u32[]{:S(2)}) collective-permute-start(f32[128,128]{1,0:T(8,128)S(1)} %get-tuple-element.58.refs_4_), channel_id=1, source_target_pairs={{0,3},{1,0},{2,1},{3,2},{4,7},{5,4},{6,5},{7,6},{8,11},{9,8},{10,9... | collective-permute-start | bytes 196616 | tf_op jit(solution)/shard_map/ppermute | solution.py:414
  162.3 17.6 %collective-permute-start.15 = (bf16[128,640]{1,0:T(8,128)(2,1)}, bf16[128,640]{1,0:T(8,128)(2,1)S(1)}, u32[]{:S(2)}, u32[]{:S(2)}) collective-permute-start(bf16[128,640]{1,0:T(8,128)(2,1)} %get-tuple-element.63), channel_id=1, source_target_pairs={{0,128},{64,192},{128,0},{192,64},{1,129},{65,193},{129,1},{193,65... | collective-permute-start | bytes 491528 | tf_op jit(solution)/shard_map/ppermute | solution.py:410
  166.8 5.7 %collective-permute-start.11 = (f32[128,128]{1,0:T(8,128)S(1)}, f32[128,128]{1,0:T(8,128)S(1)}, u32[]{:S(2)}, u32[]{:S(2)}) collective-permute-start(f32[128,128]{1,0:T(8,128)S(1)} %get-tuple-element.60.refs_2_), channel_id=1, source_target_pairs={{0,4},{4,0},{1,5},{5,1},{2,6},{6,2},{3,7},{7,3},{8,12},{12,8},{9,1... | collective-permute-start | bytes 196616 | tf_op jit(solution)/shard_map/ppermute | solution.py:454
  174.2 5.7 %collective-permute-start.14 = (f32[128,128]{1,0:T(8,128)S(1)}, f32[128,128]{1,0:T(8,128)S(1)}, u32[]{:S(2)}, u32[]{:S(2)}) collective-permute-start(f32[128,128]{1,0:T(8,128)S(1)} %get-tuple-element.62), channel_id=1, source_target_pairs={{0,8},{8,16},{16,24},{24,0},{1,9},{9,17},{17,25},{25,1},{2,10},{10... | collective-permute-start | bytes 196616 | tf_op jit(solution)/shard_map/ppermute | solution.py:414
  175.7 5.8 %collective-permute-start.13 = (f32[128,128]{1,0:T(8,128)S(1)}, f32[128,128]{1,0:T(8,128)S(1)}, u32[]{:S(2)}, u32[]{:S(2)}) collective-permute-start(f32[128,128]{1,0:T(8,128)S(1)} %get-tuple-element.62), channel_id=1, source_target_pairs={{0,16},{8,24},{16,0},{24,8},{1,17},{9,25},{17,1},{25,9},{2,18},{10... | collective-permute-start | bytes 196616 | tf_op jit(solution)/shard_map/ppermute | solution.py:414
  178.5 4.3 %collective-permute-start.12 = (f32[128,128]{1,0:T(8,128)S(1)}, f32[128,128]{1,0:T(8,128)S(1)}, u32[]{:S(2)}, u32[]{:S(2)}) collective-permute-start(f32[128,128]{1,0:T(8,128)S(1)} %get-tuple-element.62), channel_id=1, source_target_pairs={{0,24},{8,0},{16,8},{24,16},{1,25},{9,1},{17,9},{25,17},{2,26},{10... | collective-permute-start | bytes 196616 | tf_op jit(solution)/shard_map/ppermute | solution.py:414
  186.7 1.5 collective-permute-start.16
  189.2 9.6 %collective-permute-start.19 = (bf16[144,256]{1,0:T(8,128)(2,1)S(1)}, bf16[144,256]{1,0:T(8,128)(2,1)S(1)}, u32[]{:S(2)}, u32[]{:S(2)}) collective-permute-start(bf16[144,256]{1,0:T(8,128)(2,1)S(1)} %message.1.refs_4_), channel_id=1, source_target_pairs={{0,192},{64,0},{128,64},{192,128},{1,193},{65,1},{129,65},{193,129... | collective-permute-start | bytes 221192 | tf_op jit(solution)/shard_map/ppermute | solution.py:410
  192.8 10.4 %collective-permute-start.18 = (bf16[144,256]{1,0:T(8,128)(2,1)S(1)}, bf16[144,256]{1,0:T(8,128)(2,1)S(1)}, u32[]{:S(2)}, u32[]{:S(2)}) collective-permute-start(bf16[144,256]{1,0:T(8,128)(2,1)S(1)} %message.1.refs_4_), channel_id=1, source_target_pairs={{0,128},{64,192},{128,0},{192,64},{1,129},{65,193},{129,1},{193,65... | collective-permute-start | bytes 221192 | tf_op jit(solution)/shard_map/ppermute | solution.py:410
  193.4 9.8 %collective-permute-start.17 = (bf16[144,256]{1,0:T(8,128)(2,1)S(1)}, bf16[144,256]{1,0:T(8,128)(2,1)S(1)}, u32[]{:S(2)}, u32[]{:S(2)}) collective-permute-start(bf16[144,256]{1,0:T(8,128)(2,1)S(1)} %message.1.refs_4_), channel_id=1, source_target_pairs={{0,64},{64,128},{128,192},{192,0},{1,65},{65,129},{129,193},{193,1... | collective-permute-start | bytes 221192 | tf_op jit(solution)/shard_map/ppermute | solution.py:410

commit v2 on v1

--- a/solution.py
+++ b/solution.py
@@ -70,15 +70,41 @@
     return hi, mid, x - hi - mid
 
 
-def pack_kernel(ids, q_ref, do_ref, o_ref, kv_ref, rq_ref, rk_ref, rv_ref, a_ref, *outs):
-    *outs, mine, tables = outs
-    row = lax.broadcasted_iota(jnp.int32, (EXTRA, HD), 0)
-    ones = jnp.ones((EXTRA, HD), f32)
-
-    def rows_of(x):
-        hi, mid, lo = thirds(x)
-        return jnp.where(row == 0, hi, jnp.where(row == 1, mid, jnp.where(row == 2, lo, 0.0))).astype(bf16)
-
+def rows_of(x):
+    row = lax.broadcasted_iota(jnp.int32, x.shape, 0)
+    hi, mid, lo = thirds(x)
+    return jnp.where(row == 0, hi, jnp.where(row == 1, mid, jnp.where(row == 2, lo, 0.0))).astype(bf16)
+
+
+def local_kernel(ids, kv_ref, rq_ref, rk_ref, rv_ref, a_ref, mine, tables):
+    head = ids[0]
+    cols = pl.ds(pl.multiple_of(head * HD, HD), HD)
+    q = rq_ref[:, cols].astype(f32) * SCALE
+    k = rk_ref[:, cols].astype(f32)
+    v = rv_ref[...].astype(f32)
+    pick = lax.broadcasted_iota(jnp.int32, a_ref.shape, 0) == head
+    a = jnp.sum(jnp.where(pick, a_ref[...], 0.0), axis=0, keepdims=True)
+    a = jnp.broadcast_to(a, (HD, TOK))
+    t = lax.broadcasted_iota(jnp.int32, (TOK, TOK), 0)
+    s = lax.broadcasted_iota(jnp.int32, (TOK, TOK), 1)
+    cum = dot((s <= t).astype(f32), a, 1, 1)
+    across = dot(a, (t <= s).astype(f32), 1, 0)
+    decay = jnp.exp(jnp.where(s <= t, cum - across, -jnp.inf))
+    total = cum[TOK - 1 : TOK, :]
+    state = dot(k * jnp.exp(total - cum), v, 0, 0)
+    mine[0:TOK, :] = kv_ref[...]
+    mine[TOK : TOK + HD, :] = state.astype(bf16)
+    mine[TOK + HD :, :] = rows_of(jnp.broadcast_to(total, (EXTRA, HD)))
+    tables[0] = q
+    tables[1] = k
+    tables[2] = cum
+    tables[3] = decay
+    tables[4] = decay * dot(q, k, 1, 1)
+    tables[5] = state
+
+
+def pack_kernel(ids, q_ref, do_ref, o_ref, *outs):
+    ones = jnp.ones((EXTRA, HD), bf16)
     for k, out in enumerate(outs):
 
         @pl.when(pl.program_id(0) == k)
@@ -88,55 +114,26 @@
             for h in range(GROUP):
                 cols = slice(h * HD, (h + 1) * HD)
                 product = do_ref[:, cols].astype(f32) * o_ref[:, cols].astype(f32)
-                out[TOK : TOK + EXTRA, cols] = rows_of(dot(ones, product, 1, 1))
+                hi = product.astype(bf16)
+                lo = (product - hi.astype(f32)).astype(bf16)
+                delta = [
+                    lax.dot_general(ones, x, (((1,), (1,)), ((), ())), preferred_element_type=f32) for x in (hi, lo)
+                ]
+                out[TOK : TOK + EXTRA, cols] = rows_of(delta[0] + delta[1])
             out[TOK : TOK + EXTRA, WIDE : 2 * WIDE] = jnp.zeros((EXTRA, WIDE), bf16)
 
-    @pl.when(pl.program_id(0) == 0)
-    def _():
-        head = ids[0]
-        q = rq_ref[...].astype(f32) * SCALE
-        k = rk_ref[...].astype(f32)
-        v = rv_ref[...].astype(f32)
-        pick = lax.broadcasted_iota(jnp.int32, a_ref.shape, 0) == head
-        a = jnp.sum(jnp.where(pick, a_ref[...], 0.0), axis=0, keepdims=True)
-        a = jnp.broadcast_to(a, (HD, TOK))
-        t = lax.broadcasted_iota(jnp.int32, (TOK, TOK), 0)
-        s = lax.broadcasted_iota(jnp.int32, (TOK, TOK), 1)
-        cum = dot((s <= t).astype(f32), a, 1, 1)
-        across = dot(a, (t <= s).astype(f32), 1, 0)
-        decay = jnp.exp(jnp.where(s <= t, cum - across, -jnp.inf))
-        total = cum[TOK - 1 : TOK, :]
-        state = dot(k * jnp.exp(total - cum), v, 0, 0)
-        tables[0] = q
-        tables[1] = k
-        tables[2] = cum
-        tables[3] = decay
-        tables[4] = decay * dot(q, k, 1, 1)
-        tables[5] = state
-        total = rows_of(jnp.broadcast_to(total, (EXTRA, HD)))
-        mine[0:TOK, :] = kv_ref[...]
-        high = state.astype(bf16)
-        mine[TOK : TOK + HD, :] = high
-        mine[TOK + HD : TOK + 2 * HD, :] = (state - high.astype(f32)).astype(bf16)
-        mine[TOK + 2 * HD :, :] = total
-
-
-def pack_rows(ids, queries, grad_out, attn_out, shared_kv, ret_query, ret_key, ret_value, log_decay):
+
+def pack_rows(ids, *args):
     pack = (TOK + EXTRA, 2 * WIDE)
-    mine = (TOK + 2 * HD + EXTRA, HD)
-    tables = (6, TOK, HD)
     rows = pl.BlockSpec((TOK, WIDE), lambda k, ids: (0, lax.rem(ids[0] + k, 4)))
-    own = pl.BlockSpec((TOK, HD), lambda k, ids: (0, ids[0]))
-    whole = lambda shape: pl.BlockSpec(shape, lambda k, ids: (0,) * len(shape))
-    args = (queries, grad_out, attn_out, shared_kv, ret_query, ret_key, ret_value, log_decay)
     return pl.pallas_call(
         pack_kernel,
-        out_shape=[pltpu.HBM(pack, bf16)] * 4 + [pltpu.HBM(mine, bf16), pltpu.HBM(tables, f32)],
+        out_shape=[pltpu.HBM(pack, bf16)] * 4,
         grid_spec=pltpu.PrefetchScalarGridSpec(
             num_scalar_prefetch=1,
             grid=(4,),
-            in_specs=[rows] * 3 + [whole(shared_kv.shape), own, own, whole(ret_value.shape), whole(log_decay.shape)],
-            out_specs=[whole(pack)] * 4 + [whole(mine), whole(tables)],
+            in_specs=[rows] * 3,
+            out_specs=[pl.BlockSpec(pack, lambda k, ids: (0, 0))] * 4,
         ),
         compiler_params=pltpu.CompilerParams(vmem_limit_bytes=16 * 2**20),
         name="pack_rows",
@@ -189,9 +186,11 @@
         delta[0:1, i * WIDE : (i + 1) * WIDE] = d[0:1] + d[1:2] + d[2:3]
     dk[...] = jnp.zeros_like(dk)
     dv[...] = jnp.zeros_like(dv)
-    blocks = (c * TOK + TOK + B - 1) // B
+    turned = c + 8 * (3 - 2 * lax.div(c, 8))
 
     def tile(t, _):
+        at = jnp.where(t < count // 2, turned, c)
+        blocks = lax.div(at * TOK + TOK + B - 1, B)
         t0 = pl.multiple_of(t * T, T)
         q = qs[pl.ds(t0, T), :]
         do = dos[pl.ds(t0, T), :]
@@ -203,7 +202,7 @@
             s = s * (SCALE * LOG2E)
             if masked:
                 key = j0 + lax.broadcasted_iota(jnp.int32, (B, T), 0)
-                row = c * TOK + (lax.broadcasted_iota(jnp.int32, (B, T), 1) & (TOK - 1))
+                row = at * TOK + (lax.broadcasted_iota(jnp.int32, (B, T), 1) & (TOK - 1))
                 s = jnp.where(key <= row, s, -jnp.inf)
             p_s[pl.ds(j0, B), :] = s
             return jnp.maximum(m, jnp.max(s, axis=0, keepdims=True))
@@ -247,19 +246,19 @@
     @pl.when(core == 0)
     def _():
         keep[...] = dk[...]
-        send[...] = dv[...]
+        send[...] = dv[...].astype(bf16)
 
     @pl.when(core != 0)
     def _():
         keep[...] = dv[...]
-        send[...] = dk[...]
+        send[...] = dk[...].astype(bf16)
 
 
 def attention(ids, own, other, packs, B=1024, T=WIDE):
     count, length, rows = len(packs), BLOCKS * TOK, len(packs) * WIDE
     got = call(
         functools.partial(attn_kernel, count, B, T),
-        [((TOK, WIDE), bf16)] * count + [((length, HD), f32)] * 2,
+        [((TOK, WIDE), bf16)] * count + [((length, HD), f32), ((length, HD), bf16)],
         [ids, own, other, *packs],
         "attention",
         1 + count,
@@ -275,7 +274,7 @@
             pltpu.VMEM((length, HD), f32),
             pltpu.VMEM((length, HD), f32),
         ],
-        limit=50,
+        limit=44,
         flops=10 * rows * length * HD,
         nbytes=12 * length * HD,
         free=(count, count + 1),
@@ -286,12 +285,11 @@
 def retain_kernel(ids, all_ref, tables, v_ref, out_ref, totals_ref):
     def step(b, state):
         i, p = place_of(ids, b)
-        added = all_ref[i, p, TOK : TOK + 2 * HD, :].astype(f32)
-        return jnp.exp(totals_ref[pl.ds(b, 1), :]) * state + (added[0:HD] + added[HD:])
+        return jnp.exp(totals_ref[pl.ds(b, 1), :]) * state + all_ref[i, p, TOK : TOK + HD, :].astype(f32)
 
     for b in range(BLOCKS):
         i, p = place_of(ids, jnp.int32(b))
-        totals_ref[b : b + 1, :] = jnp.sum(all_ref[i, p, TOK + 2 * HD :, :].astype(f32), axis=0, keepdims=True)
+        totals_ref[b : b + 1, :] = jnp.sum(all_ref[i, p, TOK + HD :, :].astype(f32), axis=0, keepdims=True)
     state = lax.fori_loop(0, ids[1], step, jnp.zeros((HD, HD), f32))
     q, cum, inner = tables[0], tables[2], tables[4]
     out_ref[0] = state
@@ -406,8 +404,11 @@
         out[:, pl.ds(start, WIDE)] = ref[...]
 
 
-def shift(x, k):
-    return lax.ppermute(x, "zhi", [(i, (i + k) % 4) for i in range(4)])
+def shift(x, k, turn=False):
+    if not turn:
+        return lax.ppermute(x, "zhi", [(i, (i + k) % 4) for i in range(4)])
+    pairs = [(4 * i + y, (i + k) % 4 * 4 + 3 - y) for i in range(4) for y in range(4)]
+    return lax.ppermute(x, ("zhi", "y"), pairs)
 
 
 def from_next(x, axis, k):
@@ -425,24 +426,30 @@
 def on_device(queries, attn_out, grad_out, shared_kv, ret_query, ret_key, ret_value, log_decay):
     z = lax.axis_index("zhi")
     ids = jnp.stack([z, lax.axis_index(CTX), lax.axis_index("core")]).astype(jnp.int32)
-    *packs, mine, tables = pack_rows(
-        ids, queries[0], grad_out[0], attn_out[0], shared_kv, ret_query, ret_key, ret_value, log_decay.T
-    )
-    from1, from3, from2 = shift(packs[1], 1), shift(packs[3], 3), shift(packs[2], 2)
+    mine, tables = call(
+        local_kernel,
+        [((TOK + HD + EXTRA, HD), bf16), ((6, TOK, HD), f32)],
+        [ids, shared_kv, ret_query, ret_key, ret_value, log_decay.T],
+        "retention_local",
+        free=(0,),
+    )
+    packs = pack_rows(ids, queries[0], grad_out[0], attn_out[0])
     theirs = lax.ppermute(mine, "zlo", [(0, 1), (1, 0)])
-    (copies,) = call(copies_kernel, [((16, 2, *mine.shape), bf16)], [ids, theirs, mine], "copies", 1)
+    theirs, packs = lax.optimization_barrier((theirs, packs))
+    from1, from3, from2 = shift(packs[1], 1, True), shift(packs[3], 3, True), shift(packs[2], 2)
+    (copies,) = call(copies_kernel, [((16, 2, *mine.shape), bf16)], [ids, theirs, mine], "copies", 2)
     blocks = lax.all_to_all(copies, ("y", "x"), 0, 0)
     own = blocks[:, :, 0:TOK]
     own, from1, from3, from2 = lax.optimization_barrier((own, from1, from3, from2))
     other = swap(own)
     (dq1, dq3, dq2, dq0), (keep, send) = attention(ids, own, other, [from1, from3, from2, packs[0]])
-    back1, back3, back2 = shift(dq1, 3), shift(dq3, 1), shift(dq2, 2)
+    back1, back3, back2 = shift(dq1, 3, True), shift(dq3, 1, True), shift(dq2, 2)
 
     square = ((TOK, HD), f32)
     states, totals = call(
         retain_kernel, [((3, TOK, HD), f32), ((BLOCKS, HD), f32)], [ids, blocks, tables, ret_value], "retention_forward", 1
     )
-    part = (keep + swap(send)).astype(bf16)
+    part = (keep + swap(send).astype(f32)).astype(bf16)
     parts = spread(part.reshape(BLOCKS, TOK, HD))
     parts, back1, back3 = lax.optimization_barrier((parts, back1, back3))
     grad, carry = call(

time: 207 us -> 197 us (0.952)
  starting transfers between devices: 83.4 us -> 61.6 us
  Pallas kernels: 46.3 us -> 58.1 us
    all_to_all x1, starting transfers between devices: 37.1 us -> 5.22 us  [spread(): return lax.all_to_all(x, CTX, 0, 0)]
    ppermute x0 -> x4, waiting for transfers between devices: none -> 23.3 us  [shift(): return lax.ppermute(x, ('zhi', 'y'), pairs)]
    ppermute x0 -> x4, starting transfers between devices: none -> 17.2 us  [shift(): return lax.ppermute(x, ('zhi', 'y'), pairs)]
    ppermute x9 -> x5, waiting for transfers between devices: 20 us -> 3.49 us  [shift(): return lax.ppermute(x, 'zhi', [(i, (i + k) % 4) for i in range(4)])]
    pallas_call x10 -> x11, Pallas kernels: 39.5 us -> 53.2 us  [call(): pl.pallas_call(functools.partial(loaded, kernel, len(inputs), len(outs)),...]
    ppermute x9 -> x5, starting transfers between devices: 24.9 us -> 21 us  [shift(): return lax.ppermute(x, 'zhi', [(i, (i + k) % 4) for i in range(4)])]
    ppermute x1, waiting for transfers between devices: 3.08 us -> 0.01 us  [on_device(): theirs = lax.ppermute(mine, 'zlo', [(0, 1), (1, 0)])]
    all_to_all x1, waiting for transfers between devices: 31 us -> 28.5 us  [on_device(): blocks = lax.all_to_all(copies, ('y', 'x'), 0, 0)]
  transfers between devices with their start and end apart: 22 -> 22, of which waited for: 13 -> 12; matrix products, arithmetic and copies ran while one was open for 0% -> 0% of each run, Pallas kernels for 5% -> 7%
where the time goes in v2:
time: 197 us; the launch traced here: 193 us
  waiting for transfers between devices  70.4 us (36%)
  starting transfers between devices  61.6 us (31%)
  Pallas kernels  58.1 us (29%)
    pallas_call x11, Pallas kernels, call(): pl.pallas_call(functools.partial(loaded, kernel, len(inputs), len(outs)),...  53.2 us
    all_to_all x1, waiting for transfers between devices, on_device(): blocks = lax.all_to_all(copies, ('y', 'x'), 0, 0)  28.5 us
    ppermute x4, waiting for transfers between devices, shift(): return lax.ppermute(x, ('zhi', 'y'), pairs)  23.3 us
    ppermute x5, starting transfers between devices, shift(): return lax.ppermute(x, 'zhi', [(i, (i + k) % 4) for i in range(4)])  21 us
    ppermute x4, starting transfers between devices, shift(): return lax.ppermute(x, ('zhi', 'y'), pairs)  17.2 us
    ppermute x6, starting transfers between devices, from_next(): return lax.ppermute(x, axis, [(i, (i - k) % 4) for i in range(4)])  8.24 us
    all_to_all x1, starting transfers between devices, on_device(): blocks = lax.all_to_all(copies, ('y', 'x'), 0, 0)  7.49 us
    ppermute x3, waiting for transfers between devices, swap(): return lax.ppermute(x, 'core', [(0, 1), (1, 0)])  6.55 us
  transfers between devices with their start and end apart: 22, of which 12 were waited for; matrix products, arithmetic and copies ran while one was open for 0% of the time, Pallas kernels for 7%

profile of v2, /device:TPU:2, one launch (start us, length us, event | category | flops | bytes accessed | tf_op | source)
XLA Modules:
  0.0 193.2 jit_solution(1199366617542004325)
XLA Ops:
  0.6 0.1 pad_add_fusion.refs_0_.ids
  0.7 2.9 %retention_local.1 = (bf16[272,128]{1,0:T(8,128)(2,1)S(1)}, f32[6,128,128]{2,1,0:T(8,128)}) custom-call(s32[3]{0:T(128)S(1)} %pad_add_fusion.refs_0_.ids, bf16[128,128]{1,0:T(8,128)(2,1)} %refs_1_.1, bf16[128,512]{1,0:T(8,128)(2,1)} %refs_2_.1, bf16[128,512]{1,0:T(8,128)(2,1)} %refs_3_.2, bf16[128,128]{1,0:T(8,128)(2,1)} %refs_9_.1, f32[4,128]{1,0:T(4,128)} %bitcast.15), custom_call_target="tpu_custom_call" | custom-call | tf_op jit(solution)/shard_map/retention_local/pallas_call | solution.py:51
  3.6 2.0 %collective-permute-start = (bf16[272,128]{1,0:T(8,128)(2,1)S(1)}, bf16[272,128]{1,0:T(8,128)(2,1)S(1)}, u32[]{:S(2)}, u32[]{:S(2)}) collective-permute-start(bf16[272,128]{1,0:T(8,128)(2,1)S(1)} %get-tuple-element.46.refs_2_), channel_id=1, source_target_pairs={{0,4},{4,0},{1,5},{5,1},{2,6},{6,2},{3,7},{7,3},{8,12},{12,8},{9,1... | collective-permute-start | bytes 208904 | tf_op jit(solution)/shard_map/ppermute | solution.py:437
  5.7 4.9 %pack_rows.1 = (bf16[144,1280]{1,0:T(8,128)(2,1)}, bf16[144,1280]{1,0:T(8,128)(2,1)}, bf16[144,1280]{1,0:T(8,128)(2,1)}, bf16[144,1280]{1,0:T(8,128)(2,1)}) custom-call(s32[3]{0:T(128)S(1)} %pad_add_fusion.refs_0_.ids, bf16[128,2560]{1,0:T(8,128)(2,1)} %bitcast.11, bf16[128,2560]{1,0:T(8,128)(2,1)} %bitcast.12, bf16[128,2560]{1,0:T(8,128)(2,1)} %bitcast.13), custom_call_target="tpu_custom_call" | custom-call | tf_op jit(solution)/shard_map/pack_rows/pallas_call | solution.py:129
  10.6 0.0 collective-permute-done.refs_1_
  10.6 2.4 %copies.1 = bf16[16,2,272,128]{3,2,1,0:T(8,128)(2,1)} custom-call(s32[3]{0:T(128)S(1)} %pad_add_fusion.refs_0_.ids, bf16[272,128]{1,0:T(8,128)(2,1)S(1)} %collective-permute-done.refs_1_, bf16[272,128]{1,0:T(8,128)(2,1)S(1)} %get-tuple-element.46.refs_2_), custom_call_target="tpu_custom_call" | custom-call | tf_op jit(solution)/shard_map/copies/pallas_call | solution.py:51
  13.0 7.5 %all-to-all-start = ((bf16[16,2,272,128]{3,2,1,0:T(8,128)(2,1)}), bf16[16,2,272,128]{3,2,1,0:T(8,128)(2,1)S(1)}, u32[]{:S(2)}, u32[]{:S(2)}) async-start(bf16[16,2,272,128]{3,2,1,0:T(8,128)(2,1)} %copies.1), calls=%async_computation | async-start | bytes 4456448 | tf_op jit(solution)/shard_map/all_to_all | solution.py:441
  20.5 5.4 %collective-permute-start.1 = (bf16[144,1280]{1,0:T(8,128)(2,1)}, bf16[144,1280]{1,0:T(8,128)(2,1)S(1)}, u32[]{:S(2)}, u32[]{:S(2)}) collective-permute-start(bf16[144,1280]{1,0:T(8,128)(2,1)} %get-tuple-element.52), channel_id=1, source_target_pairs={{0,88},{8,80},{16,72},{24,64},{64,152},{72,144},{80,136},{88,128},... | collective-permute-start | bytes 1105928 | tf_op jit(solution)/shard_map/ppermute | solution.py:411
  25.9 2.2 %collective-permute-start.2 = (bf16[144,1280]{1,0:T(8,128)(2,1)}, bf16[144,1280]{1,0:T(8,128)(2,1)S(1)}, u32[]{:S(2)}, u32[]{:S(2)}) collective-permute-start(bf16[144,1280]{1,0:T(8,128)(2,1)} %get-tuple-element.53), channel_id=1, source_target_pairs={{0,216},{8,208},{16,200},{24,192},{64,24},{72,16},{80,8},{88,0},{1... | collective-permute-start | bytes 1105928 | tf_op jit(solution)/shard_map/ppermute | solution.py:411
  28.1 4.9 %collective-permute-start.3 = (bf16[144,1280]{1,0:T(8,128)(2,1)}, bf16[144,1280]{1,0:T(8,128)(2,1)S(1)}, u32[]{:S(2)}, u32[]{:S(2)}) collective-permute-start(bf16[144,1280]{1,0:T(8,128)(2,1)} %get-tuple-element.54), channel_id=1, source_target_pairs={{0,128},{64,192},{128,0},{192,64},{1,129},{65,193},{129,1},{193,65... | collective-permute-start | bytes 1105928 | tf_op jit(solution)/shard_map/ppermute | solution.py:409
  33.0 28.5 %all-to-all-done.refs_1_ = bf16[16,2,272,128]{3,2,1,0:T(8,128)(2,1)S(1)} async-done(((bf16[16,2,272,128]{3,2,1,0:T(8,128)(2,1)}), bf16[16,2,272,128]{3,2,1,0:T(8,128)(2,1)S(1)}, u32[]{:S(2)}, u32[]{:S(2)}) %all-to-all-start) | async-done | bytes 2228256 | tf_op jit(solution)/shard_map/all_to_all | solution.py:441
  61.5 0.1 slice.4.refs_1_
  61.6 0.0 collective-permute-done.1.refs_3_
  61.6 9.8 %collective-permute-done.2.refs_4_ = bf16[144,1280]{1,0:T(8,128)(2,1)S(1)} collective-permute-done((bf16[144,1280]{1,0:T(8,128)(2,1)}, bf16[144,1280]{1,0:T(8,128)(2,1)S(1)}, u32[]{:S(2)}, u32[]{:S(2)}) %collective-permute-start.2) | collective-permute-done | bytes 368672 | tf_op jit(solution)/shard_map/ppermute | solution.py:411
  71.5 0.0 collective-permute-done.3.refs_5_
  71.5 0.0 collective-permute-start.4
  71.5 2.7 %collective-permute-done.4.refs_2_ = bf16[16,2,128,128]{3,2,1,0:T(8,128)(2,1)S(1)} collective-permute-done((bf16[16,2,128,128]{3,2,1,0:T(8,128)(2,1)S(1)}, bf16[16,2,128,128]{3,2,1,0:T(8,128)(2,1)S(1)}, u32[]{:S(2)}, u32[]{:S(2)}) %collective-permute-start.4) | collective-permute-done | bytes 1048608 | tf_op jit(solution)/shard_map/ppermute | solution.py:419
  74.1 29.0 %attention.1 = (bf16[128,640]{1,0:T(8,128)(2,1)}, bf16[128,640]{1,0:T(8,128)(2,1)}, bf16[128,640]{1,0:T(8,128)(2,1)}, bf16[128,640]{1,0:T(8,128)(2,1)}, f32[4096...) custom-call(s32[3]{0:T(128)S(1)} %pad_add_fusion.refs_0_.ids, bf16[16,2,128,128]{3,2,1,0:T(8,128)(2,1)S(1)} %slice.4.refs_1_, ...), custom_call_target="tpu_custom_call" | custom-call | flops 13421772800 | bytes 6291456 | tf_op jit(solution)/shard_map/attention/pallas_call | solution.py:51
  103.1 0.2 collective-permute-start.5
  103.3 2.5 %collective-permute-done.5 = bf16[4096,128]{1,0:T(8,128)(2,1)S(1)} collective-permute-done((bf16[4096,128]{1,0:T(8,128)(2,1)S(1)}, bf16[4096,128]{1,0:T(8,128)(2,1)S(1)}, u32[]{:S(2)}, u32[]{:S(2)}) %collective-permute-start.5) | collective-permute-done | bytes 1048608 | tf_op jit(solution)/shard_map/ppermute | solution.py:419
  105.9 1.2 add_convert_fusion
  107.0 5.2 %all-to-all-start.1 = ((bf16[32,128,128]{2,1,0:T(8,128)(2,1)}), bf16[32,128,128]{2,1,0:T(8,128)(2,1)S(1)}, u32[]{:S(2)}, u32[]{:S(2)}) async-start(bf16[32,128,128]{2,1,0:T(8,128)(2,1)} %bitcast.10), calls=%async_computation.1 | async-start | bytes 2097152 | tf_op jit(solution)/shard_map/all_to_all | solution.py:423
  112.3 6.6 %collective-permute-start.6 = (bf16[128,640]{1,0:T(8,128)(2,1)}, bf16[128,640]{1,0:T(8,128)(2,1)S(1)}, u32[]{:S(2)}, u32[]{:S(2)}) collective-permute-start(bf16[128,640]{1,0:T(8,128)(2,1)} %get-tuple-element.62), channel_id=1, source_target_pairs={{0,216},{8,208},{16,200},{24,192},{64,24},{72,16},{80,8},{88,0},{1... | collective-permute-start | bytes 491528 | tf_op jit(solution)/shard_map/ppermute | solution.py:411
  118.9 3.0 %collective-permute-start.7 = (bf16[128,640]{1,0:T(8,128)(2,1)}, bf16[128,640]{1,0:T(8,128)(2,1)S(1)}, u32[]{:S(2)}, u32[]{:S(2)}) collective-permute-start(bf16[128,640]{1,0:T(8,128)(2,1)} %get-tuple-element.63), channel_id=1, source_target_pairs={{0,88},{8,80},{16,72},{24,64},{64,152},{72,144},{80,136},{88,128},... | collective-permute-start | bytes 491528 | tf_op jit(solution)/shard_map/ppermute | solution.py:411
  121.9 2.9 %retention_forward.1 = (f32[3,128,128]{2,1,0:T(8,128)}, f32[32,128]{1,0:T(8,128)}) custom-call(s32[3]{0:T(128)S(1)} %pad_add_fusion.refs_0_.ids, bf16[16,2,272,128]{3,2,1,0:T(8,128)(2,1)S(1)} %all-to-all-done.refs_1_, f32[6,128,128]{2,1,0:T(8,128)} %get-tuple-element.66.refs_2_.refs_3_.refs_8_, bf16[128,128]{1,0:T(8,128)(2,1)} %refs_9_.1), custom_call_target="tpu_custom_call" | custom-call | tf_op jit(solution)/shard_map/retention_forward/pallas_call | solution.py:51
  124.8 2.2 %collective-permute-done.6.refs_1_ = bf16[128,640]{1,0:T(8,128)(2,1)S(1)} collective-permute-done((bf16[128,640]{1,0:T(8,128)(2,1)}, bf16[128,640]{1,0:T(8,128)(2,1)S(1)}, u32[]{:S(2)}, u32[]{:S(2)}) %collective-permute-start.6) | collective-permute-done | bytes 163872 | tf_op jit(solution)/shard_map/ppermute | solution.py:411
  127.0 11.2 %collective-permute-done.7.refs_3_ = bf16[128,640]{1,0:T(8,128)(2,1)S(1)} collective-permute-done((bf16[128,640]{1,0:T(8,128)(2,1)}, bf16[128,640]{1,0:T(8,128)(2,1)S(1)}, u32[]{:S(2)}, u32[]{:S(2)}) %collective-permute-start.7) | collective-permute-done | bytes 163872 | tf_op jit(solution)/shard_map/ppermute | solution.py:411
  138.2 0.0 copy-start
  138.2 0.7 copy-done
  138.9 0.0 all-to-all-done.1.refs_1_
  138.9 0.0 copy-start.1
  138.9 2.9 %norm_backward.1 = (f32[128,128]{1,0:T(8,128)}, f32[128,128]{1,0:T(8,128)S(1)}) custom-call(s32[3]{0:T(128)S(1)} %pad_add_fusion.refs_0_.ids, bf16[32,128,128]{2,1,0:T(8,128)(2,1)S(1)} %all-to-all-done.1.refs_1_, f32[3,128,128]{2,1,0:T(8,128)} %get-tuple-element.67.refs_2_.refs_7_, f32[6,128,128]{2,1,0:T(8,128)} %get-tuple-element.66.refs_2_.refs_3_.refs_8_), custom_call_target="tpu_custom_call" | custom-call | tf_op jit(solution)/shard_map/norm_backward/pallas_call | solution.py:51
  141.8 0.9 collective-permute-start.10
  142.7 1.2 collective-permute-start.9
  143.9 2.1 %collective-permute-start.8 = (f32[128,128]{1,0:T(8,128)S(1)}, f32[128,128]{1,0:T(8,128)S(1)}, u32[]{:S(2)}, u32[]{:S(2)}) collective-permute-start(f32[128,128]{1,0:T(8,128)S(1)} %get-tuple-element.68.refs_4_), channel_id=1, source_target_pairs={{0,3},{1,0},{2,1},{3,2},{4,7},{5,4},{6,5},{7,6},{8,11},{9,8},{10,9... | collective-permute-start | bytes 196616 | tf_op jit(solution)/shard_map/ppermute | solution.py:415
  146.0 9.5 %collective-permute-start.15 = (bf16[128,640]{1,0:T(8,128)(2,1)}, bf16[128,640]{1,0:T(8,128)(2,1)S(1)}, u32[]{:S(2)}, u32[]{:S(2)}) collective-permute-start(bf16[128,640]{1,0:T(8,128)(2,1)} %get-tuple-element.73), channel_id=1, source_target_pairs={{0,128},{64,192},{128,0},{192,64},{1,129},{65,193},{129,1},{193,65... | collective-permute-start | bytes 491528 | tf_op jit(solution)/shard_map/ppermute | solution.py:409
  155.5 0.0 collective-permute-done.10.refs_3_
  155.5 0.0 collective-permute-done.9.refs_2_
  155.5 0.0 collective-permute-done.8.refs_1_
  155.5 1.8 scan_x.1
  157.2 0.1 collective-permute-start.11
  157.3 4.4 %collective-permute-done.11.refs_1_ = f32[128,128]{1,0:T(8,128)S(1)} collective-permute-done((f32[128,128]{1,0:T(8,128)S(1)}, f32[128,128]{1,0:T(8,128)S(1)}, u32[]{:S(2)}, u32[]{:S(2)}) %collective-permute-start.11) | collective-permute-done | bytes 65568 | tf_op jit(solution)/shard_map/ppermute | solution.py:461
  161.7 1.6 scan_z.1
  163.3 0.1 collective-permute-start.14
  163.4 4.0 %collective-permute-start.13 = (f32[128,128]{1,0:T(8,128)S(1)}, f32[128,128]{1,0:T(8,128)S(1)}, u32[]{:S(2)}, u32[]{:S(2)}) collective-permute-start(f32[128,128]{1,0:T(8,128)S(1)} %get-tuple-element.72), channel_id=1, source_target_pairs={{0,16},{8,24},{16,0},{24,8},{1,17},{9,25},{17,1},{25,9},{2,18},{10... | collective-permute-start | bytes 196616 | tf_op jit(solution)/shard_map/ppermute | solution.py:415
  167.4 0.0 collective-permute-start.12
  167.4 0.0 collective-permute-done.15.refs_2_
  167.4 1.5 collective-permute-done.14.refs_3_
  168.9 1.4 collective-permute-done.13.refs_2_
  170.3 1.3 collective-permute-done.12.refs_1_
  171.6 4.0 %retention_grads.1 = (f32[128,128]{1,0:T(8,128)}, f32[144,256]{1,0:T(8,128)S(1)}) custom-call(s32[3]{0:T(128)S(1)} %pad_add_fusion.refs_0_.ids, f32[128,128]{1,0:T(8,128)S(1)} %collective-permute-done.12.refs_1_, f32[128,128]{1,0:T(8,128)S(1)} %collective-permute-done.13.refs_2_, f32[128,128]{1,0:T(8,128)S(1)} %collective-permute-done.14.refs_3_, ...), custom_call_target="tpu_custom_call" | custom-call | tf_op jit(solution)/shard_map/retention_grads/pallas_call | solution.py:51
  175.6 0.1 collective-permute-start.16
  175.7 1.4 collective-permute-done.16.refs_1_
  177.1 1.0 message.1.refs_4_
  178.1 0.1 collective-permute-start.19
  178.2 3.7 %collective-permute-start.18 = (bf16[144,256]{1,0:T(8,128)(2,1)S(1)}, bf16[144,256]{1,0:T(8,128)(2,1)S(1)}, u32[]{:S(2)}, u32[]{:S(2)}) collective-permute-start(bf16[144,256]{1,0:T(8,128)(2,1)S(1)} %message.1.refs_4_), channel_id=1, source_target_pairs={{0,128},{64,192},{128,0},{192,64},{1,129},{65,193},{129,1},{193,65... | collective-permute-start | bytes 221192 | tf_op jit(solution)/shard_map/ppermute | solution.py:409
  181.8 2.8 %collective-permute-start.17 = (bf16[144,256]{1,0:T(8,128)(2,1)S(1)}, bf16[144,256]{1,0:T(8,128)(2,1)S(1)}, u32[]{:S(2)}, u32[]{:S(2)}) collective-permute-start(bf16[144,256]{1,0:T(8,128)(2,1)S(1)} %message.1.refs_4_), channel_id=1, source_target_pairs={{0,64},{64,128},{128,192},{192,0},{1,65},{65,129},{129,193},{193,1... | collective-permute-start | bytes 221192 | tf_op jit(solution)/shard_map/ppermute | solution.py:409
  184.7 0.0 copy-done.1
  184.7 3.0 %query_rows.1 = bf16[128,2560]{1,0:T(8,128)(2,1)} custom-call(s32[3]{0:T(128)S(1)} %pad_add_fusion.refs_0_.ids, bf16[128,640]{1,0:T(8,128)(2,1)S(1)} %collective-permute-done.6.refs_1_, bf16[128,640]{1,0:T(8,128)(2,1)S(1)} %collective-permute-done.15.refs_2_, bf16[128,640]{1,0:T(8,128)(2,1)S(1)} %copy-done.1, bf16[128,640]{1,0:T(8,128)(2,1)} %get-tuple-element.76.refs_4_), custom_call_target="tpu_custom_call" | custom-call | tf_op jit(solution)/shard_map/query_rows/pallas_call | solution.py:51
  187.7 0.0 collective-permute-done.19.refs_3_
  187.7 0.0 collective-permute-done.18.refs_2_
  187.7 3.5 %collective-permute-done.17.refs_1_ = bf16[144,256]{1,0:T(8,128)(2,1)S(1)} collective-permute-done((bf16[144,256]{1,0:T(8,128)(2,1)S(1)}, bf16[144,256]{1,0:T(8,128)(2,1)S(1)}, u32[]{:S(2)}, u32[]{:S(2)}) %collective-permute-start.17) | collective-permute-done | bytes 73760 | tf_op jit(solution)/shard_map/ppermute | solution.py:409
  191.2 1.8 finish.1
Async XLA Ops:
  3.6 6.9 %collective-permute-start = (bf16[272,128]{1,0:T(8,128)(2,1)S(1)}, bf16[272,128]{1,0:T(8,128)(2,1)S(1)}, u32[]{:S(2)}, u32[]{:S(2)}) collective-permute-start(bf16[272,128]{1,0:T(8,128)(2,1)S(1)} %get-tuple-element.46.refs_2_), channel_id=1, source_target_pairs={{0,4},{4,0},{1,5},{5,1},{2,6},{6,2},{3,7},{7,3},{8,12},{12,8},{9,1... | collective-permute-start | bytes 208904 | tf_op jit(solution)/shard_map/ppermute | solution.py:437
  13.0 48.5 %all-to-all-start = ((bf16[16,2,272,128]{3,2,1,0:T(8,128)(2,1)}), bf16[16,2,272,128]{3,2,1,0:T(8,128)(2,1)S(1)}, u32[]{:S(2)}, u32[]{:S(2)}) async-start(bf16[16,2,272,128]{3,2,1,0:T(8,128)(2,1)} %copies.1), calls=%async_computation | async-start | bytes 4456448 | tf_op jit(solution)/shard_map/all_to_all | solution.py:441
  20.5 41.1 %collective-permute-start.1 = (bf16[144,1280]{1,0:T(8,128)(2,1)}, bf16[144,1280]{1,0:T(8,128)(2,1)S(1)}, u32[]{:S(2)}, u32[]{:S(2)}) collective-permute-start(bf16[144,1280]{1,0:T(8,128)(2,1)} %get-tuple-element.52), channel_id=1, source_target_pairs={{0,88},{8,80},{16,72},{24,64},{64,152},{72,144},{80,136},{88,128},... | collective-permute-start | bytes 1105928 | tf_op jit(solution)/shard_map/ppermute | solution.py:411
  25.9 45.6 %collective-permute-start.2 = (bf16[144,1280]{1,0:T(8,128)(2,1)}, bf16[144,1280]{1,0:T(8,128)(2,1)S(1)}, u32[]{:S(2)}, u32[]{:S(2)}) collective-permute-start(bf16[144,1280]{1,0:T(8,128)(2,1)} %get-tuple-element.53), channel_id=1, source_target_pairs={{0,216},{8,208},{16,200},{24,192},{64,24},{72,16},{80,8},{88,0},{1... | collective-permute-start | bytes 1105928 | tf_op jit(solution)/shard_map/ppermute | solution.py:411
  28.1 43.4 %collective-permute-start.3 = (bf16[144,1280]{1,0:T(8,128)(2,1)}, bf16[144,1280]{1,0:T(8,128)(2,1)S(1)}, u32[]{:S(2)}, u32[]{:S(2)}) collective-permute-start(bf16[144,1280]{1,0:T(8,128)(2,1)} %get-tuple-element.54), channel_id=1, source_target_pairs={{0,128},{64,192},{128,0},{192,64},{1,129},{65,193},{129,1},{193,65... | collective-permute-start | bytes 1105928 | tf_op jit(solution)/shard_map/ppermute | solution.py:409
  71.5 2.7 %collective-permute-start.4 = (bf16[16,2,128,128]{3,2,1,0:T(8,128)(2,1)S(1)}, bf16[16,2,128,128]{3,2,1,0:T(8,128)(2,1)S(1)}, u32[]{:S(2)}, u32[]{:S(2)}) collective-permute-start(bf16[16,2,128,128]{3,2,1,0:T(8,128)(2,1)S(1)} %slice.4.refs_1_), channel_id=1, source_target_pairs={{0,32},{32,0},{1,33},{33,1},{2,34},{34,2},{3,35},{35,3},{4,36},{36... | collective-permute-start | bytes 3145736 | tf_op jit(solution)/shard_map/ppermute | solution.py:419
  103.1 2.7 %collective-permute-start.5 = (bf16[4096,128]{1,0:T(8,128)(2,1)S(1)}, bf16[4096,128]{1,0:T(8,128)(2,1)S(1)}, u32[]{:S(2)}, u32[]{:S(2)}) collective-permute-start(bf16[4096,128]{1,0:T(8,128)(2,1)S(1)} %get-tuple-element.61), channel_id=1, source_target_pairs={{0,32},{32,0},{1,33},{33,1},{2,34},{34,2},{3,35},{35,3},{4,36},{36... | collective-permute-start | bytes 3145736 | tf_op jit(solution)/shard_map/ppermute | solution.py:419
  107.0 31.9 %all-to-all-start.1 = ((bf16[32,128,128]{2,1,0:T(8,128)(2,1)}), bf16[32,128,128]{2,1,0:T(8,128)(2,1)S(1)}, u32[]{:S(2)}, u32[]{:S(2)}) async-start(bf16[32,128,128]{2,1,0:T(8,128)(2,1)} %bitcast.10), calls=%async_computation.1 | async-start | bytes 2097152 | tf_op jit(solution)/shard_map/all_to_all | solution.py:423
  112.3 14.8 %collective-permute-start.6 = (bf16[128,640]{1,0:T(8,128)(2,1)}, bf16[128,640]{1,0:T(8,128)(2,1)S(1)}, u32[]{:S(2)}, u32[]{:S(2)}) collective-permute-start(bf16[128,640]{1,0:T(8,128)(2,1)} %get-tuple-element.62), channel_id=1, source_target_pairs={{0,216},{8,208},{16,200},{24,192},{64,24},{72,16},{80,8},{88,0},{1... | collective-permute-start | bytes 491528 | tf_op jit(solution)/shard_map/ppermute | solution.py:411
  118.9 19.3 %collective-permute-start.7 = (bf16[128,640]{1,0:T(8,128)(2,1)}, bf16[128,640]{1,0:T(8,128)(2,1)S(1)}, u32[]{:S(2)}, u32[]{:S(2)}) collective-permute-start(bf16[128,640]{1,0:T(8,128)(2,1)} %get-tuple-element.63), channel_id=1, source_target_pairs={{0,88},{8,80},{16,72},{24,64},{64,152},{72,144},{80,136},{88,128},... | collective-permute-start | bytes 491528 | tf_op jit(solution)/shard_map/ppermute | solution.py:411
  138.2 0.7 copy-start
  138.9 45.8 %copy-start.1 = (bf16[128,640]{1,0:T(8,128)(2,1)S(1)}, bf16[128,640]{1,0:T(8,128)(2,1)}, u32[]{:S(2)}) copy-start(bf16[128,640]{1,0:T(8,128)(2,1)} %copy-done) | copy-start | bytes 491524
  141.8 13.7 %collective-permute-start.10 = (f32[128,128]{1,0:T(8,128)S(1)}, f32[128,128]{1,0:T(8,128)S(1)}, u32[]{:S(2)}, u32[]{:S(2)}) collective-permute-start(f32[128,128]{1,0:T(8,128)S(1)} %get-tuple-element.68.refs_4_), channel_id=1, source_target_pairs={{0,1},{1,2},{2,3},{3,0},{4,5},{5,6},{6,7},{7,4},{8,9},{9,10},{10,1... | collective-permute-start | bytes 196616 | tf_op jit(solution)/shard_map/ppermute | solution.py:415
  142.7 12.7 %collective-permute-start.9 = (f32[128,128]{1,0:T(8,128)S(1)}, f32[128,128]{1,0:T(8,128)S(1)}, u32[]{:S(2)}, u32[]{:S(2)}) collective-permute-start(f32[128,128]{1,0:T(8,128)S(1)} %get-tuple-element.68.refs_4_), channel_id=1, source_target_pairs={{0,2},{1,3},{2,0},{3,1},{4,6},{5,7},{6,4},{7,5},{8,10},{9,11},{10,... | collective-permute-start | bytes 196616 | tf_op jit(solution)/shard_map/ppermute | solution.py:415
  143.9 11.6 %collective-permute-start.8 = (f32[128,128]{1,0:T(8,128)S(1)}, f32[128,128]{1,0:T(8,128)S(1)}, u32[]{:S(2)}, u32[]{:S(2)}) collective-permute-start(f32[128,128]{1,0:T(8,128)S(1)} %get-tuple-element.68.refs_4_), channel_id=1, source_target_pairs={{0,3},{1,0},{2,1},{3,2},{4,7},{5,4},{6,5},{7,6},{8,11},{9,8},{10,9... | collective-permute-start | bytes 196616 | tf_op jit(solution)/shard_map/ppermute | solution.py:415
  146.0 21.4 %collective-permute-start.15 = (bf16[128,640]{1,0:T(8,128)(2,1)}, bf16[128,640]{1,0:T(8,128)(2,1)S(1)}, u32[]{:S(2)}, u32[]{:S(2)}) collective-permute-start(bf16[128,640]{1,0:T(8,128)(2,1)} %get-tuple-element.73), channel_id=1, source_target_pairs={{0,128},{64,192},{128,0},{192,64},{1,129},{65,193},{129,1},{193,65... | collective-permute-start | bytes 491528 | tf_op jit(solution)/shard_map/ppermute | solution.py:409
  157.2 4.5 %collective-permute-start.11 = (f32[128,128]{1,0:T(8,128)S(1)}, f32[128,128]{1,0:T(8,128)S(1)}, u32[]{:S(2)}, u32[]{:S(2)}) collective-permute-start(f32[128,128]{1,0:T(8,128)S(1)} %get-tuple-element.70.refs_2_), channel_id=1, source_target_pairs={{0,4},{4,0},{1,5},{5,1},{2,6},{6,2},{3,7},{7,3},{8,12},{12,8},{9,1... | collective-permute-start | bytes 196616 | tf_op jit(solution)/shard_map/ppermute | solution.py:461
  163.3 5.6 %collective-permute-start.14 = (f32[128,128]{1,0:T(8,128)S(1)}, f32[128,128]{1,0:T(8,128)S(1)}, u32[]{:S(2)}, u32[]{:S(2)}) collective-permute-start(f32[128,128]{1,0:T(8,128)S(1)} %get-tuple-element.72), channel_id=1, source_target_pairs={{0,8},{8,16},{16,24},{24,0},{1,9},{9,17},{17,25},{25,1},{2,10},{10... | collective-permute-start | bytes 196616 | tf_op jit(solution)/shard_map/ppermute | solution.py:415
  163.4 6.9 %collective-permute-start.13 = (f32[128,128]{1,0:T(8,128)S(1)}, f32[128,128]{1,0:T(8,128)S(1)}, u32[]{:S(2)}, u32[]{:S(2)}) collective-permute-start(f32[128,128]{1,0:T(8,128)S(1)} %get-tuple-element.72), channel_id=1, source_target_pairs={{0,16},{8,24},{16,0},{24,8},{1,17},{9,25},{17,1},{25,9},{2,18},{10... | collective-permute-start | bytes 196616 | tf_op jit(solution)/shard_map/ppermute | solution.py:415
  167.4 4.3 %collective-permute-start.12 = (f32[128,128]{1,0:T(8,128)S(1)}, f32[128,128]{1,0:T(8,128)S(1)}, u32[]{:S(2)}, u32[]{:S(2)}) collective-permute-start(f32[128,128]{1,0:T(8,128)S(1)} %get-tuple-element.72), channel_id=1, source_target_pairs={{0,24},{8,0},{16,8},{24,16},{1,25},{9,1},{17,9},{25,17},{2,26},{10... | collective-permute-start | bytes 196616 | tf_op jit(solution)/shard_map/ppermute | solution.py:415
  175.6 1.5 collective-permute-start.16
  178.1 9.6 %collective-permute-start.19 = (bf16[144,256]{1,0:T(8,128)(2,1)S(1)}, bf16[144,256]{1,0:T(8,128)(2,1)S(1)}, u32[]{:S(2)}, u32[]{:S(2)}) collective-permute-start(bf16[144,256]{1,0:T(8,128)(2,1)S(1)} %message.1.refs_4_), channel_id=1, source_target_pairs={{0,192},{64,0},{128,64},{192,128},{1,193},{65,1},{129,65},{193,129... | collective-permute-start | bytes 221192 | tf_op jit(solution)/shard_map/ppermute | solution.py:409
  178.2 9.6 %collective-permute-start.18 = (bf16[144,256]{1,0:T(8,128)(2,1)S(1)}, bf16[144,256]{1,0:T(8,128)(2,1)S(1)}, u32[]{:S(2)}, u32[]{:S(2)}) collective-permute-start(bf16[144,256]{1,0:T(8,128)(2,1)S(1)} %message.1.refs_4_), channel_id=1, source_target_pairs={{0,128},{64,192},{128,0},{192,64},{1,129},{65,193},{129,1},{193,65... | collective-permute-start | bytes 221192 | tf_op jit(solution)/shard_map/ppermute | solution.py:409
  181.8 9.4 %collective-permute-start.17 = (bf16[144,256]{1,0:T(8,128)(2,1)S(1)}, bf16[144,256]{1,0:T(8,128)(2,1)S(1)}, u32[]{:S(2)}, u32[]{:S(2)}) collective-permute-start(bf16[144,256]{1,0:T(8,128)(2,1)S(1)} %message.1.refs_4_), channel_id=1, source_target_pairs={{0,64},{64,128},{128,192},{192,0},{1,65},{65,129},{129,193},{193,1... | collective-permute-start | bytes 221192 | tf_op jit(solution)/shard_map/ppermute | solution.py:409

commit v3 on v2

--- a/solution.py
+++ b/solution.py
@@ -140,27 +140,26 @@
     )(ids, *map(in_hbm, args))
 
 
-def copies_kernel(ids, theirs_ref, mine_ref, out_ref):
-    for i in range(out_ref.shape[0]):
-        out_ref[i, 0] = mine_ref[...]
-        out_ref[i, 1] = theirs_ref[...]
+def copies_kernel(ids, r1, r2, r3, pair_ref, out_ref):
+    for x in range(4):
+        for k, ref in enumerate((pair_ref, r1, r2, r3)):
+            out_ref[x, k] = ref[...]
 
 
 def place_of(ids, b):
-    low = lax.rem(lax.div(b, 4), 2)
-    return lax.div(b, 8) * 4 + lax.rem(b, 4), lax.rem(low + lax.div(ids[1], 4), 2)
+    far = lax.rem(lax.div(b, 8) - lax.div(ids[1], 8) + 4, 4)
+    return lax.rem(b, 4), far, lax.rem(lax.div(b, 4) + lax.div(ids[1], 4), 2)
 
 
 def attn_kernel(count, B, T, *refs):
     ids, own, other = refs[:3]
-    packs, dqs = refs[3 : 3 + count], refs[3 + count : 3 + 2 * count]
-    keep, send, ks, vs, kt, qs, dos, delta, p_s, dq_s, dk, dv = refs[3 + 2 * count :]
+    packs, dqs = refs[3 : 3 + count], refs[4 + count : 4 + 2 * count]
+    keep, send, ks, vs, kt, qs, dos, delta, p_s, dq_s, dk, dv = refs[4 + 2 * count :]
     c, core = ids[1], ids[2]
 
     def fill(out, ref):
         def one(b, _):
-            i, p = place_of(ids, b)
-            out[pl.ds(pl.multiple_of(b * TOK, TOK), TOK), :] = ref[i, p]
+            out[pl.ds(pl.multiple_of(b * TOK, TOK), TOK), :] = ref[place_of(ids, b)]
             return 0
 
         lax.fori_loop(0, BLOCKS, one, 0)
@@ -254,12 +253,12 @@
         send[...] = dk[...].astype(bf16)
 
 
-def attention(ids, own, other, packs, B=1024, T=WIDE):
+def attention(ids, own, other, packs, token, B=1024, T=WIDE):
     count, length, rows = len(packs), BLOCKS * TOK, len(packs) * WIDE
     got = call(
         functools.partial(attn_kernel, count, B, T),
         [((TOK, WIDE), bf16)] * count + [((length, HD), f32), ((length, HD), bf16)],
-        [ids, own, other, *packs],
+        [ids, own, other, *packs, token],
         "attention",
         1 + count,
         [
@@ -284,12 +283,12 @@
 
 def retain_kernel(ids, all_ref, tables, v_ref, out_ref, totals_ref):
     def step(b, state):
-        i, p = place_of(ids, b)
-        return jnp.exp(totals_ref[pl.ds(b, 1), :]) * state + all_ref[i, p, TOK : TOK + HD, :].astype(f32)
+        added = all_ref[(*place_of(ids, b), slice(TOK, TOK + HD))]
+        return jnp.exp(totals_ref[pl.ds(b, 1), :]) * state + added.astype(f32)
 
     for b in range(BLOCKS):
-        i, p = place_of(ids, jnp.int32(b))
-        totals_ref[b : b + 1, :] = jnp.sum(all_ref[i, p, TOK + HD :, :].astype(f32), axis=0, keepdims=True)
+        parts = all_ref[(*place_of(ids, jnp.int32(b)), slice(TOK + HD, None))]
+        totals_ref[b : b + 1, :] = jnp.sum(parts.astype(f32), axis=0, keepdims=True)
     state = lax.fori_loop(0, ids[1], step, jnp.zeros((HD, HD), f32))
     q, cum, inner = tables[0], tables[2], tables[4]
     out_ref[0] = state
@@ -404,6 +403,23 @@
         out[:, pl.ds(start, WIDE)] = ref[...]
 
 
+def arrival(arrays):
+    def kernel(*refs):
+        copy = pltpu.make_async_copy(refs[0].at[0:EXTRA, 0:HD], refs[-2], refs[-1])
+        copy.start()
+        copy.wait()
+
+    return pl.pallas_call(
+        kernel,
+        out_shape=jax.ShapeDtypeStruct((EXTRA, HD), bf16),
+        in_specs=[ANY] * len(arrays),
+        out_specs=VMEM,
+        scratch_shapes=[pltpu.SemaphoreType.DMA],
+        cost_estimate=pl.CostEstimate(flops=5 * 10**10, bytes_accessed=0, transcendentals=0),
+        name="arrival",
+    )(*arrays)
+
+
 def shift(x, k, turn=False):
     if not turn:
         return lax.ppermute(x, "zhi", [(i, (i + k) % 4) for i in range(4)])
@@ -436,13 +452,16 @@
     packs = pack_rows(ids, queries[0], grad_out[0], attn_out[0])
     theirs = lax.ppermute(mine, "zlo", [(0, 1), (1, 0)])
     theirs, packs = lax.optimization_barrier((theirs, packs))
+    pair = jnp.stack([mine, theirs])
+    near = [from_next(pair, "y", k) for k in (1, 2, 3)]
+    near, packs = lax.optimization_barrier((near, packs))
     from1, from3, from2 = shift(packs[1], 1, True), shift(packs[3], 3, True), shift(packs[2], 2)
-    (copies,) = call(copies_kernel, [((16, 2, *mine.shape), bf16)], [ids, theirs, mine], "copies", 2)
-    blocks = lax.all_to_all(copies, ("y", "x"), 0, 0)
-    own = blocks[:, :, 0:TOK]
-    own, from1, from3, from2 = lax.optimization_barrier((own, from1, from3, from2))
+    (copies,) = call(copies_kernel, [((4, 4, *pair.shape), bf16)], [ids, *near, pair], "copies", 4)
+    blocks = lax.all_to_all(copies, "x", 0, 0)
+    own = blocks[:, :, :, 0:TOK]
+    own, token = lax.optimization_barrier((own, arrival([from1, from3, from2])))
     other = swap(own)
-    (dq1, dq3, dq2, dq0), (keep, send) = attention(ids, own, other, [from1, from3, from2, packs[0]])
+    (dq1, dq3, dq2, dq0), (keep, send) = attention(ids, own, other, [from1, from3, from2, packs[0]], token)
     back1, back3, back2 = shift(dq1, 3, True), shift(dq3, 1, True), shift(dq2, 2)
 
     square = ((TOK, HD), f32)
@@ -451,7 +470,7 @@
     )
     part = (keep + swap(send).astype(f32)).astype(bf16)
     parts = spread(part.reshape(BLOCKS, TOK, HD))
-    parts, back1, back3 = lax.optimization_barrier((parts, back1, back3))
+    parts, back2 = lax.optimization_barrier((parts, back2))
     grad, carry = call(
         norm_kernel, [square] * 2, [ids, parts, states, tables], "norm_backward", 1, free=(1,)
     )
@@ -461,7 +480,7 @@
     theirs = lax.ppermute(group, "zlo", [(0, 1), (1, 0)])
     both, leaving = call(scan_z_kernel, [square] * 2, [ids, theirs, group, leaving, totals], "scan_z", 3, free=(0, 1))
     far = [from_next(both, "y", k) for k in (1, 2, 3)]
-    *far, back2 = lax.optimization_barrier((*far, back2))
+    *far, back1, back3 = lax.optimization_barrier((*far, back1, back3))
     d_value, half = call(
         grads_kernel,
         [square, ((TOK + EXTRA, 2 * HD), f32)],

time: 197 us -> 184 us (0.934); the launches traced: 193 us -> 183 us
  waiting for transfers between devices: 70.4 us -> 59.1 us
  Pallas kernels: 58.1 us -> 60.5 us
    all_to_all x1, waiting for transfers between devices: 28.5 us -> 2.45 us  [on_device(): blocks = lax.all_to_all(copies, 'x', 0, 0)]
    ppermute x5, waiting for transfers between devices: 3.49 us -> 22.1 us  [shift(): return lax.ppermute(x, 'zhi', [(i, (i + k) % 4) for i in range(4)])]
    ppermute x4, waiting for transfers between devices: 23.3 us -> 16.1 us  [shift(): return lax.ppermute(x, ('zhi', 'y'), pairs)]
    ppermute x6 -> x9, starting transfers between devices: 8.24 us -> 14.7 us  [from_next(): return lax.ppermute(x, axis, [(i, (i - k) % 4) for i in range(4)])]
    ppermute x5, starting transfers between devices: 21 us -> 15.3 us  [shift(): return lax.ppermute(x, 'zhi', [(i, (i + k) % 4) for i in range(4)])]
    ppermute x6 -> x9, waiting for transfers between devices: 4.27 us -> 8.72 us  [from_next(): return lax.ppermute(x, axis, [(i, (i - k) % 4) for i in range(4)])]
    all_to_all x1, starting transfers between devices: 7.49 us -> 4.83 us  [on_device(): blocks = lax.all_to_all(copies, 'x', 0, 0)]
    ppermute x4, starting transfers between devices: 17.2 us -> 14.8 us  [shift(): return lax.ppermute(x, ('zhi', 'y'), pairs)]
  transfers between devices with their start and end apart: 22 -> 25, of which waited for: 12 -> 16; matrix products, arithmetic and copies ran while one was open for 0% -> 0% of each run, Pallas kernels for 7% -> 10%
where the time goes in v3:
time: 184 us; the launch traced here: 183 us
  Pallas kernels  60.5 us (33%)
  starting transfers between devices  60.3 us (33%)
  waiting for transfers between devices  59.1 us (32%)
    pallas_call x11, Pallas kernels, call(): pl.pallas_call(functools.partial(loaded, kernel, len(inputs), len(outs)),...  54.3 us
    ppermute x5, waiting for transfers between devices, shift(): return lax.ppermute(x, 'zhi', [(i, (i + k) % 4) for i in range(4)])  22.1 us
    ppermute x4, waiting for transfers between devices, shift(): return lax.ppermute(x, ('zhi', 'y'), pairs)  16.1 us
    ppermute x5, starting transfers between devices, shift(): return lax.ppermute(x, 'zhi', [(i, (i + k) % 4) for i in range(4)])  15.3 us
    ppermute x4, starting transfers between devices, shift(): return lax.ppermute(x, ('zhi', 'y'), pairs)  14.8 us
    ppermute x9, starting transfers between devices, from_next(): return lax.ppermute(x, axis, [(i, (i - k) % 4) for i in range(4)])  14.7 us
    ppermute x9, waiting for transfers between devices, from_next(): return lax.ppermute(x, axis, [(i, (i - k) % 4) for i in range(4)])  8.72 us
    all_to_all x1, starting transfers between devices, spread(): return lax.all_to_all(x, CTX, 0, 0)  6.93 us
  transfers between devices with their start and end apart: 25, of which 16 were waited for; matrix products, arithmetic and copies ran while one was open for 0% of the time, Pallas kernels for 10%

profile of v3, /device:TPU:2, one launch (start us, length us, event | category | flops | bytes accessed | tf_op | source)
XLA Modules:
  0.0 183.0 jit_solution(5082933496877383664)
XLA Ops:
  0.6 0.1 pad_add_fusion.refs_0_.ids
  0.7 2.9 %retention_local.1 = (bf16[272,128]{1,0:T(8,128)(2,1)S(1)}, f32[6,128,128]{2,1,0:T(8,128)}) custom-call(s32[3]{0:T(128)S(1)} %pad_add_fusion.refs_0_.ids, bf16[128,128]{1,0:T(8,128)(2,1)} %refs_1_.1, bf16[128,512]{1,0:T(8,128)(2,1)} %refs_2_.1, bf16[128,512]{1,0:T(8,128)(2,1)} %refs_3_.2, bf16[128,128]{1,0:T(8,128)(2,1)} %refs_9_.1, f32[4,128]{1,0:T(4,128)} %bitcast.19), custom_call_target="tpu_custom_call" | custom-call | tf_op jit(solution)/shard_map/retention_local/pallas_call | solution.py:51
  3.6 2.0 %collective-permute-start = (bf16[272,128]{1,0:T(8,128)(2,1)S(1)}, bf16[272,128]{1,0:T(8,128)(2,1)S(1)}, u32[]{:S(2)}, u32[]{:S(2)}) collective-permute-start(bf16[272,128]{1,0:T(8,128)(2,1)S(1)} %get-tuple-element.51), channel_id=1, source_target_pairs={{0,4},{4,0},{1,5},{5,1},{2,6},{6,2},{3,7},{7,3},{8,12},{12,8},{9,1... | collective-permute-start | bytes 208904 | tf_op jit(solution)/shard_map/ppermute | solution.py:453
  5.7 4.9 %pack_rows.1 = (bf16[144,1280]{1,0:T(8,128)(2,1)}, bf16[144,1280]{1,0:T(8,128)(2,1)}, bf16[144,1280]{1,0:T(8,128)(2,1)}, bf16[144,1280]{1,0:T(8,128)(2,1)}) custom-call(s32[3]{0:T(128)S(1)} %pad_add_fusion.refs_0_.ids, bf16[128,2560]{1,0:T(8,128)(2,1)} %bitcast.14, bf16[128,2560]{1,0:T(8,128)(2,1)} %bitcast.15, bf16[128,2560]{1,0:T(8,128)(2,1)} %bitcast.16), custom_call_target="tpu_custom_call" | custom-call | tf_op jit(solution)/shard_map/pack_rows/pallas_call | solution.py:129
  10.6 0.0 collective-permute-done
  10.6 1.7 collective-permute-start.3
  12.2 2.9 %collective-permute-start.2 = (bf16[2,272,128]{2,1,0:T(8,128)(2,1)S(1)}, bf16[2,272,128]{2,1,0:T(8,128)(2,1)S(1)}, u32[]{:S(2)}, u32[]{:S(2)}) collective-permute-start(bf16[2,272,128]{2,1,0:T(8,128)(2,1)S(1)} %pad_maximum_fusion.refs_4_), channel_id=1, source_target_pairs={{0,16},{8,24},{16,0},{24,8},{1,17},{9,25},{17,1},{25,9},{2,18},{10... | collective-permute-start | bytes 417800 | tf_op jit(solution)/shard_map/ppermute | solution.py:431
  15.1 1.3 collective-permute-start.1
  16.5 0.9 collective-permute-done.3.refs_3_
  17.4 3.9 %collective-permute-done.2.refs_2_ = bf16[2,272,128]{2,1,0:T(8,128)(2,1)S(1)} collective-permute-done((bf16[2,272,128]{2,1,0:T(8,128)(2,1)S(1)}, bf16[2,272,128]{2,1,0:T(8,128)(2,1)S(1)}, u32[]{:S(2)}, u32[]{:S(2)}) %collective-permute-start.2) | collective-permute-done | bytes 139296 | tf_op jit(solution)/shard_map/ppermute | solution.py:431
  21.2 0.0 collective-permute-done.1.refs_1_
  21.2 4.9 %collective-permute-start.4 = (bf16[144,1280]{1,0:T(8,128)(2,1)}, bf16[144,1280]{1,0:T(8,128)(2,1)S(1)}, u32[]{:S(2)}, u32[]{:S(2)}) collective-permute-start(bf16[144,1280]{1,0:T(8,128)(2,1)} %get-tuple-element.64), channel_id=1, source_target_pairs={{0,88},{8,80},{16,72},{24,64},{64,152},{72,144},{80,136},{88,128},... | collective-permute-start | bytes 1105928 | tf_op jit(solution)/shard_map/ppermute | solution.py:427
  26.1 2.1 %collective-permute-start.5 = (bf16[144,1280]{1,0:T(8,128)(2,1)}, bf16[144,1280]{1,0:T(8,128)(2,1)S(1)}, u32[]{:S(2)}, u32[]{:S(2)}) collective-permute-start(bf16[144,1280]{1,0:T(8,128)(2,1)} %get-tuple-element.65), channel_id=1, source_target_pairs={{0,216},{8,208},{16,200},{24,192},{64,24},{72,16},{80,8},{88,0},{1... | collective-permute-start | bytes 1105928 | tf_op jit(solution)/shard_map/ppermute | solution.py:427
  28.3 5.5 %collective-permute-start.6 = (bf16[144,1280]{1,0:T(8,128)(2,1)}, bf16[144,1280]{1,0:T(8,128)(2,1)S(1)}, u32[]{:S(2)}, u32[]{:S(2)}) collective-permute-start(bf16[144,1280]{1,0:T(8,128)(2,1)} %get-tuple-element.66), channel_id=1, source_target_pairs={{0,128},{64,192},{128,0},{192,64},{1,129},{65,193},{129,1},{193,65... | collective-permute-start | bytes 1105928 | tf_op jit(solution)/shard_map/ppermute | solution.py:425
  33.8 2.8 %copies.1 = bf16[4,4,2,272,128]{4,3,2,1,0:T(8,128)(2,1)} custom-call(s32[3]{0:T(128)S(1)} %pad_add_fusion.refs_0_.ids, bf16[2,272,128]{2,1,0:T(8,128)(2,1)S(1)} %collective-permute-done.1.refs_1_, bf16[2,272,128]{2,1,0:T(8,128)(2,1)S(1)} %collective-permute-done.2.refs_2_, bf16[2,272,128]{2,1,0:T(8,128)(2,1)S(1)} %collective-permute-done.3.refs_3_, ...), custom_call_target="tpu_custom_call" | custom-call | tf_op jit(solution)/shard_map/copies/pallas_call | solution.py:51
  36.6 4.8 %all-to-all-start = ((bf16[4,4,2,272,128]{4,3,2,1,0:T(8,128)(2,1)}), bf16[4,4,2,272,128]{4,3,2,1,0:T(8,128)(2,1)S(1)}, u32[]{:S(2)}, u32[]{:S(2)}) async-start(bf16[4,4,2,272,128]{4,3,2,1,0:T(8,128)(2,1)} %copies.1), calls=%async_computation | async-start | bytes 4456448 | tf_op jit(solution)/shard_map/all_to_all | solution.py:460
  41.4 2.5 %collective-permute-done.4.refs_0_.refs_3_ = bf16[144,1280]{1,0:T(8,128)(2,1)S(1)} collective-permute-done((bf16[144,1280]{1,0:T(8,128)(2,1)}, bf16[144,1280]{1,0:T(8,128)(2,1)S(1)}, u32[]{:S(2)}, u32[]{:S(2)}) %collective-permute-start.4) | collective-permute-done | bytes 368672 | tf_op jit(solution)/shard_map/ppermute | solution.py:427
  43.9 13.6 %collective-permute-done.5.refs_1_.refs_4_ = bf16[144,1280]{1,0:T(8,128)(2,1)S(1)} collective-permute-done((bf16[144,1280]{1,0:T(8,128)(2,1)}, bf16[144,1280]{1,0:T(8,128)(2,1)S(1)}, u32[]{:S(2)}, u32[]{:S(2)}) %collective-permute-start.5) | collective-permute-done | bytes 368672 | tf_op jit(solution)/shard_map/ppermute | solution.py:427
  57.5 3.7 %collective-permute-done.6.refs_2_.refs_5_ = bf16[144,1280]{1,0:T(8,128)(2,1)S(1)} collective-permute-done((bf16[144,1280]{1,0:T(8,128)(2,1)}, bf16[144,1280]{1,0:T(8,128)(2,1)S(1)}, u32[]{:S(2)}, u32[]{:S(2)}) %collective-permute-start.6) | collective-permute-done | bytes 368672 | tf_op jit(solution)/shard_map/ppermute | solution.py:425
  61.2 0.7 copy-done.4
  61.9 1.3 arrival.1.refs_7_
  63.2 2.4 %all-to-all-done.refs_1_ = bf16[4,4,2,272,128]{4,3,2,1,0:T(8,128)(2,1)S(1)} async-done(((bf16[4,4,2,272,128]{4,3,2,1,0:T(8,128)(2,1)}), bf16[4,4,2,272,128]{4,3,2,1,0:T(8,128)(2,1)S(1)}, u32[]{:S(2)}, u32[]{:S(2)}) %all-to-all-start) | async-done | bytes 2228256 | tf_op jit(solution)/shard_map/all_to_all | solution.py:460
  65.7 0.1 slice.4.refs_1_
  65.8 0.1 collective-permute-start.7
  65.9 2.6 %collective-permute-done.7.refs_2_ = bf16[4,4,2,128,128]{4,3,2,1,0:T(8,128)(2,1)S(1)} collective-permute-done((bf16[4,4,2,128,128]{4,3,2,1,0:T(8,128)(2,1)S(1)}, bf16[4,4,2,128,128]{4,3,2,1,0:T(8,128)(2,1)S(1)}, u32[]{:S(2)}, u32[]{:S(2)}) %collective-permute-start.7) | collective-permute-done | bytes 1048608 | tf_op jit(solution)/shard_map/ppermute | solution.py:435
  68.5 29.6 %attention.1 = (bf16[128,640]{1,0:T(8,128)(2,1)}, bf16[128,640]{1,0:T(8,128)(2,1)}, bf16[128,640]{1,0:T(8,128)(2,1)}, bf16[128,640]{1,0:T(8,128)(2,1)}, f32[4096...) custom-call(s32[3]{0:T(128)S(1)} %pad_add_fusion.refs_0_.ids, bf16[4,4,2,128,128]{4,3,2,1,0:T(8,128)(2,1)S(1)} %slice.4.refs_1_, ...), custom_call_target="tpu_custom_call" | custom-call | flops 13421772800 | bytes 6291456 | tf_op jit(solution)/shard_map/attention/pallas_call | solution.py:51
  98.2 0.4 collective-permute-start.8
  98.6 2.5 %collective-permute-done.8 = bf16[4096,128]{1,0:T(8,128)(2,1)S(1)} collective-permute-done((bf16[4096,128]{1,0:T(8,128)(2,1)S(1)}, bf16[4096,128]{1,0:T(8,128)(2,1)S(1)}, u32[]{:S(2)}, u32[]{:S(2)}) %collective-permute-start.8) | collective-permute-done | bytes 1048608 | tf_op jit(solution)/shard_map/ppermute | solution.py:435
  101.1 1.2 add_convert_fusion
  102.3 6.9 %all-to-all-start.1 = ((bf16[32,128,128]{2,1,0:T(8,128)(2,1)}), bf16[32,128,128]{2,1,0:T(8,128)(2,1)S(1)}, u32[]{:S(2)}, u32[]{:S(2)}) async-start(bf16[32,128,128]{2,1,0:T(8,128)(2,1)} %bitcast.13), calls=%async_computation.1 | async-start | bytes 2097152 | tf_op jit(solution)/shard_map/all_to_all | solution.py:439
  109.2 2.7 %collective-permute-start.9 = (bf16[128,640]{1,0:T(8,128)(2,1)}, bf16[128,640]{1,0:T(8,128)(2,1)S(1)}, u32[]{:S(2)}, u32[]{:S(2)}) collective-permute-start(bf16[128,640]{1,0:T(8,128)(2,1)} %get-tuple-element.72), channel_id=1, source_target_pairs={{0,128},{64,192},{128,0},{192,64},{1,129},{65,193},{129,1},{193,65... | collective-permute-start | bytes 491528 | tf_op jit(solution)/shard_map/ppermute | solution.py:425
  111.9 2.9 %retention_forward.1 = (f32[3,128,128]{2,1,0:T(8,128)}, f32[32,128]{1,0:T(8,128)}) custom-call(s32[3]{0:T(128)S(1)} %pad_add_fusion.refs_0_.ids, bf16[4,4,2,272,128]{4,3,2,1,0:T(8,128)(2,1)S(1)} %all-to-all-done.refs_1_, f32[6,128,128]{2,1,0:T(8,128)} %get-tuple-element.74.refs_2_.refs_3_.refs_8_, bf16[128,128]{1,0:T(8,128)(2,1)} %refs_9_.1), custom_call_target="tpu_custom_call" | custom-call | tf_op jit(solution)/shard_map/retention_forward/pallas_call | solution.py:51
  114.8 13.4 %collective-permute-done.9.refs_2_ = bf16[128,640]{1,0:T(8,128)(2,1)S(1)} collective-permute-done((bf16[128,640]{1,0:T(8,128)(2,1)}, bf16[128,640]{1,0:T(8,128)(2,1)S(1)}, u32[]{:S(2)}, u32[]{:S(2)}) %collective-permute-start.9) | collective-permute-done | bytes 163872 | tf_op jit(solution)/shard_map/ppermute | solution.py:425
  128.3 0.0 all-to-all-done.1.refs_1_
  128.3 2.9 %norm_backward.1 = (f32[128,128]{1,0:T(8,128)}, f32[128,128]{1,0:T(8,128)S(1)}) custom-call(s32[3]{0:T(128)S(1)} %pad_add_fusion.refs_0_.ids, bf16[32,128,128]{2,1,0:T(8,128)(2,1)S(1)} %all-to-all-done.1.refs_1_, f32[3,128,128]{2,1,0:T(8,128)} %get-tuple-element.75.refs_2_.refs_7_, f32[6,128,128]{2,1,0:T(8,128)} %get-tuple-element.74.refs_2_.refs_3_.refs_8_), custom_call_target="tpu_custom_call" | custom-call | tf_op jit(solution)/shard_map/norm_backward/pallas_call | solution.py:51
  131.1 1.5 collective-permute-start.12
  132.7 2.2 %collective-permute-start.11 = (f32[128,128]{1,0:T(8,128)S(1)}, f32[128,128]{1,0:T(8,128)S(1)}, u32[]{:S(2)}, u32[]{:S(2)}) collective-permute-start(f32[128,128]{1,0:T(8,128)S(1)} %get-tuple-element.76.refs_4_), channel_id=1, source_target_pairs={{0,2},{1,3},{2,0},{3,1},{4,6},{5,7},{6,4},{7,5},{8,10},{9,11},{10,... | collective-permute-start | bytes 196616 | tf_op jit(solution)/shard_map/ppermute | solution.py:431
  134.9 1.0 collective-permute-start.10
  135.9 7.8 %collective-permute-start.17 = (bf16[128,640]{1,0:T(8,128)(2,1)}, bf16[128,640]{1,0:T(8,128)(2,1)S(1)}, u32[]{:S(2)}, u32[]{:S(2)}) collective-permute-start(bf16[128,640]{1,0:T(8,128)(2,1)} %get-tuple-element.81), channel_id=1, source_target_pairs={{0,216},{8,208},{16,200},{24,192},{64,24},{72,16},{80,8},{88,0},{1... | collective-permute-start | bytes 491528 | tf_op jit(solution)/shard_map/ppermute | solution.py:427
  143.7 0.0 collective-permute-start.18
  143.7 0.0 collective-permute-done.12.refs_3_
  143.7 0.0 collective-permute-done.11.refs_2_
  143.7 0.0 collective-permute-done.10.refs_1_
  143.7 1.8 scan_x.1
  145.5 1.2 collective-permute-start.13
  146.7 3.2 %collective-permute-done.13.refs_1_ = f32[128,128]{1,0:T(8,128)S(1)} collective-permute-done((f32[128,128]{1,0:T(8,128)S(1)}, f32[128,128]{1,0:T(8,128)S(1)}, u32[]{:S(2)}, u32[]{:S(2)}) %collective-permute-start.13) | collective-permute-done | bytes 65568 | tf_op jit(solution)/shard_map/ppermute | solution.py:480
  149.9 1.6 scan_z.1
  151.5 0.3 collective-permute-start.16
  151.8 3.4 %collective-permute-start.15 = (f32[128,128]{1,0:T(8,128)S(1)}, f32[128,128]{1,0:T(8,128)S(1)}, u32[]{:S(2)}, u32[]{:S(2)}) collective-permute-start(f32[128,128]{1,0:T(8,128)S(1)} %get-tuple-element.80), channel_id=1, source_target_pairs={{0,16},{8,24},{16,0},{24,8},{1,17},{9,25},{17,1},{25,9},{2,18},{10... | collective-permute-start | bytes 196616 | tf_op jit(solution)/shard_map/ppermute | solution.py:431
  155.2 0.3 collective-permute-start.14
  155.5 1.5 collective-permute-done.16.refs_3_
  157.0 1.1 collective-permute-done.15.refs_2_
  158.1 1.3 collective-permute-done.14.refs_1_
  159.5 4.0 %retention_grads.1 = (f32[128,128]{1,0:T(8,128)}, f32[144,256]{1,0:T(8,128)S(1)}) custom-call(s32[3]{0:T(128)S(1)} %pad_add_fusion.refs_0_.ids, f32[128,128]{1,0:T(8,128)S(1)} %collective-permute-done.14.refs_1_, f32[128,128]{1,0:T(8,128)S(1)} %collective-permute-done.15.refs_2_, f32[128,128]{1,0:T(8,128)S(1)} %collective-permute-done.16.refs_3_, ...), custom_call_target="tpu_custom_call" | custom-call | tf_op jit(solution)/shard_map/retention_grads/pallas_call | solution.py:51
  163.5 0.1 collective-permute-start.19
  163.6 1.4 collective-permute-done.19.refs_1_
  164.9 1.0 message.1.refs_4_
  165.9 4.7 %collective-permute-start.22 = (bf16[144,256]{1,0:T(8,128)(2,1)S(1)}, bf16[144,256]{1,0:T(8,128)(2,1)S(1)}, u32[]{:S(2)}, u32[]{:S(2)}) collective-permute-start(bf16[144,256]{1,0:T(8,128)(2,1)S(1)} %message.1.refs_4_), channel_id=1, source_target_pairs={{0,192},{64,0},{128,64},{192,128},{1,193},{65,1},{129,65},{193,129... | collective-permute-start | bytes 221192 | tf_op jit(solution)/shard_map/ppermute | solution.py:425
  170.5 0.6 collective-permute-start.21
  171.1 1.9 %collective-permute-start.20 = (bf16[144,256]{1,0:T(8,128)(2,1)S(1)}, bf16[144,256]{1,0:T(8,128)(2,1)S(1)}, u32[]{:S(2)}, u32[]{:S(2)}) collective-permute-start(bf16[144,256]{1,0:T(8,128)(2,1)S(1)} %message.1.refs_4_), channel_id=1, source_target_pairs={{0,64},{64,128},{128,192},{192,0},{1,65},{65,129},{129,193},{193,1... | collective-permute-start | bytes 221192 | tf_op jit(solution)/shard_map/ppermute | solution.py:425
  173.0 3.0 %query_rows.1 = bf16[128,2560]{1,0:T(8,128)(2,1)} custom-call(s32[3]{0:T(128)S(1)} %pad_add_fusion.refs_0_.ids, bf16[128,640]{1,0:T(8,128)(2,1)S(1)} %collective-permute-done.17.refs_1_, bf16[128,640]{1,0:T(8,128)(2,1)S(1)} %collective-permute-done.9.refs_2_, bf16[128,640]{1,0:T(8,128)(2,1)S(1)} %collective-permute-done.18.refs_3_, ...), custom_call_target="tpu_custom_call" | custom-call | tf_op jit(solution)/shard_map/query_rows/pallas_call | solution.py:51
  176.0 1.1 collective-permute-done.22.refs_3_
  177.2 3.9 %collective-permute-done.21.refs_2_ = bf16[144,256]{1,0:T(8,128)(2,1)S(1)} collective-permute-done((bf16[144,256]{1,0:T(8,128)(2,1)S(1)}, bf16[144,256]{1,0:T(8,128)(2,1)S(1)}, u32[]{:S(2)}, u32[]{:S(2)}) %collective-permute-start.21) | collective-permute-done | bytes 73760 | tf_op jit(solution)/shard_map/ppermute | solution.py:425
  181.0 1.8 finish.1
  (15 shorter events, 0.0 us)
Async XLA Ops:
  3.6 6.9 %collective-permute-start = (bf16[272,128]{1,0:T(8,128)(2,1)S(1)}, bf16[272,128]{1,0:T(8,128)(2,1)S(1)}, u32[]{:S(2)}, u32[]{:S(2)}) collective-permute-start(bf16[272,128]{1,0:T(8,128)(2,1)S(1)} %get-tuple-element.51), channel_id=1, source_target_pairs={{0,4},{4,0},{1,5},{5,1},{2,6},{6,2},{3,7},{7,3},{8,12},{12,8},{9,1... | collective-permute-start | bytes 208904 | tf_op jit(solution)/shard_map/ppermute | solution.py:453
  10.6 6.8 %collective-permute-start.3 = (bf16[2,272,128]{2,1,0:T(8,128)(2,1)S(1)}, bf16[2,272,128]{2,1,0:T(8,128)(2,1)S(1)}, u32[]{:S(2)}, u32[]{:S(2)}) collective-permute-start(bf16[2,272,128]{2,1,0:T(8,128)(2,1)S(1)} %pad_maximum_fusion.refs_4_), channel_id=1, source_target_pairs={{0,8},{8,16},{16,24},{24,0},{1,9},{9,17},{17,25},{25,1},{2,10},{10... | collective-permute-start | bytes 417800 | tf_op jit(solution)/shard_map/ppermute | solution.py:431
  12.2 9.0 %collective-permute-start.2 = (bf16[2,272,128]{2,1,0:T(8,128)(2,1)S(1)}, bf16[2,272,128]{2,1,0:T(8,128)(2,1)S(1)}, u32[]{:S(2)}, u32[]{:S(2)}) collective-permute-start(bf16[2,272,128]{2,1,0:T(8,128)(2,1)S(1)} %pad_maximum_fusion.refs_4_), channel_id=1, source_target_pairs={{0,16},{8,24},{16,0},{24,8},{1,17},{9,25},{17,1},{25,9},{2,18},{10... | collective-permute-start | bytes 417800 | tf_op jit(solution)/shard_map/ppermute | solution.py:431
  15.1 6.1 %collective-permute-start.1 = (bf16[2,272,128]{2,1,0:T(8,128)(2,1)S(1)}, bf16[2,272,128]{2,1,0:T(8,128)(2,1)S(1)}, u32[]{:S(2)}, u32[]{:S(2)}) collective-permute-start(bf16[2,272,128]{2,1,0:T(8,128)(2,1)S(1)} %pad_maximum_fusion.refs_4_), channel_id=1, source_target_pairs={{0,24},{8,0},{16,8},{24,16},{1,25},{9,1},{17,9},{25,17},{2,26},{10... | collective-permute-start | bytes 417800 | tf_op jit(solution)/shard_map/ppermute | solution.py:431
  21.2 22.7 %collective-permute-start.4 = (bf16[144,1280]{1,0:T(8,128)(2,1)}, bf16[144,1280]{1,0:T(8,128)(2,1)S(1)}, u32[]{:S(2)}, u32[]{:S(2)}) collective-permute-start(bf16[144,1280]{1,0:T(8,128)(2,1)} %get-tuple-element.64), channel_id=1, source_target_pairs={{0,88},{8,80},{16,72},{24,64},{64,152},{72,144},{80,136},{88,128},... | collective-permute-start | bytes 1105928 | tf_op jit(solution)/shard_map/ppermute | solution.py:427
  26.1 31.3 %collective-permute-start.5 = (bf16[144,1280]{1,0:T(8,128)(2,1)}, bf16[144,1280]{1,0:T(8,128)(2,1)S(1)}, u32[]{:S(2)}, u32[]{:S(2)}) collective-permute-start(bf16[144,1280]{1,0:T(8,128)(2,1)} %get-tuple-element.65), channel_id=1, source_target_pairs={{0,216},{8,208},{16,200},{24,192},{64,24},{72,16},{80,8},{88,0},{1... | collective-permute-start | bytes 1105928 | tf_op jit(solution)/shard_map/ppermute | solution.py:427
  28.3 32.9 %collective-permute-start.6 = (bf16[144,1280]{1,0:T(8,128)(2,1)}, bf16[144,1280]{1,0:T(8,128)(2,1)S(1)}, u32[]{:S(2)}, u32[]{:S(2)}) collective-permute-start(bf16[144,1280]{1,0:T(8,128)(2,1)} %get-tuple-element.66), channel_id=1, source_target_pairs={{0,128},{64,192},{128,0},{192,64},{1,129},{65,193},{129,1},{193,65... | collective-permute-start | bytes 1105928 | tf_op jit(solution)/shard_map/ppermute | solution.py:425
  36.6 29.1 %all-to-all-start = ((bf16[4,4,2,272,128]{4,3,2,1,0:T(8,128)(2,1)}), bf16[4,4,2,272,128]{4,3,2,1,0:T(8,128)(2,1)S(1)}, u32[]{:S(2)}, u32[]{:S(2)}) async-start(bf16[4,4,2,272,128]{4,3,2,1,0:T(8,128)(2,1)} %copies.1), calls=%async_computation | async-start | bytes 4456448 | tf_op jit(solution)/shard_map/all_to_all | solution.py:460
  43.9 17.3 %copy-start = (bf16[144,1280]{1,0:T(8,128)(2,1)}, bf16[144,1280]{1,0:T(8,128)(2,1)S(1)}, u32[]{:S(2)}) copy-start(bf16[144,1280]{1,0:T(8,128)(2,1)S(1)} %collective-permute-done.4.refs_0_.refs_3_) | copy-start | bytes 1105924
  57.5 3.7 %copy-start.2 = (bf16[144,1280]{1,0:T(8,128)(2,1)}, bf16[144,1280]{1,0:T(8,128)(2,1)S(1)}, u32[]{:S(2)}) copy-start(bf16[144,1280]{1,0:T(8,128)(2,1)S(1)} %collective-permute-done.5.refs_1_.refs_4_) | copy-start | bytes 1105924
  61.2 0.7 copy-start.4
  63.2 5.3 %copy-start.1 = (bf16[144,1280]{1,0:T(8,128)(2,1)S(1)}, bf16[144,1280]{1,0:T(8,128)(2,1)}, u32[]{:S(2)}) copy-start(bf16[144,1280]{1,0:T(8,128)(2,1)} %copy-done) | copy-start | bytes 1105924
  63.2 5.3 %copy-start.3 = (bf16[144,1280]{1,0:T(8,128)(2,1)S(1)}, bf16[144,1280]{1,0:T(8,128)(2,1)}, u32[]{:S(2)}) copy-start(bf16[144,1280]{1,0:T(8,128)(2,1)} %copy-done.2) | copy-start | bytes 1105924
  63.2 5.3 %copy-start.5 = (bf16[144,1280]{1,0:T(8,128)(2,1)S(1)}, bf16[144,1280]{1,0:T(8,128)(2,1)}, u32[]{:S(2)}) copy-start(bf16[144,1280]{1,0:T(8,128)(2,1)} %copy-done.4) | copy-start | bytes 1105924
  65.8 2.7 %collective-permute-start.7 = (bf16[4,4,2,128,128]{4,3,2,1,0:T(8,128)(2,1)S(1)}, bf16[4,4,2,128,128]{4,3,2,1,0:T(8,128)(2,1)S(1)}, u32[]{:S(2)}, u32[]{:S(2)}) collective-permute-start(bf16[4,4,2,128,128]{4,3,2,1,0:T(8,128)(2,1)S(1)} %slice.4.refs_1_), channel_id=1, source_target_pairs={{0,32},{32,0},{1,33},{33,1},{2,34},{34,2},{3,35},{35,3},{4,36},{36... | collective-permute-start | bytes 3145736 | tf_op jit(solution)/shard_map/ppermute | solution.py:435
  98.2 2.9 %collective-permute-start.8 = (bf16[4096,128]{1,0:T(8,128)(2,1)S(1)}, bf16[4096,128]{1,0:T(8,128)(2,1)S(1)}, u32[]{:S(2)}, u32[]{:S(2)}) collective-permute-start(bf16[4096,128]{1,0:T(8,128)(2,1)S(1)} %get-tuple-element.71), channel_id=1, source_target_pairs={{0,32},{32,0},{1,33},{33,1},{2,34},{34,2},{3,35},{35,3},{4,36},{36... | collective-permute-start | bytes 3145736 | tf_op jit(solution)/shard_map/ppermute | solution.py:435
  102.3 26.0 %all-to-all-start.1 = ((bf16[32,128,128]{2,1,0:T(8,128)(2,1)}), bf16[32,128,128]{2,1,0:T(8,128)(2,1)S(1)}, u32[]{:S(2)}, u32[]{:S(2)}) async-start(bf16[32,128,128]{2,1,0:T(8,128)(2,1)} %bitcast.13), calls=%async_computation.1 | async-start | bytes 2097152 | tf_op jit(solution)/shard_map/all_to_all | solution.py:439
  109.2 19.0 %collective-permute-start.9 = (bf16[128,640]{1,0:T(8,128)(2,1)}, bf16[128,640]{1,0:T(8,128)(2,1)S(1)}, u32[]{:S(2)}, u32[]{:S(2)}) collective-permute-start(bf16[128,640]{1,0:T(8,128)(2,1)} %get-tuple-element.72), channel_id=1, source_target_pairs={{0,128},{64,192},{128,0},{192,64},{1,129},{65,193},{129,1},{193,65... | collective-permute-start | bytes 491528 | tf_op jit(solution)/shard_map/ppermute | solution.py:425
  131.1 12.5 %collective-permute-start.12 = (f32[128,128]{1,0:T(8,128)S(1)}, f32[128,128]{1,0:T(8,128)S(1)}, u32[]{:S(2)}, u32[]{:S(2)}) collective-permute-start(f32[128,128]{1,0:T(8,128)S(1)} %get-tuple-element.76.refs_4_), channel_id=1, source_target_pairs={{0,1},{1,2},{2,3},{3,0},{4,5},{5,6},{6,7},{7,4},{8,9},{9,10},{10,1... | collective-permute-start | bytes 196616 | tf_op jit(solution)/shard_map/ppermute | solution.py:431
  132.7 11.0 %collective-permute-start.11 = (f32[128,128]{1,0:T(8,128)S(1)}, f32[128,128]{1,0:T(8,128)S(1)}, u32[]{:S(2)}, u32[]{:S(2)}) collective-permute-start(f32[128,128]{1,0:T(8,128)S(1)} %get-tuple-element.76.refs_4_), channel_id=1, source_target_pairs={{0,2},{1,3},{2,0},{3,1},{4,6},{5,7},{6,4},{7,5},{8,10},{9,11},{10,... | collective-permute-start | bytes 196616 | tf_op jit(solution)/shard_map/ppermute | solution.py:431
  134.9 8.8 %collective-permute-start.10 = (f32[128,128]{1,0:T(8,128)S(1)}, f32[128,128]{1,0:T(8,128)S(1)}, u32[]{:S(2)}, u32[]{:S(2)}) collective-permute-start(f32[128,128]{1,0:T(8,128)S(1)} %get-tuple-element.76.refs_4_), channel_id=1, source_target_pairs={{0,3},{1,0},{2,1},{3,2},{4,7},{5,4},{6,5},{7,6},{8,11},{9,8},{10,9... | collective-permute-start | bytes 196616 | tf_op jit(solution)/shard_map/ppermute | solution.py:431
  135.9 19.6 %collective-permute-start.17 = (bf16[128,640]{1,0:T(8,128)(2,1)}, bf16[128,640]{1,0:T(8,128)(2,1)S(1)}, u32[]{:S(2)}, u32[]{:S(2)}) collective-permute-start(bf16[128,640]{1,0:T(8,128)(2,1)} %get-tuple-element.81), channel_id=1, source_target_pairs={{0,216},{8,208},{16,200},{24,192},{64,24},{72,16},{80,8},{88,0},{1... | collective-permute-start | bytes 491528 | tf_op jit(solution)/shard_map/ppermute | solution.py:427
  143.7 11.8 %collective-permute-start.18 = (bf16[128,640]{1,0:T(8,128)(2,1)}, bf16[128,640]{1,0:T(8,128)(2,1)S(1)}, u32[]{:S(2)}, u32[]{:S(2)}) collective-permute-start(bf16[128,640]{1,0:T(8,128)(2,1)} %get-tuple-element.82), channel_id=1, source_target_pairs={{0,88},{8,80},{16,72},{24,64},{64,152},{72,144},{80,136},{88,128},... | collective-permute-start | bytes 491528 | tf_op jit(solution)/shard_map/ppermute | solution.py:427
  145.5 4.4 %collective-permute-start.13 = (f32[128,128]{1,0:T(8,128)S(1)}, f32[128,128]{1,0:T(8,128)S(1)}, u32[]{:S(2)}, u32[]{:S(2)}) collective-permute-start(f32[128,128]{1,0:T(8,128)S(1)} %get-tuple-element.78.refs_2_), channel_id=1, source_target_pairs={{0,4},{4,0},{1,5},{5,1},{2,6},{6,2},{3,7},{7,3},{8,12},{12,8},{9,1... | collective-permute-start | bytes 196616 | tf_op jit(solution)/shard_map/ppermute | solution.py:480
  151.5 5.6 %collective-permute-start.16 = (f32[128,128]{1,0:T(8,128)S(1)}, f32[128,128]{1,0:T(8,128)S(1)}, u32[]{:S(2)}, u32[]{:S(2)}) collective-permute-start(f32[128,128]{1,0:T(8,128)S(1)} %get-tuple-element.80), channel_id=1, source_target_pairs={{0,8},{8,16},{16,24},{24,0},{1,9},{9,17},{17,25},{25,1},{2,10},{10... | collective-permute-start | bytes 196616 | tf_op jit(solution)/shard_map/ppermute | solution.py:431
  151.8 6.3 %collective-permute-start.15 = (f32[128,128]{1,0:T(8,128)S(1)}, f32[128,128]{1,0:T(8,128)S(1)}, u32[]{:S(2)}, u32[]{:S(2)}) collective-permute-start(f32[128,128]{1,0:T(8,128)S(1)} %get-tuple-element.80), channel_id=1, source_target_pairs={{0,16},{8,24},{16,0},{24,8},{1,17},{9,25},{17,1},{25,9},{2,18},{10... | collective-permute-start | bytes 196616 | tf_op jit(solution)/shard_map/ppermute | solution.py:431
  155.2 4.3 %collective-permute-start.14 = (f32[128,128]{1,0:T(8,128)S(1)}, f32[128,128]{1,0:T(8,128)S(1)}, u32[]{:S(2)}, u32[]{:S(2)}) collective-permute-start(f32[128,128]{1,0:T(8,128)S(1)} %get-tuple-element.80), channel_id=1, source_target_pairs={{0,24},{8,0},{16,8},{24,16},{1,25},{9,1},{17,9},{25,17},{2,26},{10... | collective-permute-start | bytes 196616 | tf_op jit(solution)/shard_map/ppermute | solution.py:431
  163.5 1.5 collective-permute-start.19
  165.9 11.3 %collective-permute-start.22 = (bf16[144,256]{1,0:T(8,128)(2,1)S(1)}, bf16[144,256]{1,0:T(8,128)(2,1)S(1)}, u32[]{:S(2)}, u32[]{:S(2)}) collective-permute-start(bf16[144,256]{1,0:T(8,128)(2,1)S(1)} %message.1.refs_4_), channel_id=1, source_target_pairs={{0,192},{64,0},{128,64},{192,128},{1,193},{65,1},{129,65},{193,129... | collective-permute-start | bytes 221192 | tf_op jit(solution)/shard_map/ppermute | solution.py:425
  170.5 10.5 %collective-permute-start.21 = (bf16[144,256]{1,0:T(8,128)(2,1)S(1)}, bf16[144,256]{1,0:T(8,128)(2,1)S(1)}, u32[]{:S(2)}, u32[]{:S(2)}) collective-permute-start(bf16[144,256]{1,0:T(8,128)(2,1)S(1)} %message.1.refs_4_), channel_id=1, source_target_pairs={{0,128},{64,192},{128,0},{192,64},{1,129},{65,193},{129,1},{193,65... | collective-permute-start | bytes 221192 | tf_op jit(solution)/shard_map/ppermute | solution.py:425
  171.1 9.9 %collective-permute-start.20 = (bf16[144,256]{1,0:T(8,128)(2,1)S(1)}, bf16[144,256]{1,0:T(8,128)(2,1)S(1)}, u32[]{:S(2)}, u32[]{:S(2)}) collective-permute-start(bf16[144,256]{1,0:T(8,128)(2,1)S(1)} %message.1.refs_4_), channel_id=1, source_target_pairs={{0,64},{64,128},{128,192},{192,0},{1,65},{65,129},{129,193},{193,1... | collective-permute-start | bytes 221192 | tf_op jit(solution)/shard_map/ppermute | solution.py:425

commit v4 on v3

--- a/solution.py
+++ b/solution.py
@@ -339,9 +339,17 @@
     out_ref[...] = leaving_ref[...] + jnp.where(first, decay_over(totals, c + 1, start + 4) * theirs, 0.0)
 
 
-def grads_kernel(
-    ids, r1, r2, r3, leaving_ref, totals, grad_ref, states, tables, v_ref, dv_ref, part_ref, held
-):
+def near_kernel(ids, grad_ref, states, tables, v_ref, out_ref):
+    grad, state = grad_ref[...], states[0]
+    q, k, cum, decay, inner = (tables[i] for i in range(5))
+    pair = decay * dot(grad, v_ref[...].astype(f32), 1, 1)
+    out_ref[0] = (jnp.exp(cum) * dot(grad, state, 1, 1) + dot(pair, k, 1, 0)) * SCALE
+    out_ref[1] = dot(pair, q, 0, 0)
+    out_ref[2] = dot(inner, grad, 0, 0)
+    out_ref[3] = jnp.broadcast_to(jnp.sum(grad * states[2], axis=1, keepdims=True), (TOK, HD))
+
+
+def grads_kernel(ids, r1, r2, r3, leaving_ref, near_ref, totals, states, tables, v_ref, dv_ref, part_ref, held):
     c = ids[1]
     y = lax.div(c, 8)
     for k, ref in enumerate((r1, r2, r3)):
@@ -353,21 +361,17 @@
 
     later = lax.fori_loop(0, 3 - y, step, jnp.zeros((HD, HD), f32))
     leaving = leaving_ref[...] + decay_over(totals, c + 1, y * 8 + 8) * later
-    grad, state = grad_ref[...], states[0]
-    q, k, cum, decay, inner = (tables[i] for i in range(5))
-    v = v_ref[...].astype(f32)
+    k, cum = tables[1], tables[2]
     total = cum[TOK - 1 : TOK, :]
     tail = jnp.exp(total - cum)
-    pair = decay * dot(grad, v, 1, 1)
-    dq = jnp.exp(cum) * dot(grad, state, 1, 1) + dot(pair, k, 1, 0)
-    dk = dot(pair, q, 0, 0) + tail * dot(v, leaving, 1, 1)
-    dv_ref[...] = dot(inner, grad, 0, 0) + tail * dot(k, leaving, 1, 0)
+    dk = near_ref[1] + tail * dot(v_ref[...].astype(f32), leaving, 1, 1)
+    dv_ref[...] = near_ref[2] + tail * dot(k, leaving, 1, 0)
     through = jnp.sum(jnp.sum(leaving * states[1], axis=1, keepdims=True), axis=0, keepdims=True)
-    change = jnp.sum(grad * states[2], axis=1, keepdims=True) - jnp.sum(k * dk, axis=1, keepdims=True)
+    change = near_ref[3] - jnp.sum(k * dk, axis=1, keepdims=True)
     t = lax.broadcasted_iota(jnp.int32, (TOK, TOK), 0)
     s = lax.broadcasted_iota(jnp.int32, (TOK, TOK), 1)
-    da = dot(jnp.broadcast_to(change, (TOK, HD)), (s <= t).astype(f32), 0, 0) + through
-    part_ref[0:TOK, 0:HD] = dq * SCALE
+    da = dot(change, (s <= t).astype(f32), 0, 0) + through
+    part_ref[0:TOK, 0:HD] = near_ref[0]
     part_ref[0:TOK, HD : 2 * HD] = dk
     part_ref[TOK : TOK + EXTRA, 0:HD] = da[0:EXTRA]
     part_ref[TOK : TOK + EXTRA, HD : 2 * HD] = jnp.zeros((EXTRA, HD), f32)
@@ -475,6 +479,9 @@
         norm_kernel, [square] * 2, [ids, parts, states, tables], "norm_backward", 1, free=(1,)
     )
     held = pltpu.VMEM((4, HD, HD), f32)
+    (ahead,) = call(
+        near_kernel, [((4, TOK, HD), f32)], [ids, grad, states, tables, ret_value], "grads_near", flops=10**9, nbytes=10**6, free=(0,)
+    )
     near = [from_next(carry, "x", k) for k in (1, 2, 3)]
     group, leaving = call(scan_x_kernel, [square] * 2, [ids, *near, carry, totals], "scan_x", 4, [held], free=(0, 1))
     theirs = lax.ppermute(group, "zlo", [(0, 1), (1, 0)])
@@ -484,9 +491,9 @@
     d_value, half = call(
         grads_kernel,
         [square, ((TOK + EXTRA, 2 * HD), f32)],
-        [ids, *far, leaving, totals, grad, states, tables, ret_value],
+        [ids, *far, leaving, ahead, totals, states, tables, ret_value],
         "retention_grads",
-        4,
+        5,
         [held],
         free=(1,),
     )

time: 184 us -> 183 us (level)
  waiting for transfers between devices: 59.1 us -> 56.7 us
    ppermute x9, waiting for transfers between devices: 8.72 us -> 6.33 us  [from_next(): return lax.ppermute(x, axis, [(i, (i - k) % 4) for i in range(4)])]
    pallas_call x11 -> x12, Pallas kernels: 54.3 us -> 56 us  [call(): pl.pallas_call(functools.partial(loaded, kernel, len(inputs), len(outs)),...]
  transfers between devices with their start and end apart: 25 -> 25, of which waited for: 16 -> 15; matrix products, arithmetic and copies ran while one was open for 0% -> 0% of each run, Pallas kernels for 10% -> 11%
where the time goes in v4:
time: 183 us; the launch traced here: 182 us
  Pallas kernels  62.2 us (34%)
  starting transfers between devices  60.3 us (33%)
  waiting for transfers between devices  56.7 us (31%)
    pallas_call x12, Pallas kernels, call(): pl.pallas_call(functools.partial(loaded, kernel, len(inputs), len(outs)),...  56 us
    ppermute x5, waiting for transfers between devices, shift(): return lax.ppermute(x, 'zhi', [(i, (i + k) % 4) for i in range(4)])  22.1 us
    ppermute x4, waiting for transfers between devices, shift(): return lax.ppermute(x, ('zhi', 'y'), pairs)  16.1 us
    ppermute x5, starting transfers between devices, shift(): return lax.ppermute(x, 'zhi', [(i, (i + k) % 4) for i in range(4)])  15.3 us
    ppermute x4, starting transfers between devices, shift(): return lax.ppermute(x, ('zhi', 'y'), pairs)  14.8 us
    ppermute x9, starting transfers between devices, from_next(): return lax.ppermute(x, axis, [(i, (i - k) % 4) for i in range(4)])  14.7 us
    all_to_all x1, starting transfers between devices, spread(): return lax.all_to_all(x, CTX, 0, 0)  6.93 us
    ppermute x3, waiting for transfers between devices, swap(): return lax.ppermute(x, 'core', [(0, 1), (1, 0)])  6.54 us
  transfers between devices with their start and end apart: 25, of which 15 were waited for; matrix products, arithmetic and copies ran while one was open for 0% of the time, Pallas kernels for 11%

profile of v4, /device:TPU:2, one launch (start us, length us, event | category | flops | bytes accessed | tf_op | source)
XLA Modules:
  0.0 182.4 jit_solution(14994001322473589079)
XLA Ops:
  0.6 0.1 pad_add_fusion.refs_0_.ids
  0.7 2.9 %retention_local.1 = (bf16[272,128]{1,0:T(8,128)(2,1)S(1)}, f32[6,128,128]{2,1,0:T(8,128)}) custom-call(s32[3]{0:T(128)S(1)} %pad_add_fusion.refs_0_.ids, bf16[128,128]{1,0:T(8,128)(2,1)} %refs_1_.1, bf16[128,512]{1,0:T(8,128)(2,1)} %refs_2_.1, bf16[128,512]{1,0:T(8,128)(2,1)} %refs_3_.2, bf16[128,128]{1,0:T(8,128)(2,1)} %refs_9_.1, f32[4,128]{1,0:T(4,128)} %bitcast.19), custom_call_target="tpu_custom_call" | custom-call | tf_op jit(solution)/shard_map/retention_local/pallas_call | solution.py:51
  3.6 2.0 %collective-permute-start = (bf16[272,128]{1,0:T(8,128)(2,1)S(1)}, bf16[272,128]{1,0:T(8,128)(2,1)S(1)}, u32[]{:S(2)}, u32[]{:S(2)}) collective-permute-start(bf16[272,128]{1,0:T(8,128)(2,1)S(1)} %get-tuple-element.51), channel_id=1, source_target_pairs={{0,4},{4,0},{1,5},{5,1},{2,6},{6,2},{3,7},{7,3},{8,12},{12,8},{9,1... | collective-permute-start | bytes 208904 | tf_op jit(solution)/shard_map/ppermute | solution.py:457
  5.7 4.9 %pack_rows.1 = (bf16[144,1280]{1,0:T(8,128)(2,1)}, bf16[144,1280]{1,0:T(8,128)(2,1)}, bf16[144,1280]{1,0:T(8,128)(2,1)}, bf16[144,1280]{1,0:T(8,128)(2,1)}) custom-call(s32[3]{0:T(128)S(1)} %pad_add_fusion.refs_0_.ids, bf16[128,2560]{1,0:T(8,128)(2,1)} %bitcast.14, bf16[128,2560]{1,0:T(8,128)(2,1)} %bitcast.15, bf16[128,2560]{1,0:T(8,128)(2,1)} %bitcast.16), custom_call_target="tpu_custom_call" | custom-call | tf_op jit(solution)/shard_map/pack_rows/pallas_call | solution.py:129
  10.6 0.0 collective-permute-done
  10.6 1.7 collective-permute-start.3
  12.2 2.9 %collective-permute-start.2 = (bf16[2,272,128]{2,1,0:T(8,128)(2,1)S(1)}, bf16[2,272,128]{2,1,0:T(8,128)(2,1)S(1)}, u32[]{:S(2)}, u32[]{:S(2)}) collective-permute-start(bf16[2,272,128]{2,1,0:T(8,128)(2,1)S(1)} %pad_maximum_fusion.refs_4_), channel_id=1, source_target_pairs={{0,16},{8,24},{16,0},{24,8},{1,17},{9,25},{17,1},{25,9},{2,18},{10... | collective-permute-start | bytes 417800 | tf_op jit(solution)/shard_map/ppermute | solution.py:435
  15.1 1.3 collective-permute-start.1
  16.5 0.9 collective-permute-done.3.refs_3_
  17.4 3.9 %collective-permute-done.2.refs_2_ = bf16[2,272,128]{2,1,0:T(8,128)(2,1)S(1)} collective-permute-done((bf16[2,272,128]{2,1,0:T(8,128)(2,1)S(1)}, bf16[2,272,128]{2,1,0:T(8,128)(2,1)S(1)}, u32[]{:S(2)}, u32[]{:S(2)}) %collective-permute-start.2) | collective-permute-done | bytes 139296 | tf_op jit(solution)/shard_map/ppermute | solution.py:435
  21.2 4.9 %collective-permute-start.4 = (bf16[144,1280]{1,0:T(8,128)(2,1)}, bf16[144,1280]{1,0:T(8,128)(2,1)S(1)}, u32[]{:S(2)}, u32[]{:S(2)}) collective-permute-start(bf16[144,1280]{1,0:T(8,128)(2,1)} %get-tuple-element.64), channel_id=1, source_target_pairs={{0,88},{8,80},{16,72},{24,64},{64,152},{72,144},{80,136},{88,128},... | collective-permute-start | bytes 1105928 | tf_op jit(solution)/shard_map/ppermute | solution.py:431
  26.1 2.1 %collective-permute-start.5 = (bf16[144,1280]{1,0:T(8,128)(2,1)}, bf16[144,1280]{1,0:T(8,128)(2,1)S(1)}, u32[]{:S(2)}, u32[]{:S(2)}) collective-permute-start(bf16[144,1280]{1,0:T(8,128)(2,1)} %get-tuple-element.65), channel_id=1, source_target_pairs={{0,216},{8,208},{16,200},{24,192},{64,24},{72,16},{80,8},{88,0},{1... | collective-permute-start | bytes 1105928 | tf_op jit(solution)/shard_map/ppermute | solution.py:431
  28.3 5.5 %collective-permute-start.6 = (bf16[144,1280]{1,0:T(8,128)(2,1)}, bf16[144,1280]{1,0:T(8,128)(2,1)S(1)}, u32[]{:S(2)}, u32[]{:S(2)}) collective-permute-start(bf16[144,1280]{1,0:T(8,128)(2,1)} %get-tuple-element.66), channel_id=1, source_target_pairs={{0,128},{64,192},{128,0},{192,64},{1,129},{65,193},{129,1},{193,65... | collective-permute-start | bytes 1105928 | tf_op jit(solution)/shard_map/ppermute | solution.py:429
  33.8 2.8 %copies.1 = bf16[4,4,2,272,128]{4,3,2,1,0:T(8,128)(2,1)} custom-call(s32[3]{0:T(128)S(1)} %pad_add_fusion.refs_0_.ids, bf16[2,272,128]{2,1,0:T(8,128)(2,1)S(1)} %collective-permute-done.1.refs_1_, bf16[2,272,128]{2,1,0:T(8,128)(2,1)S(1)} %collective-permute-done.2.refs_2_, bf16[2,272,128]{2,1,0:T(8,128)(2,1)S(1)} %collective-permute-done.3.refs_3_, ...), custom_call_target="tpu_custom_call" | custom-call | tf_op jit(solution)/shard_map/copies/pallas_call | solution.py:51
  36.6 4.8 %all-to-all-start = ((bf16[4,4,2,272,128]{4,3,2,1,0:T(8,128)(2,1)}), bf16[4,4,2,272,128]{4,3,2,1,0:T(8,128)(2,1)S(1)}, u32[]{:S(2)}, u32[]{:S(2)}) async-start(bf16[4,4,2,272,128]{4,3,2,1,0:T(8,128)(2,1)} %copies.1), calls=%async_computation | async-start | bytes 4456448 | tf_op jit(solution)/shard_map/all_to_all | solution.py:464
  41.4 2.5 %collective-permute-done.4.refs_0_.refs_3_ = bf16[144,1280]{1,0:T(8,128)(2,1)S(1)} collective-permute-done((bf16[144,1280]{1,0:T(8,128)(2,1)}, bf16[144,1280]{1,0:T(8,128)(2,1)S(1)}, u32[]{:S(2)}, u32[]{:S(2)}) %collective-permute-start.4) | collective-permute-done | bytes 368672 | tf_op jit(solution)/shard_map/ppermute | solution.py:431
  43.9 13.6 %collective-permute-done.5.refs_1_.refs_4_ = bf16[144,1280]{1,0:T(8,128)(2,1)S(1)} collective-permute-done((bf16[144,1280]{1,0:T(8,128)(2,1)}, bf16[144,1280]{1,0:T(8,128)(2,1)S(1)}, u32[]{:S(2)}, u32[]{:S(2)}) %collective-permute-start.5) | collective-permute-done | bytes 368672 | tf_op jit(solution)/shard_map/ppermute | solution.py:431
  57.5 3.7 %collective-permute-done.6.refs_2_.refs_5_ = bf16[144,1280]{1,0:T(8,128)(2,1)S(1)} collective-permute-done((bf16[144,1280]{1,0:T(8,128)(2,1)}, bf16[144,1280]{1,0:T(8,128)(2,1)S(1)}, u32[]{:S(2)}, u32[]{:S(2)}) %collective-permute-start.6) | collective-permute-done | bytes 368672 | tf_op jit(solution)/shard_map/ppermute | solution.py:429
  61.2 0.7 copy-done.4
  61.9 1.3 arrival.1.refs_7_
  63.2 2.4 %all-to-all-done.refs_1_ = bf16[4,4,2,272,128]{4,3,2,1,0:T(8,128)(2,1)S(1)} async-done(((bf16[4,4,2,272,128]{4,3,2,1,0:T(8,128)(2,1)}), bf16[4,4,2,272,128]{4,3,2,1,0:T(8,128)(2,1)S(1)}, u32[]{:S(2)}, u32[]{:S(2)}) %all-to-all-start) | async-done | bytes 2228256 | tf_op jit(solution)/shard_map/all_to_all | solution.py:464
  65.7 0.1 slice.4.refs_1_
  65.8 0.1 collective-permute-start.7
  65.9 2.6 %collective-permute-done.7.refs_2_ = bf16[4,4,2,128,128]{4,3,2,1,0:T(8,128)(2,1)S(1)} collective-permute-done((bf16[4,4,2,128,128]{4,3,2,1,0:T(8,128)(2,1)S(1)}, bf16[4,4,2,128,128]{4,3,2,1,0:T(8,128)(2,1)S(1)}, u32[]{:S(2)}, u32[]{:S(2)}) %collective-permute-start.7) | collective-permute-done | bytes 1048608 | tf_op jit(solution)/shard_map/ppermute | solution.py:439
  68.5 29.6 %attention.1 = (bf16[128,640]{1,0:T(8,128)(2,1)}, bf16[128,640]{1,0:T(8,128)(2,1)}, bf16[128,640]{1,0:T(8,128)(2,1)}, bf16[128,640]{1,0:T(8,128)(2,1)}, f32[4096...) custom-call(s32[3]{0:T(128)S(1)} %pad_add_fusion.refs_0_.ids, bf16[4,4,2,128,128]{4,3,2,1,0:T(8,128)(2,1)S(1)} %slice.4.refs_1_, ...), custom_call_target="tpu_custom_call" | custom-call | flops 13421772800 | bytes 6291456 | tf_op jit(solution)/shard_map/attention/pallas_call | solution.py:51
  98.2 0.4 collective-permute-start.8
  98.6 2.5 %collective-permute-done.8 = bf16[4096,128]{1,0:T(8,128)(2,1)S(1)} collective-permute-done((bf16[4096,128]{1,0:T(8,128)(2,1)S(1)}, bf16[4096,128]{1,0:T(8,128)(2,1)S(1)}, u32[]{:S(2)}, u32[]{:S(2)}) %collective-permute-start.8) | collective-permute-done | bytes 1048608 | tf_op jit(solution)/shard_map/ppermute | solution.py:439
  101.1 1.2 add_convert_fusion
  102.3 6.9 %all-to-all-start.1 = ((bf16[32,128,128]{2,1,0:T(8,128)(2,1)}), bf16[32,128,128]{2,1,0:T(8,128)(2,1)S(1)}, u32[]{:S(2)}, u32[]{:S(2)}) async-start(bf16[32,128,128]{2,1,0:T(8,128)(2,1)} %bitcast.13), calls=%async_computation.1 | async-start | bytes 2097152 | tf_op jit(solution)/shard_map/all_to_all | solution.py:443
  109.2 2.7 %collective-permute-start.9 = (bf16[128,640]{1,0:T(8,128)(2,1)}, bf16[128,640]{1,0:T(8,128)(2,1)S(1)}, u32[]{:S(2)}, u32[]{:S(2)}) collective-permute-start(bf16[128,640]{1,0:T(8,128)(2,1)} %get-tuple-element.72), channel_id=1, source_target_pairs={{0,128},{64,192},{128,0},{192,64},{1,129},{65,193},{129,1},{193,65... | collective-permute-start | bytes 491528 | tf_op jit(solution)/shard_map/ppermute | solution.py:429
  111.9 2.9 %retention_forward.1 = (f32[3,128,128]{2,1,0:T(8,128)}, f32[32,128]{1,0:T(8,128)}) custom-call(s32[3]{0:T(128)S(1)} %pad_add_fusion.refs_0_.ids, bf16[4,4,2,272,128]{4,3,2,1,0:T(8,128)(2,1)S(1)} %all-to-all-done.refs_1_, f32[6,128,128]{2,1,0:T(8,128)} %get-tuple-element.74.refs_2_.refs_3_.refs_8_, bf16[128,128]{1,0:T(8,128)(2,1)} %refs_9_.1), custom_call_target="tpu_custom_call" | custom-call | tf_op jit(solution)/shard_map/retention_forward/pallas_call | solution.py:51
  114.8 13.4 %collective-permute-done.9.refs_2_ = bf16[128,640]{1,0:T(8,128)(2,1)S(1)} collective-permute-done((bf16[128,640]{1,0:T(8,128)(2,1)}, bf16[128,640]{1,0:T(8,128)(2,1)S(1)}, u32[]{:S(2)}, u32[]{:S(2)}) %collective-permute-start.9) | collective-permute-done | bytes 163872 | tf_op jit(solution)/shard_map/ppermute | solution.py:429
  128.3 0.0 all-to-all-done.1.refs_1_
  128.3 2.9 %norm_backward.1 = (f32[128,128]{1,0:T(8,128)}, f32[128,128]{1,0:T(8,128)S(1)}) custom-call(s32[3]{0:T(128)S(1)} %pad_add_fusion.refs_0_.ids, bf16[32,128,128]{2,1,0:T(8,128)(2,1)S(1)} %all-to-all-done.1.refs_1_, f32[3,128,128]{2,1,0:T(8,128)} %get-tuple-element.75.refs_2_.refs_7_, f32[6,128,128]{2,1,0:T(8,128)} %get-tuple-element.74.refs_2_.refs_3_.refs_8_), custom_call_target="tpu_custom_call" | custom-call | tf_op jit(solution)/shard_map/norm_backward/pallas_call | solution.py:51
  131.1 1.5 collective-permute-start.12
  132.7 2.2 %collective-permute-start.11 = (f32[128,128]{1,0:T(8,128)S(1)}, f32[128,128]{1,0:T(8,128)S(1)}, u32[]{:S(2)}, u32[]{:S(2)}) collective-permute-start(f32[128,128]{1,0:T(8,128)S(1)} %get-tuple-element.76.refs_4_), channel_id=1, source_target_pairs={{0,2},{1,3},{2,0},{3,1},{4,6},{5,7},{6,4},{7,5},{8,10},{9,11},{10,... | collective-permute-start | bytes 196616 | tf_op jit(solution)/shard_map/ppermute | solution.py:435
  134.9 1.0 collective-permute-start.10
  135.9 7.8 %collective-permute-start.17 = (bf16[128,640]{1,0:T(8,128)(2,1)}, bf16[128,640]{1,0:T(8,128)(2,1)S(1)}, u32[]{:S(2)}, u32[]{:S(2)}) collective-permute-start(bf16[128,640]{1,0:T(8,128)(2,1)} %get-tuple-element.81), channel_id=1, source_target_pairs={{0,216},{8,208},{16,200},{24,192},{64,24},{72,16},{80,8},{88,0},{1... | collective-permute-start | bytes 491528 | tf_op jit(solution)/shard_map/ppermute | solution.py:431
  143.7 0.0 collective-permute-start.18
  143.7 0.0 collective-permute-done.12.refs_3_
  143.7 0.0 collective-permute-done.11.refs_2_
  143.7 1.8 scan_x.1
  145.5 1.2 collective-permute-start.13
  146.7 3.2 %collective-permute-done.13.refs_1_ = f32[128,128]{1,0:T(8,128)S(1)} collective-permute-done((f32[128,128]{1,0:T(8,128)S(1)}, f32[128,128]{1,0:T(8,128)S(1)}, u32[]{:S(2)}, u32[]{:S(2)}) %collective-permute-start.13) | collective-permute-done | bytes 65568 | tf_op jit(solution)/shard_map/ppermute | solution.py:487
  149.9 1.6 scan_z.1
  151.5 0.3 collective-permute-start.16
  151.8 3.4 %collective-permute-start.15 = (f32[128,128]{1,0:T(8,128)S(1)}, f32[128,128]{1,0:T(8,128)S(1)}, u32[]{:S(2)}, u32[]{:S(2)}) collective-permute-start(f32[128,128]{1,0:T(8,128)S(1)} %get-tuple-element.80), channel_id=1, source_target_pairs={{0,16},{8,24},{16,0},{24,8},{1,17},{9,25},{17,1},{25,9},{2,18},{10... | collective-permute-start | bytes 196616 | tf_op jit(solution)/shard_map/ppermute | solution.py:435
  155.2 0.3 collective-permute-start.14
  155.5 2.4 %grads_near.1.refs_5_ = f32[4,128,128]{2,1,0:T(8,128)S(1)} custom-call(s32[3]{0:T(128)S(1)} %pad_add_fusion.refs_0_.ids, f32[128,128]{1,0:T(8,128)} %get-tuple-element.91.refs_1_, f32[3,128,128]{2,1,0:T(8,128)} %get-tuple-element.75.refs_2_.refs_7_, f32[6,128,128]{2,1,0:T(8,128)} %get-tuple-element.74.refs_2_.refs_3_.refs_8_, bf16[128,128]{1,0:T(8,128)(2,1)} %refs_9_.1), custom_call_target="tpu_custom_call" | custom-call | flops 1000000000 | bytes 1000000 | tf_op jit(solution)/shard_map/grads_near/pallas_call | solution.py:51
  157.9 0.0 collective-permute-done.17.refs_1_
  157.9 0.3 collective-permute-done.15.refs_2_
  158.1 1.3 collective-permute-done.14.refs_1_
  159.5 3.4 %retention_grads.1 = (f32[128,128]{1,0:T(8,128)}, f32[144,256]{1,0:T(8,128)S(1)}) custom-call(s32[3]{0:T(128)S(1)} %pad_add_fusion.refs_0_.ids, f32[128,128]{1,0:T(8,128)S(1)} %collective-permute-done.14.refs_1_, f32[128,128]{1,0:T(8,128)S(1)} %collective-permute-done.15.refs_2_, f32[128,128]{1,0:T(8,128)S(1)} %collective-permute-done.16.refs_3_, ...), custom_call_target="tpu_custom_call" | custom-call | tf_op jit(solution)/shard_map/retention_grads/pallas_call | solution.py:51
  162.9 0.1 collective-permute-start.19
  163.0 1.4 collective-permute-done.19.refs_1_
  164.3 1.0 message.1.refs_4_
  165.3 4.6 %collective-permute-start.22 = (bf16[144,256]{1,0:T(8,128)(2,1)S(1)}, bf16[144,256]{1,0:T(8,128)(2,1)S(1)}, u32[]{:S(2)}, u32[]{:S(2)}) collective-permute-start(bf16[144,256]{1,0:T(8,128)(2,1)S(1)} %message.1.refs_4_), channel_id=1, source_target_pairs={{0,192},{64,0},{128,64},{192,128},{1,193},{65,1},{129,65},{193,129... | collective-permute-start | bytes 221192 | tf_op jit(solution)/shard_map/ppermute | solution.py:429
  169.9 0.6 collective-permute-start.21
  170.5 1.9 %collective-permute-start.20 = (bf16[144,256]{1,0:T(8,128)(2,1)S(1)}, bf16[144,256]{1,0:T(8,128)(2,1)S(1)}, u32[]{:S(2)}, u32[]{:S(2)}) collective-permute-start(bf16[144,256]{1,0:T(8,128)(2,1)S(1)} %message.1.refs_4_), channel_id=1, source_target_pairs={{0,64},{64,128},{128,192},{192,0},{1,65},{65,129},{129,193},{193,1... | collective-permute-start | bytes 221192 | tf_op jit(solution)/shard_map/ppermute | solution.py:429
  172.4 3.0 %query_rows.1 = bf16[128,2560]{1,0:T(8,128)(2,1)} custom-call(s32[3]{0:T(128)S(1)} %pad_add_fusion.refs_0_.ids, bf16[128,640]{1,0:T(8,128)(2,1)S(1)} %collective-permute-done.17.refs_1_, bf16[128,640]{1,0:T(8,128)(2,1)S(1)} %collective-permute-done.9.refs_2_, bf16[128,640]{1,0:T(8,128)(2,1)S(1)} %collective-permute-done.18.refs_3_, ...), custom_call_target="tpu_custom_call" | custom-call | tf_op jit(solution)/shard_map/query_rows/pallas_call | solution.py:51
  175.4 1.1 collective-permute-done.22.refs_3_
  176.6 3.9 %collective-permute-done.21.refs_2_ = bf16[144,256]{1,0:T(8,128)(2,1)S(1)} collective-permute-done((bf16[144,256]{1,0:T(8,128)(2,1)S(1)}, bf16[144,256]{1,0:T(8,128)(2,1)S(1)}, u32[]{:S(2)}, u32[]{:S(2)}) %collective-permute-start.21) | collective-permute-done | bytes 73760 | tf_op jit(solution)/shard_map/ppermute | solution.py:429
  180.4 0.0 collective-permute-done.20.refs_1_
  180.4 1.8 finish.1
  (16 shorter events, 0.0 us)
Async XLA Ops:
  3.6 6.9 %collective-permute-start = (bf16[272,128]{1,0:T(8,128)(2,1)S(1)}, bf16[272,128]{1,0:T(8,128)(2,1)S(1)}, u32[]{:S(2)}, u32[]{:S(2)}) collective-permute-start(bf16[272,128]{1,0:T(8,128)(2,1)S(1)} %get-tuple-element.51), channel_id=1, source_target_pairs={{0,4},{4,0},{1,5},{5,1},{2,6},{6,2},{3,7},{7,3},{8,12},{12,8},{9,1... | collective-permute-start | bytes 208904 | tf_op jit(solution)/shard_map/ppermute | solution.py:457
  10.6 6.8 %collective-permute-start.3 = (bf16[2,272,128]{2,1,0:T(8,128)(2,1)S(1)}, bf16[2,272,128]{2,1,0:T(8,128)(2,1)S(1)}, u32[]{:S(2)}, u32[]{:S(2)}) collective-permute-start(bf16[2,272,128]{2,1,0:T(8,128)(2,1)S(1)} %pad_maximum_fusion.refs_4_), channel_id=1, source_target_pairs={{0,8},{8,16},{16,24},{24,0},{1,9},{9,17},{17,25},{25,1},{2,10},{10... | collective-permute-start | bytes 417800 | tf_op jit(solution)/shard_map/ppermute | solution.py:435
  12.2 9.0 %collective-permute-start.2 = (bf16[2,272,128]{2,1,0:T(8,128)(2,1)S(1)}, bf16[2,272,128]{2,1,0:T(8,128)(2,1)S(1)}, u32[]{:S(2)}, u32[]{:S(2)}) collective-permute-start(bf16[2,272,128]{2,1,0:T(8,128)(2,1)S(1)} %pad_maximum_fusion.refs_4_), channel_id=1, source_target_pairs={{0,16},{8,24},{16,0},{24,8},{1,17},{9,25},{17,1},{25,9},{2,18},{10... | collective-permute-start | bytes 417800 | tf_op jit(solution)/shard_map/ppermute | solution.py:435
  15.1 6.1 %collective-permute-start.1 = (bf16[2,272,128]{2,1,0:T(8,128)(2,1)S(1)}, bf16[2,272,128]{2,1,0:T(8,128)(2,1)S(1)}, u32[]{:S(2)}, u32[]{:S(2)}) collective-permute-start(bf16[2,272,128]{2,1,0:T(8,128)(2,1)S(1)} %pad_maximum_fusion.refs_4_), channel_id=1, source_target_pairs={{0,24},{8,0},{16,8},{24,16},{1,25},{9,1},{17,9},{25,17},{2,26},{10... | collective-permute-start | bytes 417800 | tf_op jit(solution)/shard_map/ppermute | solution.py:435
  21.2 22.7 %collective-permute-start.4 = (bf16[144,1280]{1,0:T(8,128)(2,1)}, bf16[144,1280]{1,0:T(8,128)(2,1)S(1)}, u32[]{:S(2)}, u32[]{:S(2)}) collective-permute-start(bf16[144,1280]{1,0:T(8,128)(2,1)} %get-tuple-element.64), channel_id=1, source_target_pairs={{0,88},{8,80},{16,72},{24,64},{64,152},{72,144},{80,136},{88,128},... | collective-permute-start | bytes 1105928 | tf_op jit(solution)/shard_map/ppermute | solution.py:431
  26.1 31.3 %collective-permute-start.5 = (bf16[144,1280]{1,0:T(8,128)(2,1)}, bf16[144,1280]{1,0:T(8,128)(2,1)S(1)}, u32[]{:S(2)}, u32[]{:S(2)}) collective-permute-start(bf16[144,1280]{1,0:T(8,128)(2,1)} %get-tuple-element.65), channel_id=1, source_target_pairs={{0,216},{8,208},{16,200},{24,192},{64,24},{72,16},{80,8},{88,0},{1... | collective-permute-start | bytes 1105928 | tf_op jit(solution)/shard_map/ppermute | solution.py:431
  28.3 32.9 %collective-permute-start.6 = (bf16[144,1280]{1,0:T(8,128)(2,1)}, bf16[144,1280]{1,0:T(8,128)(2,1)S(1)}, u32[]{:S(2)}, u32[]{:S(2)}) collective-permute-start(bf16[144,1280]{1,0:T(8,128)(2,1)} %get-tuple-element.66), channel_id=1, source_target_pairs={{0,128},{64,192},{128,0},{192,64},{1,129},{65,193},{129,1},{193,65... | collective-permute-start | bytes 1105928 | tf_op jit(solution)/shard_map/ppermute | solution.py:429
  36.6 29.1 %all-to-all-start = ((bf16[4,4,2,272,128]{4,3,2,1,0:T(8,128)(2,1)}), bf16[4,4,2,272,128]{4,3,2,1,0:T(8,128)(2,1)S(1)}, u32[]{:S(2)}, u32[]{:S(2)}) async-start(bf16[4,4,2,272,128]{4,3,2,1,0:T(8,128)(2,1)} %copies.1), calls=%async_computation | async-start | bytes 4456448 | tf_op jit(solution)/shard_map/all_to_all | solution.py:464
  43.9 17.3 %copy-start = (bf16[144,1280]{1,0:T(8,128)(2,1)}, bf16[144,1280]{1,0:T(8,128)(2,1)S(1)}, u32[]{:S(2)}) copy-start(bf16[144,1280]{1,0:T(8,128)(2,1)S(1)} %collective-permute-done.4.refs_0_.refs_3_) | copy-start | bytes 1105924
  57.5 3.7 %copy-start.2 = (bf16[144,1280]{1,0:T(8,128)(2,1)}, bf16[144,1280]{1,0:T(8,128)(2,1)S(1)}, u32[]{:S(2)}) copy-start(bf16[144,1280]{1,0:T(8,128)(2,1)S(1)} %collective-permute-done.5.refs_1_.refs_4_) | copy-start | bytes 1105924
  61.2 0.7 copy-start.4
  63.2 5.3 %copy-start.1 = (bf16[144,1280]{1,0:T(8,128)(2,1)S(1)}, bf16[144,1280]{1,0:T(8,128)(2,1)}, u32[]{:S(2)}) copy-start(bf16[144,1280]{1,0:T(8,128)(2,1)} %copy-done) | copy-start | bytes 1105924
  63.2 5.3 %copy-start.3 = (bf16[144,1280]{1,0:T(8,128)(2,1)S(1)}, bf16[144,1280]{1,0:T(8,128)(2,1)}, u32[]{:S(2)}) copy-start(bf16[144,1280]{1,0:T(8,128)(2,1)} %copy-done.2) | copy-start | bytes 1105924
  63.2 5.3 %copy-start.5 = (bf16[144,1280]{1,0:T(8,128)(2,1)S(1)}, bf16[144,1280]{1,0:T(8,128)(2,1)}, u32[]{:S(2)}) copy-start(bf16[144,1280]{1,0:T(8,128)(2,1)} %copy-done.4) | copy-start | bytes 1105924
  65.8 2.7 %collective-permute-start.7 = (bf16[4,4,2,128,128]{4,3,2,1,0:T(8,128)(2,1)S(1)}, bf16[4,4,2,128,128]{4,3,2,1,0:T(8,128)(2,1)S(1)}, u32[]{:S(2)}, u32[]{:S(2)}) collective-permute-start(bf16[4,4,2,128,128]{4,3,2,1,0:T(8,128)(2,1)S(1)} %slice.4.refs_1_), channel_id=1, source_target_pairs={{0,32},{32,0},{1,33},{33,1},{2,34},{34,2},{3,35},{35,3},{4,36},{36... | collective-permute-start | bytes 3145736 | tf_op jit(solution)/shard_map/ppermute | solution.py:439
  98.2 2.9 %collective-permute-start.8 = (bf16[4096,128]{1,0:T(8,128)(2,1)S(1)}, bf16[4096,128]{1,0:T(8,128)(2,1)S(1)}, u32[]{:S(2)}, u32[]{:S(2)}) collective-permute-start(bf16[4096,128]{1,0:T(8,128)(2,1)S(1)} %get-tuple-element.71), channel_id=1, source_target_pairs={{0,32},{32,0},{1,33},{33,1},{2,34},{34,2},{3,35},{35,3},{4,36},{36... | collective-permute-start | bytes 3145736 | tf_op jit(solution)/shard_map/ppermute | solution.py:439
  102.3 26.0 %all-to-all-start.1 = ((bf16[32,128,128]{2,1,0:T(8,128)(2,1)}), bf16[32,128,128]{2,1,0:T(8,128)(2,1)S(1)}, u32[]{:S(2)}, u32[]{:S(2)}) async-start(bf16[32,128,128]{2,1,0:T(8,128)(2,1)} %bitcast.13), calls=%async_computation.1 | async-start | bytes 2097152 | tf_op jit(solution)/shard_map/all_to_all | solution.py:443
  109.2 19.0 %collective-permute-start.9 = (bf16[128,640]{1,0:T(8,128)(2,1)}, bf16[128,640]{1,0:T(8,128)(2,1)S(1)}, u32[]{:S(2)}, u32[]{:S(2)}) collective-permute-start(bf16[128,640]{1,0:T(8,128)(2,1)} %get-tuple-element.72), channel_id=1, source_target_pairs={{0,128},{64,192},{128,0},{192,64},{1,129},{65,193},{129,1},{193,65... | collective-permute-start | bytes 491528 | tf_op jit(solution)/shard_map/ppermute | solution.py:429
  131.1 12.5 %collective-permute-start.12 = (f32[128,128]{1,0:T(8,128)S(1)}, f32[128,128]{1,0:T(8,128)S(1)}, u32[]{:S(2)}, u32[]{:S(2)}) collective-permute-start(f32[128,128]{1,0:T(8,128)S(1)} %get-tuple-element.76.refs_4_), channel_id=1, source_target_pairs={{0,1},{1,2},{2,3},{3,0},{4,5},{5,6},{6,7},{7,4},{8,9},{9,10},{10,1... | collective-permute-start | bytes 196616 | tf_op jit(solution)/shard_map/ppermute | solution.py:435
  132.7 11.0 %collective-permute-start.11 = (f32[128,128]{1,0:T(8,128)S(1)}, f32[128,128]{1,0:T(8,128)S(1)}, u32[]{:S(2)}, u32[]{:S(2)}) collective-permute-start(f32[128,128]{1,0:T(8,128)S(1)} %get-tuple-element.76.refs_4_), channel_id=1, source_target_pairs={{0,2},{1,3},{2,0},{3,1},{4,6},{5,7},{6,4},{7,5},{8,10},{9,11},{10,... | collective-permute-start | bytes 196616 | tf_op jit(solution)/shard_map/ppermute | solution.py:435
  134.9 8.8 %collective-permute-start.10 = (f32[128,128]{1,0:T(8,128)S(1)}, f32[128,128]{1,0:T(8,128)S(1)}, u32[]{:S(2)}, u32[]{:S(2)}) collective-permute-start(f32[128,128]{1,0:T(8,128)S(1)} %get-tuple-element.76.refs_4_), channel_id=1, source_target_pairs={{0,3},{1,0},{2,1},{3,2},{4,7},{5,4},{6,5},{7,6},{8,11},{9,8},{10,9... | collective-permute-start | bytes 196616 | tf_op jit(solution)/shard_map/ppermute | solution.py:435
  135.9 21.9 %collective-permute-start.17 = (bf16[128,640]{1,0:T(8,128)(2,1)}, bf16[128,640]{1,0:T(8,128)(2,1)S(1)}, u32[]{:S(2)}, u32[]{:S(2)}) collective-permute-start(bf16[128,640]{1,0:T(8,128)(2,1)} %get-tuple-element.81), channel_id=1, source_target_pairs={{0,216},{8,208},{16,200},{24,192},{64,24},{72,16},{80,8},{88,0},{1... | collective-permute-start | bytes 491528 | tf_op jit(solution)/shard_map/ppermute | solution.py:431
  143.7 14.2 %collective-permute-start.18 = (bf16[128,640]{1,0:T(8,128)(2,1)}, bf16[128,640]{1,0:T(8,128)(2,1)S(1)}, u32[]{:S(2)}, u32[]{:S(2)}) collective-permute-start(bf16[128,640]{1,0:T(8,128)(2,1)} %get-tuple-element.82), channel_id=1, source_target_pairs={{0,88},{8,80},{16,72},{24,64},{64,152},{72,144},{80,136},{88,128},... | collective-permute-start | bytes 491528 | tf_op jit(solution)/shard_map/ppermute | solution.py:431
  145.5 4.4 %collective-permute-start.13 = (f32[128,128]{1,0:T(8,128)S(1)}, f32[128,128]{1,0:T(8,128)S(1)}, u32[]{:S(2)}, u32[]{:S(2)}) collective-permute-start(f32[128,128]{1,0:T(8,128)S(1)} %get-tuple-element.78.refs_2_), channel_id=1, source_target_pairs={{0,4},{4,0},{1,5},{5,1},{2,6},{6,2},{3,7},{7,3},{8,12},{12,8},{9,1... | collective-permute-start | bytes 196616 | tf_op jit(solution)/shard_map/ppermute | solution.py:487
  151.5 6.4 %collective-permute-start.16 = (f32[128,128]{1,0:T(8,128)S(1)}, f32[128,128]{1,0:T(8,128)S(1)}, u32[]{:S(2)}, u32[]{:S(2)}) collective-permute-start(f32[128,128]{1,0:T(8,128)S(1)} %get-tuple-element.80), channel_id=1, source_target_pairs={{0,8},{8,16},{16,24},{24,0},{1,9},{9,17},{17,25},{25,1},{2,10},{10... | collective-permute-start | bytes 196616 | tf_op jit(solution)/shard_map/ppermute | solution.py:435
  151.8 6.3 %collective-permute-start.15 = (f32[128,128]{1,0:T(8,128)S(1)}, f32[128,128]{1,0:T(8,128)S(1)}, u32[]{:S(2)}, u32[]{:S(2)}) collective-permute-start(f32[128,128]{1,0:T(8,128)S(1)} %get-tuple-element.80), channel_id=1, source_target_pairs={{0,16},{8,24},{16,0},{24,8},{1,17},{9,25},{17,1},{25,9},{2,18},{10... | collective-permute-start | bytes 196616 | tf_op jit(solution)/shard_map/ppermute | solution.py:435
  155.2 4.3 %collective-permute-start.14 = (f32[128,128]{1,0:T(8,128)S(1)}, f32[128,128]{1,0:T(8,128)S(1)}, u32[]{:S(2)}, u32[]{:S(2)}) collective-permute-start(f32[128,128]{1,0:T(8,128)S(1)} %get-tuple-element.80), channel_id=1, source_target_pairs={{0,24},{8,0},{16,8},{24,16},{1,25},{9,1},{17,9},{25,17},{2,26},{10... | collective-permute-start | bytes 196616 | tf_op jit(solution)/shard_map/ppermute | solution.py:435
  162.9 1.5 collective-permute-start.19
  165.3 11.3 %collective-permute-start.22 = (bf16[144,256]{1,0:T(8,128)(2,1)S(1)}, bf16[144,256]{1,0:T(8,128)(2,1)S(1)}, u32[]{:S(2)}, u32[]{:S(2)}) collective-permute-start(bf16[144,256]{1,0:T(8,128)(2,1)S(1)} %message.1.refs_4_), channel_id=1, source_target_pairs={{0,192},{64,0},{128,64},{192,128},{1,193},{65,1},{129,65},{193,129... | collective-permute-start | bytes 221192 | tf_op jit(solution)/shard_map/ppermute | solution.py:429
  169.9 10.5 %collective-permute-start.21 = (bf16[144,256]{1,0:T(8,128)(2,1)S(1)}, bf16[144,256]{1,0:T(8,128)(2,1)S(1)}, u32[]{:S(2)}, u32[]{:S(2)}) collective-permute-start(bf16[144,256]{1,0:T(8,128)(2,1)S(1)} %message.1.refs_4_), channel_id=1, source_target_pairs={{0,128},{64,192},{128,0},{192,64},{1,129},{65,193},{129,1},{193,65... | collective-permute-start | bytes 221192 | tf_op jit(solution)/shard_map/ppermute | solution.py:429
  170.5 9.9 %collective-permute-start.20 = (bf16[144,256]{1,0:T(8,128)(2,1)S(1)}, bf16[144,256]{1,0:T(8,128)(2,1)S(1)}, u32[]{:S(2)}, u32[]{:S(2)}) collective-permute-start(bf16[144,256]{1,0:T(8,128)(2,1)S(1)} %message.1.refs_4_), channel_id=1, source_target_pairs={{0,64},{64,128},{128,192},{192,0},{1,65},{65,129},{129,193},{193,1... | collective-permute-start | bytes 221192 | tf_op jit(solution)/shard_map/ppermute | solution.py:429
